TPU v7x, 256 devices: a whole 4x4x8 slice. The times are simulated.
256 devices in a mesh: row: 32 (over x, z), col: 8 (over y, core).
Axes of the slice: x: 4, y: 4, z: 8, core: 2. Of those that a mesh axis runs over, the one named last changes fastest.
Arguments:
- momentum: float32 [2, 7168, 2048], P(None, 'row', 'col'), may hold values from -6 to 6
- gradient: bfloat16 [2, 7168, 2048], P(None, 'row', 'col'), may hold values from -6 to 6
- basis_in: bfloat16 [2, 2048, 512], P(None, 'col'), may hold values from -0.125 to 0.125
Outputs:
- momentum_new: float32 [2, 7168, 2048], P(None, 'row', 'col')
- direction: bfloat16 [2, 7168, 2048], P(None, 'row', 'col')
All inputs are finite; a program needn't handle non-finite values.
Results may differ from a plain program's by a relative error of at most 0.02.
Values may be sent and summed in bfloat16 or wider, within the bound.
No kernel may reach another device: no remote copies, remote signals or barrier semaphores. Data moves between devices by JAX's collectives and lax.ppermute only.
A program may use at most 64 MiB of HBM per device.

v0:
```python
import math

import jax
import jax.numpy as jnp
from jax import lax
from jax.sharding import PartitionSpec as P

ROWS = 7168
COLS = 2048
RANK = 512


def orthonormalize(gram_full, panel):
    factor = jnp.linalg.cholesky(gram_full)
    solved = lax.linalg.triangular_solve(
        factor, panel, left_side=False, lower=True, transpose_a=True
    )
    return solved.astype(jnp.bfloat16)


def local(momentum, gradient, basis_in):
    buffer = momentum + gradient.astype(jnp.float32)
    buffer_half = buffer.astype(jnp.bfloat16)
    partial_value = jnp.einsum(
        "erc,eck->erk", buffer_half, basis_in, preferred_element_type=jnp.float32
    )
    projected = lax.psum(partial_value, "col")
    gram_partial = jnp.einsum("erk,erl->ekl", projected, projected, precision=lax.Precision.HIGHEST)
    gram_piece = lax.psum_scatter(gram_partial, "row", scatter_dimension=1, tiled=True)
    gram_full = lax.all_gather(gram_piece, "row", axis=1, tiled=True)
    orthonormal = orthonormalize(gram_full, projected)
    reduced = lax.psum(
        jnp.einsum(
            "erc,erk->eck", buffer_half, orthonormal, preferred_element_type=jnp.float32
        ).astype(jnp.bfloat16),
        "row",
    ).astype(jnp.float32)
    squares = lax.psum(jnp.sum(reduced * reduced, axis=1, keepdims=True), "col")
    new_basis = (reduced * lax.rsqrt(squares + 1e-06)).astype(jnp.bfloat16)
    momentum_new = buffer - 0.1 * jnp.einsum(
        "erk,eck->erc", orthonormal.astype(jnp.float32), reduced, precision=lax.Precision.HIGHEST
    )
    update_scale = math.sqrt(ROWS * COLS / RANK)
    direction = (
        update_scale
        * jnp.einsum("erk,eck->erc", orthonormal, new_basis, preferred_element_type=jnp.float32)
    ).astype(jnp.bfloat16)
    return (momentum_new, direction)


def solution(mesh):
    placed = (P(None, "row", "col"), P(None, "row", "col"), P(None, "col", None))
    return jax.shard_map(
        local,
        mesh=mesh,
        in_specs=placed,
        out_specs=(P(None, "row", "col"), P(None, "row", "col")),
        check_vma=False,
    )
```

profile of v0, /device:TPU:1, one launch (start us, length us, event | category | flops | bytes accessed | tf_op | source)
XLA Modules:
  0.0 761.4 jit_solution(5562151100556253094)
XLA Ops:
  7.2 1.0 copy-done
  8.2 2.3 fusion.37
  10.6 69.0 %all-reduce.6.cloned.1.call-done = f32[2,224,512]{2,1,0:T(8,128)} async-done(((f32[2,224,512]{2,1,0:T(8,128)}), f32[2,224,512]{2,1,0:T(8,128)}) %all-reduce.6.cloned.1.call-update) | async-done | bytes 917520 | tf_op jit(solution)/shard_map/psum | solution.py:27
  79.6 3.4 fusion.43
  82.9 2.9 copy.32
  85.9 0.6 copy-done.7
  86.5 0.6 dynamic-slice.4
  87.8 149.4 %all-reduce.10.cloned.1.call-done = f32[2,512,512]{2,0,1:T(2,128)} async-done(((f32[2,512,512]{2,0,1:T(2,128)}), f32[2,512,512]{2,0,1:T(2,128)}) %all-reduce.10.cloned.1.call-update) | async-done | bytes 2097168
  237.1 1.5 constant_dynamic-slice_fusion.1
  239.2 0.6 iota_multiply_fusion
  239.8 0.6 iota_compare_fusion.2
  240.4 0.8 iota_compare_fusion
  241.2 74.7 %all-gather.2.cloned.1.call-done = f32[2,512,512]{2,0,1:T(2,128)} async-done(((f32[2,16,512]{2,0,1:T(2,128)}), f32[2,512,512]{2,0,1:T(2,128)}) %all-gather.2.cloned.1.call-update) | async-done | bytes 2097168 | tf_op jit(solution)/shard_map/all_gather | solution.py:30
  315.8 4.3 copy.33
  320.1 2.2 fusion
  322.3 1.3 copy-done.3
  323.7 23.5 %custom-call.34 = f32[2,128,128]{2,1,0:T(8,128)S(1)} custom-call(f32[2,128,128]{2,1,0:T(8,128)S(1)} %cholesky.274), custom_call_target="Cholesky" | custom-call | tf_op jit(solution)/shard_map/jit(cholesky)/cholesky | solution.py:14
  347.2 19.7 %custom-call.35 = f32[2,1,128,128]{2,3,1,0:T(8,128)S(1)} custom-call(f32[2,1,128,128]{3,2,1,0:T(8,128)S(1)} %select_bitcast_fusion.2), custom_call_target="InvertDiagBlocksLowerTriangular" | custom-call | tf_op jit(solution)/shard_map/jit(cholesky)/cholesky | solution.py:14
  367.1 1.5 constant_dynamic-update-slice_fusion.3
  368.6 1.5 convolution_subtract_fusion
  370.1 23.5 %custom-call.36 = f32[2,128,128]{2,1,0:T(8,128)S(1)} custom-call(f32[2,128,128]{2,1,0:T(8,128)S(1)} %cholesky.278), custom_call_target="Cholesky" | custom-call | tf_op jit(solution)/shard_map/jit(cholesky)/cholesky | solution.py:14
  393.6 19.8 %custom-call.37 = f32[2,1,128,128]{2,3,1,0:T(8,128)S(1)} custom-call(f32[2,1,128,128]{3,2,1,0:T(8,128)S(1)} %get-tuple-element.27), custom_call_target="InvertDiagBlocksLowerTriangular" | custom-call | tf_op jit(solution)/shard_map/jit(cholesky)/cholesky | solution.py:14
  413.9 1.6 convolution_subtract_fusion.1
  415.5 23.5 %custom-call.38 = f32[2,128,128]{2,1,0:T(8,128)S(1)} custom-call(f32[2,128,128]{2,1,0:T(8,128)S(1)} %cholesky.283), custom_call_target="Cholesky" | custom-call | tf_op jit(solution)/shard_map/jit(cholesky)/cholesky | solution.py:14
  438.9 19.7 %custom-call.39 = f32[2,1,128,128]{2,3,1,0:T(8,128)S(1)} custom-call(f32[2,1,128,128]{3,2,1,0:T(8,128)S(1)} %get-tuple-element.25), custom_call_target="InvertDiagBlocksLowerTriangular" | custom-call | tf_op jit(solution)/shard_map/jit(cholesky)/cholesky | solution.py:14
  458.9 1.5 convolution_subtract_fusion.5
  460.4 23.7 %custom-call.40 = f32[2,128,128]{2,1,0:T(8,128)S(1)} custom-call(f32[2,128,128]{2,1,0:T(8,128)S(1)} %convolution_subtract_fusion.5), custom_call_target="Cholesky" | custom-call | tf_op jit(solution)/shard_map/jit(cholesky)/cholesky | solution.py:14
  484.1 0.8 select_reduce_fusion.2
  485.2 2.8 select_select_fusion
  488.0 14.4 %while.1 = (s32[]{:T(128)}, f32[2,512,512]{2,1,0:T(8,128)}, s32[4,2]{0,1:T(2,128)S(1)}, f32[4,2,128,128]{3,2,0,1:T(8,128)}, s32[]{:T(128)}) while((s32[]{:T(128)}, f32[2,512,512]{2,1,0:T(8,128)}, s32[4,2]{0,1:T(2,128)S(1)}, f32[4,2,128,128]{3,2,0,1:T(8,128)}, s32[]{:T(128)}) %tuple.35), condition=%wide.while_cond, body=%wide.while_body.sunk | while | flops 2 | bytes 263777 | solution.py:15
  488.1 0.5 fusion.54
  488.6 3.0 bitcast_dynamic-update-slice_fusion.2
  491.7 0.5 fusion.54
  492.2 3.0 bitcast_dynamic-update-slice_fusion.2
  495.3 0.5 fusion.54
  495.8 3.0 bitcast_dynamic-update-slice_fusion.2
  498.9 0.5 fusion.54
  499.4 3.0 bitcast_dynamic-update-slice_fusion.2
  502.4 79.4 %custom-call.41 = f32[2,4,128,128]{2,3,1,0:T(8,128)S(1)} custom-call(f32[2,4,128,128]{3,2,1,0:T(8,128)} %bitcast.72), custom_call_target="InvertDiagBlocksLowerTriangular" | custom-call | tf_op jit(solution)/shard_map/triangular_solve | solution.py:15
  582.2 1.3 convolution_subtract_fusion.3
  583.8 1.6 convolution_subtract_fusion.2
  585.8 1.8 convolution_subtract_fusion.4
  587.9 1.2 convolution_convert_fusion
  589.1 144.1 %all-reduce.8.cloned.1.call-done = bf16[2,256,512]{2,1,0:T(8,128)(2,1)} async-done(((bf16[2,256,512]{2,1,0:T(8,128)(2,1)}), bf16[2,256,512]{2,1,0:T(8,128)(2,1)}) %all-reduce.8.cloned.1.call-update) | async-done | bytes 524304 | tf_op jit(solution)/shard_map/psum | solution.py:32
  733.2 1.2 fusion.3
  734.4 17.0 %psum.23 = f32[2,1,512]{2,0,1:T(2,128)S(1)} all-reduce(f32[2,1,512]{2,0,1:T(2,128)S(1)} %bitcast.71), channel_id=1, replica_groups=mesh['row'=32,'col'=8] {'col'}, use_global_device_ids=true, to_apply=%region_12.13 | all-reduce | flops 1024 | bytes 8192 | tf_op jit(solution)/shard_map/psum | solution.py:38
  751.5 2.1 fusion.1
  753.6 1.0 fusion.2
  (47 shorter events, 3.7 us)
Async XLA Ops:
  7.2 1.0 copy-start
  7.2 72.4 %all-reduce.6.cloned.1.call-start = ((), (), s32[]{:S(2)}) async-start(), calls=%async_computation | async-start | bytes 1835008 | tf_op jit(solution)/shard_map/psum | solution.py:27
  10.5 226.6 %all-reduce.10.cloned.1.call-start = ((), (), s32[]{:S(2)}) async-start(), calls=%async_computation.3 | async-start | bytes 4194304
  85.9 0.7 copy-start.7
  85.9 230.0 %all-gather.2.cloned.1.call-start = ((), (), s32[]{:S(2)}) async-start(), calls=%async_computation.1 | async-start | bytes 2162688 | tf_op jit(solution)/shard_map/all_gather | solution.py:30
  238.6 494.6 %all-reduce.8.cloned.1.call-start = ((), (), s32[]{:S(2)}) async-start(), calls=%async_computation.2 | async-start | bytes 1048576 | tf_op jit(solution)/shard_map/psum | solution.py:32
  315.8 4.3 copy-start.1
  322.3 1.4 copy-start.3
  485.2 2.8 copy-start.8
  485.2 96.6 %copy-start.2 = (f32[2,224,512]{2,1,0:T(8,128)S(1)}, f32[2,224,512]{2,1,0:T(8,128)}, u32[]{:S(2)}) copy-start(f32[2,224,512]{2,1,0:T(8,128)} %all-reduce.6.cloned.1.call-done) | copy-start | bytes 2752516
  583.8 4.1 copy-start.5
  583.8 4.1 copy-start.6
  733.2 20.4 %copy-start.4 = (bf16[2,256,512]{2,1,0:T(8,128)(2,1)S(1)}, bf16[2,256,512]{2,1,0:T(8,128)(2,1)}, u32[]{:S(2)}) copy-start(bf16[2,256,512]{2,1,0:T(8,128)(2,1)} %all-reduce.8.cloned.1.call-done) | copy-start | bytes 1572868
Sparse Core Ops, SparseCore 0:
  10.6 68.8 all-reduce.5
  86.0 151.0 all-reduce.9
  240.3 75.4 all-gather.1
  589.2 143.9 all-reduce.7
where the time goes:
time: 766 us; the launch traced here: 761 us
  waiting for transfers between devices  437 us (57%)
  other arithmetic  242 us (32%)
  local copies, waits for them, and re-layouts  26.9 us (4%)
  matrix products  22.7 us (3%)
  blocking collectives  17 us (2%)
  between operations  14.9 us (2%)
    another operation x16, other arithmetic, orthonormalize(): factor = jnp.linalg.cholesky(gram_full)  155 us
    unnamed x5, waiting for transfers between devices  149 us
    psum x1, waiting for transfers between devices, local(): lax.psum(jnp.einsum('erc,erk->eck', buffer_half, orthonormal, preferred_e...  144 us
    another operation x4, other arithmetic, orthonormalize(): lax.linalg.triangular_solve(factor, panel, left_side=False, lower=True, t...  83.6 us
    all_gather x1, waiting for transfers between devices, local(): gram_full = lax.all_gather(gram_piece, 'row', axis=1, tiled=True)  74.7 us
    psum x1, waiting for transfers between devices, local(): projected = lax.psum(partial_value, 'col')  69 us
    psum x1, blocking collectives, local(): squares = lax.psum(jnp.sum(reduced * reduced, axis=1, keepdims=True), 'col')  17 us
  transfers between devices with their start and end apart: 4, of which 4 were waited for; matrix products, arithmetic and copies ran while one was open for 0% of the time, Pallas kernels for 0%

commit v1 on v0

v1 whole, which is shorter than its diff:
```python
import math

import jax
import jax.numpy as jnp
from jax import lax
from jax.experimental import pallas as pl
from jax.experimental.pallas import tpu as pltpu
from jax.sharding import PartitionSpec as P

ROWS = 7168
COLS = 2048
RANK = 512
EXPERTS = 2
BLOCK = 128
PANEL = 8
BLOCKS = RANK // BLOCK
PANELS = BLOCK // PANEL
HIGHEST = lax.Precision.HIGHEST


def lanes_of(value, lane):
    return jnp.broadcast_to(value[:, lane : lane + 1], (PANEL, BLOCK))


def row_of(value, row):
    return jnp.broadcast_to(value[row : row + 1, :], (PANEL, BLOCK))


def small_inverse(panel, base, row):
    cols = [lanes_of(panel, base + j) for j in range(PANEL)]
    snap = [jnp.zeros((PANEL, BLOCK), jnp.float32) for _ in range(PANEL)]
    roots = jnp.zeros((PANEL, BLOCK), jnp.float32)
    for j in range(PANEL):
        here = row == j
        root = lax.rsqrt(row_of(cols[j], j))
        inv = root * root
        roots = jnp.where(here, root, roots)
        pivot = cols[j]
        for k in range(PANEL):
            if k == j:
                continue
            entry = row_of(cols[k], j)
            if k < j:
                snap[k] = jnp.where(here, entry, snap[k])
            scaled = entry * inv
            cols[k] = jnp.where(here, scaled, cols[k] - pivot * scaled)
        cols[j] = jnp.where(here, inv, -(pivot * inv))
        snap[j] = jnp.where(here, 1.0, snap[j])
    return cols, [roots * s for s in snap]


def combine(cols, value):
    terms = [cols[j] * row_of(value, j) for j in range(PANEL)]
    while len(terms) > 1:
        terms = [terms[i] + terms[i + 1] for i in range(0, len(terms), 2)]
    return terms[0]


def block_inverse_factor(groups):
    row = lax.broadcasted_iota(jnp.int32, (PANEL, BLOCK), 0)
    lane = lax.broadcasted_iota(jnp.int32, (PANEL, BLOCK), 1)
    for k in range(PANELS):
        base = k * PANEL
        inside = (lane >= base) & (lane < base + PANEL)
        unit = (lane == row + base).astype(jnp.float32)
        for e in range(EXPERTS):
            panel = groups[e][k]
            full, factor = small_inverse(panel, base, row)
            panel = jnp.where(inside, unit, panel)
            groups[e][k] = combine(factor, panel)
            if k + 1 < PANELS:
                solved = combine(full, panel)
                rows = [row_of(solved, j) for j in range(PANEL)]
                for i in range(k + 1, PANELS):
                    old = groups[e][i]
                    terms = [lanes_of(old, base + j) * rows[j] for j in range(PANEL)]
                    while len(terms) > 1:
                        terms = [terms[t] + terms[t + 1] for t in range(0, len(terms), 2)]
                    groups[e][i] = jnp.where(inside, 0.0, old) - terms[0]
    return groups


def factor_kernel(gram_ref, out_ref, work_ref):
    for e in range(EXPERTS):
        for i in range(BLOCKS):
            work_ref[e, i] = gram_ref[e, i * BLOCK : (i + 1) * BLOCK, :]
    big_row = lax.broadcasted_iota(jnp.int32, (BLOCK, BLOCK), 0)
    big_lane = lax.broadcasted_iota(jnp.int32, (BLOCK, BLOCK), 1)
    wide = lax.broadcasted_iota(jnp.int32, (BLOCK, RANK), 1)

    def step(k, carry):
        at = pl.multiple_of(k * BLOCK, BLOCK)
        groups = []
        for e in range(EXPERTS):
            groups.append(
                [work_ref[e, k, i * PANEL : (i + 1) * PANEL, pl.ds(at, BLOCK)] for i in range(PANELS)]
            )
        groups = block_inverse_factor(groups)
        own = (wide >= at) & (wide < at + BLOCK)
        for e in range(EXPERTS):
            inverse = jnp.where(big_row >= big_lane, jnp.concatenate(groups[e], axis=0), 0.0)
            work_ref[e, k] = jnp.dot(
                inverse, work_ref[e, k], precision=HIGHEST, preferred_element_type=jnp.float32
            )
            work_ref[e, k, :, pl.ds(at, BLOCK)] = inverse
        for i in range(1, BLOCKS):

            @pl.when(i > k)
            def _():
                for e in range(EXPERTS):
                    left = work_ref[e, k, :, i * BLOCK : (i + 1) * BLOCK].T
                    change = jnp.dot(
                        left, work_ref[e, k], precision=HIGHEST, preferred_element_type=jnp.float32
                    )
                    work_ref[e, i] = jnp.where(own, 0.0, work_ref[e, i]) - change

        return carry

    lax.fori_loop(0, BLOCKS, step, 0)
    for e in range(EXPERTS):
        for i in range(BLOCKS):
            row = lax.broadcasted_iota(jnp.int32, (BLOCK, RANK), 0) + i * BLOCK
            out_ref[e, i * BLOCK : (i + 1) * BLOCK, :] = jnp.where(row >= wide, work_ref[e, i], 0.0)


def inverse_factor(gram):
    return pl.pallas_call(
        factor_kernel,
        out_shape=jax.ShapeDtypeStruct(gram.shape, jnp.float32),
        in_specs=[pl.BlockSpec(memory_space=pltpu.VMEM)],
        out_specs=pl.BlockSpec(memory_space=pltpu.VMEM),
        scratch_shapes=[pltpu.VMEM((EXPERTS, BLOCKS, BLOCK, RANK), jnp.float32)],
        compiler_params=pltpu.CompilerParams(vmem_limit_bytes=24 * 1024 * 1024),
    )(gram)


def spread(chunks, axis):
    return lax.all_to_all(chunks, axis, split_axis=0, concat_axis=0, tiled=True)


def share(value, axis, count):
    return spread(jnp.broadcast_to(value[None], (count,) + value.shape), axis)


def split_halves(value):
    high = value.astype(jnp.bfloat16)
    low = (value - high.astype(jnp.float32)).astype(jnp.bfloat16)
    return high, low


def make_local(row_count, col_count):
    def local(momentum, gradient, basis_in):
        experts, rows, cols = momentum.shape
        rank = basis_in.shape[-1]
        buffer = momentum + gradient.astype(jnp.float32)
        half = buffer.astype(jnp.bfloat16)
        partial = jnp.einsum("erc,eck->erk", half, basis_in, preferred_element_type=jnp.float32)
        piece = partial.astype(jnp.bfloat16).reshape(col_count, experts * rows // col_count, rank)
        mine = jnp.sum(spread(piece, "col").astype(jnp.float32), axis=0).astype(jnp.bfloat16)
        projected = share(mine, "col", col_count).reshape(experts, rows, rank)

        col = lax.axis_index("col")
        slabs = col_count // experts
        width = rank // slabs
        one = lax.dynamic_index_in_dim(projected, col % experts, 0, keepdims=False)
        slab = lax.dynamic_slice_in_dim(one, (col // experts) * width, width, axis=1)
        gram_partial = jnp.einsum("rk,rl->kl", slab, one, preferred_element_type=jnp.float32)
        wide_partial = jnp.einsum(
            "erc,erk->eck", half, projected, preferred_element_type=jnp.float32
        ).astype(jnp.bfloat16)
        gram_high, gram_low = split_halves(gram_partial.reshape(row_count, width // row_count, rank))
        wide_rows = experts * cols // row_count
        packed = jnp.concatenate(
            [wide_partial.reshape(row_count, wide_rows, rank), gram_high, gram_low], axis=1
        )
        arrived = spread(packed, "row").astype(jnp.float32)
        gram_rows = width // row_count
        wide_mine = jnp.sum(arrived[:, :wide_rows], axis=0).astype(jnp.bfloat16)
        gram_mine = jnp.sum(
            arrived[:, wide_rows : wide_rows + gram_rows] + arrived[:, wide_rows + gram_rows :], axis=0
        )
        gram_slab = share(gram_mine, "row", row_count).reshape(width, rank)
        wide = share(wide_mine, "row", row_count).reshape(experts, cols, rank)
        gram = share(gram_slab, "col", col_count).reshape(slabs, experts, width, rank)
        gram = jnp.swapaxes(gram, 0, 1).reshape(experts, rank, rank)

        inverse = inverse_factor(gram)
        inv_high, inv_low = split_halves(inverse)

        def solve(value):
            return jnp.einsum(
                "erk,elk->erl", value, inv_high, preferred_element_type=jnp.float32
            ) + jnp.einsum("erk,elk->erl", value, inv_low, preferred_element_type=jnp.float32)

        reduced = solve(wide)
        squares = jnp.sum(reduced * reduced, axis=1)
        squares = jnp.sum(share(squares, "col", col_count), axis=0)[:, None, :]
        orthonormal = solve(projected).astype(jnp.bfloat16)
        new_basis = (reduced * lax.rsqrt(squares + 1e-06)).astype(jnp.bfloat16)
        momentum_new = buffer - 0.1 * jnp.einsum(
            "erk,eck->erc",
            orthonormal,
            reduced.astype(jnp.bfloat16),
            preferred_element_type=jnp.float32,
        )
        update_scale = math.sqrt(ROWS * COLS / RANK)
        direction = (
            update_scale
            * jnp.einsum(
                "erk,eck->erc", orthonormal, new_basis, preferred_element_type=jnp.float32
            )
        ).astype(jnp.bfloat16)
        return (momentum_new, direction)

    return local


def solution(mesh):
    placed = (P(None, "row", "col"), P(None, "row", "col"), P(None, "col", None))
    return jax.shard_map(
        make_local(mesh.shape["row"], mesh.shape["col"]),
        mesh=mesh,
        in_specs=placed,
        out_specs=(P(None, "row", "col"), P(None, "row", "col")),
        check_vma=False,
    )
```

time: 766 us -> 175 us (0.23)
  waiting for transfers between devices: 437 us -> 36.2 us
  other arithmetic: 242 us -> 1.86 us
  blocking collectives: 17 us -> 62.4 us
  Pallas kernels: 0 us -> 35 us
  local copies, waits for them, and re-layouts: 26.9 us -> 6.9 us
  starting transfers between devices: 0.63 us -> 20.4 us
  between operations: 14.9 us -> 0.81 us
  matrix products: 22.7 us -> 11.1 us
    another operation x20 -> x0, other arithmetic: 239 us -> none  [the longest x16 155 us: orthonormalize(): factor = jnp.linalg.cholesky(gram_full)]
    psum x2 -> x0, waiting for transfers between devices: 213 us -> none  [the longest x1 144 us: local(): lax.psum(jnp.einsum('erc,erk->eck', buffer_half, orthonormal, preferred_e...]
    unnamed x5 -> x0, waiting for transfers between devices: 149 us -> none
    all_gather x1 -> x0, waiting for transfers between devices: 74.7 us -> none  [local(): gram_full = lax.all_gather(gram_piece, 'row', axis=1, tiled=True)]
    all_to_all x0 -> x3, blocking collectives: none -> 62.4 us  [spread(): return lax.all_to_all(chunks, axis, split_axis=0, concat_axis=0, tiled=True)]
    all_to_all x0 -> x4, waiting for transfers between devices: none -> 36.2 us  [spread(): return lax.all_to_all(chunks, axis, split_axis=0, concat_axis=0, tiled=True)]
    pallas_call x0 -> x1, Pallas kernels: none -> 35 us  [inverse_factor(): pl.pallas_call(factor_kernel, out_shape=jax.ShapeDtypeStruct(gram.shape,...]
    all_to_all x0 -> x4, starting transfers between devices: none -> 20.4 us  [spread(): return lax.all_to_all(chunks, axis, split_axis=0, concat_axis=0, tiled=True)]
  transfers between devices with their start and end apart: 4 -> 4, of which waited for: 4 -> 3; matrix products, arithmetic and copies ran while one was open for 0% -> 3% of each run, Pallas kernels for 0% -> 20%
where the time goes in v1:
time: 175 us
  blocking collectives  62.4 us (36%)
  waiting for transfers between devices  36.2 us (21%)
  Pallas kernels  35 us (20%)
  starting transfers between devices  20.4 us (12%)
  matrix products  11.1 us (6%)
  local copies, waits for them, and re-layouts  6.9 us (4%)
  other arithmetic  1.86 us (1%)
    all_to_all x3, blocking collectives, spread(): return lax.all_to_all(chunks, axis, split_axis=0, concat_axis=0, tiled=True)  62.4 us
    all_to_all x4, waiting for transfers between devices, spread(): return lax.all_to_all(chunks, axis, split_axis=0, concat_axis=0, tiled=True)  36.2 us
    pallas_call x1, Pallas kernels, inverse_factor(): pl.pallas_call(factor_kernel, out_shape=jax.ShapeDtypeStruct(gram.shape,...  35 us
    all_to_all x4, starting transfers between devices, spread(): return lax.all_to_all(chunks, axis, split_axis=0, concat_axis=0, tiled=True)  20.4 us
    broadcast_in_dim x6, local copies, waits for them, and re-layouts, share(): return spread(jnp.broadcast_to(value[None], (count,) + value.shape), axis)  4 us
    dot_general x2, matrix products, solve(): jnp.einsum('erk,elk->erl', value, inv_low, preferred_element_type=jnp.flo...  3.83 us
  transfers between devices with their start and end apart: 4, of which 3 were waited for; matrix products, arithmetic and copies ran while one was open for 3% of the time, Pallas kernels for 20%

profile of v1, /device:TPU:1, one launch (start us, length us, event | category | flops | bytes accessed | tf_op | source)
XLA Modules:
  0.0 174.7 jit_solution(15876443489310327787)
XLA Ops:
  0.6 0.0 copy-start
  0.6 0.0 copy-start.5
  0.7 0.0 copy-start.3
  0.7 1.0 copy-done
  1.7 1.4 convolution_convert_fusion.1
  3.0 14.5 %all_to_all.35 = bf16[8,56,512]{2,1,0:T(8,128)(2,1)S(1)} all-to-all(bf16[8,56,512]{2,1,0:T(8,128)(2,1)S(1)} %bitcast.34), channel_id=1, replica_groups=mesh['row'=32,'col'=8] {'col'}, dimensions={0} | all-to-all | bytes 917504 | tf_op jit(solution)/shard_map/all_to_all | solution.py:138
  17.6 0.1 reduce_sum.48
  17.6 0.8 broadcast_in_dim.12
  18.4 4.3 %all-to-all-start.1 = ((bf16[8,56,512]{2,1,0:T(8,128)(2,1)}), bf16[8,56,512]{2,1,0:T(8,128)(2,1)S(1)}, u32[]{:S(2)}, u32[]{:S(2)}) async-start(bf16[8,56,512]{2,1,0:T(8,128)(2,1)} %broadcast_in_dim.12), calls=%async_computation.1 | async-start | bytes 917504 | tf_op jit(solution)/shard_map/all_to_all | solution.py:138
  22.8 8.8 %all-to-all-done.1 = bf16[8,56,512]{2,1,0:T(8,128)(2,1)S(1)} async-done(((bf16[8,56,512]{2,1,0:T(8,128)(2,1)}), bf16[8,56,512]{2,1,0:T(8,128)(2,1)S(1)}, u32[]{:S(2)}, u32[]{:S(2)}) %all-to-all-start.1) | async-done | bytes 458784 | tf_op jit(solution)/shard_map/all_to_all | solution.py:138
  31.6 0.0 copy-done.5
  31.6 0.0 copy-done.3
  31.6 0.3 convolution_convert_fusion
  31.9 0.1 dynamic-slice_bitcast_fusion
  32.0 0.1 copy.21
  32.2 0.2 subtract_convert_fusion.1
  32.4 0.1 copy.24
  32.5 0.1 copy.23
  32.6 0.2 pad_maximum_fusion
  32.7 30.5 %all_to_all.36 = bf16[32,24,512]{2,1,0:T(8,128)(2,1)S(1)} all-to-all(bf16[32,24,512]{2,1,0:T(8,128)(2,1)S(1)} %pad_maximum_fusion), channel_id=1, replica_groups=mesh['row'=32,'col'=8] {'row'}, dimensions={0} | all-to-all | bytes 1572864 | tf_op jit(solution)/shard_map/all_to_all | solution.py:138
  63.3 0.2 convert_element_type.61
  63.5 0.0 copy-start.2
  63.5 1.1 copy-done.2
  64.6 0.1 fusion.6
  64.8 17.4 %all_to_all.37 = f32[32,4,512]{2,1,0:T(4,128)S(1)} all-to-all(f32[32,4,512]{2,1,0:T(4,128)S(1)} %broadcast_in_dim.13), channel_id=1, replica_groups=mesh['row'=32,'col'=8] {'row'}, dimensions={0} | all-to-all | bytes 524288 | tf_op jit(solution)/shard_map/all_to_all | solution.py:138
  82.1 0.1 broadcast_in_dim.14
  82.2 1.6 broadcast_in_dim.15
  83.8 7.1 %all-to-all-start.4 = ((f32[8,128,512]{2,1,0:T(8,128)}), f32[8,128,512]{2,1,0:T(8,128)S(1)}, u32[]{:S(2)}, u32[]{:S(2)}) async-start(f32[8,128,512]{2,1,0:T(8,128)} %broadcast_in_dim.15), calls=%async_computation.4 | async-start | bytes 4194304 | tf_op jit(solution)/shard_map/all_to_all | solution.py:138
  90.9 1.3 slice_reduce_fusion
  92.2 25.1 %all-to-all-done.4 = f32[8,128,512]{2,1,0:T(8,128)S(1)} async-done(((f32[8,128,512]{2,1,0:T(8,128)}), f32[8,128,512]{2,1,0:T(8,128)S(1)}, u32[]{:S(2)}, u32[]{:S(2)}) %all-to-all-start.4) | async-done | bytes 2097184 | tf_op jit(solution)/shard_map/all_to_all | solution.py:138
  117.3 0.8 broadcast_in_dim.16
  118.1 4.8 %all-to-all-start.5 = ((bf16[32,16,512]{2,1,0:T(8,128)(2,1)}), bf16[32,16,512]{2,1,0:T(8,128)(2,1)}, u32[]{:S(2)}, u32[]{:S(2)}) async-start(bf16[32,16,512]{2,1,0:T(8,128)(2,1)} %broadcast_in_dim.16), calls=%async_computation.5 | async-start | bytes 1048576 | tf_op jit(solution)/shard_map/all_to_all | solution.py:138
  122.9 0.3 copy.25
  123.2 35.0 %shard_map.50 = f32[2,512,512]{2,1,0:T(8,128)S(1)} custom-call(f32[2,512,512]{2,1,0:T(8,128)S(1)} %bitcast.26), custom_call_target="tpu_custom_call" | custom-call | tf_op jit(solution)/shard_map/pallas_call | solution.py:127
  158.2 0.5 fusion.14
  158.7 1.3 fusion
  160.0 0.0 all-to-all-done.5
  160.0 1.5 fusion.12
  161.5 0.0 copy-start.4
  161.5 2.6 %multiply_reduce_fusion = (f32[2,512]{1,0:T(2,128)S(1)}, f32[2,256,512]{2,1,0:T(8,128)}) fusion(f32[2,256,512]{2,1,0:T(8,128)S(1)} %fusion.12, bf16[2,256,512]{2,1,0:T(8,128)(2,1)} %bitcast.10, f32[2,512,512]{2,1,0:T(8,128)S(1)} %shard_map.50), kind=kOutput, calls=%fused_computation.12 | convolution fusion | flops 271318016 | bytes 4722688 | tf_op jit(solution)/shard_map/erk,elk->erl/dot_general | solution.py:193
  164.1 0.0 copy-start.1
  164.1 0.6 broadcast_in_dim.17
  164.7 4.2 %all-to-all-start.6 = ((f32[8,2,512]{2,1,0:T(2,128)}), f32[8,2,512]{2,1,0:T(2,128)S(1)}, u32[]{:S(2)}, u32[]{:S(2)}) async-start(f32[8,2,512]{2,1,0:T(2,128)} %broadcast_in_dim.17), calls=%async_computation.6 | async-start | bytes 65536 | tf_op jit(solution)/shard_map/all_to_all | solution.py:138
  168.9 0.0 copy-done.4
  168.9 2.4 %fusion.1 = f32[2,224,256]{2,1,0:T(8,128)} fusion(bf16[2,224,512]{2,1,0:T(8,128)(2,1)S(1)} %copy-done.4, f32[2,256,512]{2,1,0:T(8,128)} %get-tuple-element.5, f32[2,224,256]{2,1,0:T(8,128)S(1)} %copy-done.3, bf16[2,224,256]{2,1,0:T(8,128)(2,1)} %param.4), kind=kOutput, calls=%fused_computation.8 | convolution fusion | flops 118161408 | bytes 2654208 | tf_op jit(solution)/shard_map/erk,eck->erc/dot_general | solution.py:200
  171.3 2.4 %all-to-all-done.6 = f32[8,2,512]{2,1,0:T(2,128)S(1)} async-done(((f32[8,2,512]{2,1,0:T(2,128)}), f32[8,2,512]{2,1,0:T(2,128)S(1)}, u32[]{:S(2)}, u32[]{:S(2)}) %all-to-all-start.6) | async-done | bytes 32800 | tf_op jit(solution)/shard_map/all_to_all | solution.py:138
  173.7 0.0 copy-done.1
  173.7 1.0 fusion.2
  (4 shorter events, 0.1 us)
Async XLA Ops:
  0.6 1.0 copy-start
  0.6 30.9 %copy-start.5 = (bf16[2,224,256]{2,1,0:T(8,128)(2,1)S(1)}, bf16[2,224,256]{2,1,0:T(8,128)(2,1)}, u32[]{:S(2)}) copy-start(bf16[2,224,256]{2,1,0:T(8,128)(2,1)} %param.4) | copy-start | bytes 688132
  0.7 30.9 %copy-start.3 = (f32[2,224,256]{2,1,0:T(8,128)S(1)}, f32[2,224,256]{2,1,0:T(8,128)}, u32[]{:S(2)}) copy-start(f32[2,224,256]{2,1,0:T(8,128)} %param.3) | copy-start | bytes 1376260
  18.4 13.1 %all-to-all-start.1 = ((bf16[8,56,512]{2,1,0:T(8,128)(2,1)}), bf16[8,56,512]{2,1,0:T(8,128)(2,1)S(1)}, u32[]{:S(2)}, u32[]{:S(2)}) async-start(bf16[8,56,512]{2,1,0:T(8,128)(2,1)} %broadcast_in_dim.12), calls=%async_computation.1 | async-start | bytes 917504 | tf_op jit(solution)/shard_map/all_to_all | solution.py:138
  63.5 1.1 copy-start.2
  83.8 33.4 %all-to-all-start.4 = ((f32[8,128,512]{2,1,0:T(8,128)}), f32[8,128,512]{2,1,0:T(8,128)S(1)}, u32[]{:S(2)}, u32[]{:S(2)}) async-start(f32[8,128,512]{2,1,0:T(8,128)} %broadcast_in_dim.15), calls=%async_computation.4 | async-start | bytes 4194304 | tf_op jit(solution)/shard_map/all_to_all | solution.py:138
  118.1 41.9 %all-to-all-start.5 = ((bf16[32,16,512]{2,1,0:T(8,128)(2,1)}), bf16[32,16,512]{2,1,0:T(8,128)(2,1)}, u32[]{:S(2)}, u32[]{:S(2)}) async-start(bf16[32,16,512]{2,1,0:T(8,128)(2,1)} %broadcast_in_dim.16), calls=%async_computation.5 | async-start | bytes 1048576 | tf_op jit(solution)/shard_map/all_to_all | solution.py:138
  161.5 7.4 %copy-start.4 = (bf16[2,224,512]{2,1,0:T(8,128)(2,1)S(1)}, bf16[2,224,512]{2,1,0:T(8,128)(2,1)}, u32[]{:S(2)}) copy-start(bf16[2,224,512]{2,1,0:T(8,128)(2,1)} %fusion) | copy-start | bytes 1376260
  164.1 9.6 %copy-start.1 = (f32[2,256,512]{2,1,0:T(8,128)S(1)}, f32[2,256,512]{2,1,0:T(8,128)}, u32[]{:S(2)}) copy-start(f32[2,256,512]{2,1,0:T(8,128)} %get-tuple-element.5) | copy-start | bytes 3145732
  164.7 8.9 %all-to-all-start.6 = ((f32[8,2,512]{2,1,0:T(2,128)}), f32[8,2,512]{2,1,0:T(2,128)S(1)}, u32[]{:S(2)}, u32[]{:S(2)}) async-start(f32[8,2,512]{2,1,0:T(2,128)} %broadcast_in_dim.17), calls=%async_computation.6 | async-start | bytes 65536 | tf_op jit(solution)/shard_map/all_to_all | solution.py:138

commit v2 on v0

v2 whole, which is shorter than its diff:
```python
import math

import jax
import jax.numpy as jnp
import numpy as np
from jax import lax
from jax.experimental import pallas as pl
from jax.experimental.pallas import tpu as pltpu
from jax.sharding import PartitionSpec as P

ROWS = 7168
COLS = 2048
RANK = 512
BLOCK = 128
PANEL = 8
BLOCKS = RANK // BLOCK
PANELS = BLOCK // PANEL
KEPT = 3
X_SIZE = 4
Z_SIZE = 8


def lanes_of(value, lane):
    return jnp.broadcast_to(value[:, lane : lane + 1], (PANEL, BLOCK))


def row_of(value, row):
    return jnp.broadcast_to(value[row : row + 1, :], (PANEL, BLOCK))


def added(terms):
    while len(terms) > 1:
        terms = [terms[i] + terms[i + 1] for i in range(0, len(terms), 2)]
    return terms[0]


def small_inverse(cols, row):
    cols = list(cols)
    factor = [jnp.zeros((PANEL, BLOCK), jnp.float32) for _ in range(PANEL)]
    for j in range(0, PANEL, 2):
        first, second = row == j, row == j + 1
        both = first | second
        left, right = cols[j], cols[j + 1]
        a, b, c = row_of(left, j), row_of(right, j), row_of(right, j + 1)
        root = lax.rsqrt(a * c - b * b)
        inv = root * root
        ia, ib, ic = c * inv, -(b * inv), a * inv
        root_a = lax.rsqrt(a)
        ratio = b * (root_a * root_a)
        root_c = lax.rsqrt(c - b * ratio)
        left_m = jnp.where(first, -1.0, jnp.where(second, 0.0, left))
        right_m = jnp.where(first, 0.0, jnp.where(second, -1.0, right))
        for k in range(PANEL):
            if k in (j, j + 1):
                continue
            top, low = row_of(cols[k], j), row_of(cols[k], j + 1)
            rest = jnp.where(both, 0.0, cols[k])
            cols[k] = rest - (left_m * (ia * top + ib * low) + right_m * (ib * top + ic * low))
            if k < j:
                factor[k] = jnp.where(
                    first, top * root_a, jnp.where(second, (low - ratio * top) * root_c, factor[k])
                )
        factor[j] = jnp.where(first, root_a, jnp.where(second, -(ratio * root_c), factor[j]))
        factor[j + 1] = jnp.where(second, root_c, factor[j + 1])
        cols[j] = -(left_m * ia + right_m * ib)
        cols[j + 1] = -(left_m * ib + right_m * ic)
    return cols, factor


def combine(cols, value):
    return added([cols[j] * row_of(value, j) for j in range(PANEL)])


def block_inverse_factor(groups):
    row = lax.broadcasted_iota(jnp.int32, (PANEL, BLOCK), 0)
    lane = lax.broadcasted_iota(jnp.int32, (PANEL, BLOCK), 1)
    block = [lanes_of(groups[0], j) for j in range(PANEL)]
    for k in range(PANELS):
        base = k * PANEL
        inside = (lane >= base) & (lane < base + PANEL)
        full, factor = small_inverse(block, row)
        panel = jnp.where(inside, (lane == row + base).astype(jnp.float32), groups[k])
        if k + 1 < PANELS:
            down = [lanes_of(groups[k + 1], base + j) for j in range(PANEL)]
            block = []
            for m in range(base + PANEL, base + 2 * PANEL):
                column = combine(full, lanes_of(groups[k], m))
                block.append(lanes_of(groups[k + 1], m) - combine(down, column))
            solved = combine(full, panel)
            rows = [row_of(solved, j) for j in range(PANEL)]
            for i in range(k + 1, PANELS):
                old = groups[i]
                change = added([lanes_of(old, base + j) * rows[j] for j in range(PANEL)])
                groups[i] = jnp.where(inside, 0.0, old) - change
        groups[k] = jnp.where(lane <= row + base, combine(factor, panel), 0.0)
    return groups


def split_halves(value):
    high = value.astype(jnp.bfloat16)
    low = (value - high.astype(jnp.float32)).astype(jnp.bfloat16)
    return high, low


def product(left, right, left_axis):
    return lax.dot_general(
        jnp.concatenate([left[0], left[0], left[1]], axis=left_axis),
        jnp.concatenate([right[0], right[1], right[0]], axis=0),
        (((left_axis,), (0,)), ((), ())),
        preferred_element_type=jnp.float32,
    )


def factor_kernel(where_ref, own_ref, one_ref, two_ref, three_ref, out_ref, slab_ref, work_ref):
    here = where_ref[0]
    for back, ref in enumerate((own_ref, one_ref, two_ref, three_ref)):
        slab_ref[lax.rem(here + (BLOCKS - back), BLOCKS)] = ref[...]

    def block(i, j):
        if j - i < KEPT:
            return slab_ref[i, :, (j - i) * BLOCK : (j - i + 1) * BLOCK]
        return slab_ref[j, :, (BLOCKS + i - j) * BLOCK : (BLOCKS + i - j + 1) * BLOCK].T

    most = jnp.maximum(
        jnp.maximum(block(0, 0), block(1, 1)), jnp.maximum(block(2, 2), block(3, 3))
    )
    most = jnp.max(jnp.max(most, axis=0, keepdims=True), axis=1, keepdims=True)
    scale = 1.0 / most
    for i in range(BLOCKS):
        for j in range(i, BLOCKS):
            work_ref[i, :, j * BLOCK : (j + 1) * BLOCK] = block(i, j) * scale
    back_scale = lax.rsqrt(most)

    for k in range(BLOCKS):
        at, to = k * BLOCK, (k + 1) * BLOCK
        groups = [work_ref[k, i * PANEL : (i + 1) * PANEL, at:to] for i in range(PANELS)]
        inverse = jnp.concatenate(block_inverse_factor(groups), axis=0)
        work_ref[k, :, at:to] = inverse
        pair = split_halves(inverse)
        if k > 0:
            work_ref[k, :, :at] = product(pair, split_halves(work_ref[k, :, :at]), 1)
        if k + 1 < BLOCKS:
            upper = product(pair, split_halves(work_ref[k, :, to:]), 1)
            work_ref[k, :, to:] = upper
            upper = split_halves(upper)
            whole = split_halves(work_ref[k])
            for i in range(k + 1, BLOCKS):
                left = tuple(part[:, (i - k - 1) * BLOCK : (i - k) * BLOCK] for part in upper)
                work_ref[i, :, i * BLOCK :] -= product(
                    left, tuple(part[:, i * BLOCK :] for part in whole), 0
                )
                change = product(left, tuple(part[:, :to] for part in whole), 0)
                if k > 0:
                    work_ref[i, :, :at] -= change[:, :at]
                work_ref[i, :, at:to] = -change[:, at:]
    for i in range(BLOCKS):
        to = (i + 1) * BLOCK
        rows = slice(i * BLOCK, to)
        out_ref[rows, :to] = (work_ref[i, :, :to] * back_scale).astype(jnp.bfloat16)
        if to < RANK:
            out_ref[rows, to:] = jnp.zeros((BLOCK, RANK - to), jnp.bfloat16)


def inverse_factor(where, slabs):
    vmem = pl.BlockSpec(memory_space=pltpu.VMEM)
    return pl.pallas_call(
        factor_kernel,
        out_shape=jax.ShapeDtypeStruct((RANK, RANK), jnp.bfloat16),
        in_specs=[pl.BlockSpec(memory_space=pltpu.SMEM)] + [vmem] * BLOCKS,
        out_specs=vmem,
        scratch_shapes=[
            pltpu.VMEM((BLOCKS, BLOCK, KEPT * BLOCK), jnp.float32),
            pltpu.VMEM((BLOCKS, BLOCK, RANK), jnp.float32),
        ],
        compiler_params=pltpu.CompilerParams(vmem_limit_bytes=24 * 1024 * 1024),
        cost_estimate=pl.CostEstimate(flops=2 * 10**10, bytes_accessed=0, transcendentals=0),
    )(where, *slabs)


def sum_kernel(*refs):
    refs[-1][...] = added([ref[...] for ref in refs[:-2]])


def summed(terms, after):
    vmem = pl.BlockSpec(memory_space=pltpu.VMEM)
    return pl.pallas_call(
        sum_kernel,
        out_shape=jax.ShapeDtypeStruct(terms[0].shape, terms[0].dtype),
        in_specs=[vmem] * len(terms) + [pl.BlockSpec(memory_space=pl.ANY)],
        out_specs=vmem,
    )(*terms, after)


def spread(chunks, axis):
    return lax.all_to_all(chunks, axis, split_axis=0, concat_axis=0, tiled=True)


def share(value, axis, count):
    return spread(jnp.broadcast_to(value[None], (count,) + value.shape), axis)


def swap(value, axis, count, mask):
    return lax.ppermute(value, axis, [(i, i ^ mask) for i in range(count)])


def pick(first, value, other):
    return jnp.stack([jnp.where(first, value, other), jnp.where(first, other, value)])


def make_local(row_count, col_count):
    def bit(index, mask):
        return lax.convert_element_type(lax.bitwise_and(index, np.uint32(mask)) != 0, jnp.uint32)

    def item(stack, index):
        return lax.dynamic_index_in_dim(stack, index, 0, keepdims=False)

    def quad(value, axis, count, low):
        return [value] + [swap(value, axis, count, step * low) for step in (1, 2, 3)]

    def row_sum(value, row, after):
        pieces = value.reshape(X_SIZE, value.shape[0] // X_SIZE, value.shape[1])
        plane = lax.div(row, np.uint32(Z_SIZE))
        terms = [item(pieces, plane)]
        for step in range(1, X_SIZE):
            send = item(pieces, lax.bitwise_xor(plane, np.uint32(step)))
            terms.append(swap(send, "row", row_count, step * Z_SIZE))
        value = added(terms)
        value = value + swap(value, "row", row_count, 4)
        value = summed(quad(value, "row", row_count, 1), after)
        parts = quad(value, "row", row_count, Z_SIZE)
        low = bit(plane, 1) == 0
        both = pick(bit(plane, 2) == 0, pick(low, parts[0], parts[1]), pick(low, parts[2], parts[3]))
        return both.reshape(X_SIZE * value.shape[0], value.shape[1])

    def local(momentum, gradient, basis_in):
        experts, rows, cols = momentum.shape
        rank = basis_in.shape[-1]
        row = lax.axis_index("row").astype(jnp.uint32)
        col = lax.axis_index("col").astype(jnp.uint32)
        expert = lax.rem(col, np.uint32(experts))
        place = lax.div(col, np.uint32(experts))
        first = expert == 0
        buffer = momentum + gradient.astype(jnp.float32)
        half = buffer.astype(jnp.bfloat16)
        partial = jnp.einsum(
            "erc,eck->erk", half, basis_in, preferred_element_type=jnp.float32
        ).astype(jnp.bfloat16)
        term = item(partial, expert) + swap(item(partial, 1 - expert), "col", col_count, 1)
        terms = [part.astype(jnp.float32) for part in quad(term, "col", col_count, experts)]
        projected = added(terms).astype(jnp.bfloat16)

        turned = lax.dynamic_slice_in_dim(
            jnp.concatenate([projected, projected[:, : (KEPT - 1) * BLOCK]], axis=1),
            place * np.uint32(BLOCK),
            KEPT * BLOCK,
            axis=1,
        )
        whole = jnp.stack(
            [item(half, expert), swap(item(half, 1 - expert), "col", col_count, 1)]
        )
        wide = jnp.einsum("hrc,rk->hck", whole, projected, preferred_element_type=jnp.float32)
        wide = wide.astype(jnp.bfloat16).reshape(row_count, 2 * cols // row_count, rank)
        wide = jnp.sum(spread(wide, "row").astype(jnp.float32), axis=0).astype(jnp.bfloat16)

        slab = row_sum(
            jnp.einsum("rk,rl->kl", turned[:, :BLOCK], turned, preferred_element_type=jnp.float32), row, wide
        )
        slabs = [slab]
        for step in range(1, BLOCKS):
            turn = [(i, (i + step * experts) % col_count) for i in range(col_count)]
            slabs.append(lax.ppermute(slab, "col", turn))
        wide = share(wide, "row", row_count).reshape(2 * cols, rank)

        inverse = inverse_factor(jnp.reshape(place, (1,)).astype(jnp.int32), slabs)

        def solve(value):
            return jnp.einsum("rk,lk->rl", value, inverse, preferred_element_type=jnp.float32)

        reduced = solve(wide)
        squares = jnp.sum(reduced * reduced, axis=0, keepdims=True)
        squares = added(quad(squares, "col", col_count, experts))
        orthonormal = solve(projected).astype(jnp.bfloat16)

        def outer(right):
            value = jnp.einsum("rk,ck->rc", orthonormal, right, preferred_element_type=jnp.float32)
            return value[:, :cols], value[:, cols:]

        own, other = outer(reduced.astype(jnp.bfloat16))
        other = swap((0.1 * other).astype(jnp.bfloat16), "col", col_count, 1)
        momentum_new = buffer - pick(first, 0.1 * own, other.astype(jnp.float32))
        new_basis = (reduced * lax.rsqrt(squares + 1e-06)).astype(jnp.bfloat16)
        update_scale = math.sqrt(ROWS * COLS / RANK)
        own, other = outer(new_basis)
        own = (update_scale * own).astype(jnp.bfloat16)
        other = swap((update_scale * other).astype(jnp.bfloat16), "col", col_count, 1)
        return (momentum_new, pick(first, own, other))

    return local


def solution(mesh):
    placed = (P(None, "row", "col"), P(None, "row", "col"), P(None, "col", None))
    return jax.shard_map(
        make_local(mesh.shape["row"], mesh.shape["col"]),
        mesh=mesh,
        in_specs=placed,
        out_specs=(P(None, "row", "col"), P(None, "row", "col")),
        check_vma=False,
    )
```

time: 766 us -> 113 us (0.15)
  waiting for transfers between devices: 437 us -> 23.6 us
  other arithmetic: 242 us -> 4.66 us
  starting transfers between devices: 0.63 us -> 57.1 us
  local copies, waits for them, and re-layouts: 26.9 us -> 2.27 us
  Pallas kernels: 0 us -> 20.5 us
  matrix products: 22.7 us -> 3.11 us
  blocking collectives: 17 us -> 0 us
  between operations: 14.9 us -> 0.93 us
    another operation x20 -> x6, other arithmetic: 239 us -> 1.63 us  [pick(): jnp.stack([jnp.where(first, value, other), jnp.where(first, other, value)])]
    psum x2 -> x0, waiting for transfers between devices: 213 us -> none  [the longest x1 144 us: local(): lax.psum(jnp.einsum('erc,erk->eck', buffer_half, orthonormal, preferred_e...]
    unnamed x5 -> x0, waiting for transfers between devices: 149 us -> none
    all_gather x1 -> x0, waiting for transfers between devices: 74.7 us -> none  [local(): gram_full = lax.all_gather(gram_piece, 'row', axis=1, tiled=True)]
    ppermute x0 -> x23, starting transfers between devices: none -> 42.5 us  [the longest x20 39.2 us: swap(): return lax.ppermute(value, axis, [(i, i ^ mask) for i in range(count)])]
    ppermute x0 -> x23, waiting for transfers between devices: none -> 23.6 us  [the longest x20 22.4 us: swap(): return lax.ppermute(value, axis, [(i, i ^ mask) for i in range(count)])]
    pallas_call x0 -> x2, Pallas kernels: none -> 20.5 us  [the longest x1 19 us: inverse_factor(): pl.pallas_call(factor_kernel, out_shape=jax.ShapeDtypeStruct((RANK, RANK)...]
    psum x1 -> x0, blocking collectives: 17 us -> none  [local(): squares = lax.psum(jnp.sum(reduced * reduced, axis=1, keepdims=True), 'col')]
  transfers between devices with their start and end apart: 4 -> 25, of which waited for: 4 -> 12; matrix products, arithmetic and copies ran while one was open for 0% -> 4% of each run, Pallas kernels for 0% -> 17%
where the time goes in v2:
time: 113 us; the launch traced here: 112 us
  starting transfers between devices  57.1 us (51%)
  waiting for transfers between devices  23.6 us (21%)
  Pallas kernels  20.5 us (18%)
  other arithmetic  4.66 us (4%)
  matrix products  3.11 us (3%)
  local copies, waits for them, and re-layouts  2.27 us (2%)
    ppermute x20, starting transfers between devices, swap(): return lax.ppermute(value, axis, [(i, i ^ mask) for i in range(count)])  39.2 us
    ppermute x20, waiting for transfers between devices, swap(): return lax.ppermute(value, axis, [(i, i ^ mask) for i in range(count)])  22.4 us
    pallas_call x1, Pallas kernels, inverse_factor(): pl.pallas_call(factor_kernel, out_shape=jax.ShapeDtypeStruct((RANK, RANK)...  19 us
    all_to_all x2, starting transfers between devices, spread(): return lax.all_to_all(chunks, axis, split_axis=0, concat_axis=0, tiled=True)  14.6 us
    ppermute x3, starting transfers between devices, local(): slabs.append(lax.ppermute(slab, 'col', turn))  3.3 us
  transfers between devices with their start and end apart: 25, of which 12 were waited for; matrix products, arithmetic and copies ran while one was open for 4% of the time, Pallas kernels for 17%

profile of v2, /device:TPU:1, one launch (start us, length us, event | category | flops | bytes accessed | tf_op | source)
XLA Modules:
  0.0 112.2 jit_solution(13934525573013373421)
XLA Ops:
  0.7 1.2 %fusion.4 = bf16[2,224,256]{2,1,0:T(8,128)(2,1)S(1)} fusion(f32[2,224,256]{2,1,0:T(8,128)} %param.3, bf16[2,224,256]{2,1,0:T(8,128)(2,1)} %param.4), kind=kLoop, calls=%fused_computation.14 | loop fusion | flops 344064 | bytes 917504 | tf_op jit(solution)/shard_map/convert_element_type | solution.py:244
  2.2 3.3 %collective-permute-start = (bf16[224,512]{1,0:T(8,128)(2,1)S(1)}, bf16[224,512]{1,0:T(8,128)(2,1)S(1)}, u32[]{:S(2)}, u32[]{:S(2)}) collective-permute-start(bf16[224,512]{1,0:T(8,128)(2,1)S(1)} %dynamic-slice_bitcast_fusion), channel_id=1, source_target_pairs={{0,1},{1,0},{2,3},{3,2},{4,5},{5,4},{6,7},{7,6},{8,9},{9,8},{10,11... | collective-permute-start | bytes 688136 | tf_op jit(solution)/shard_map/ppermute | solution.py:203
  5.6 1.1 collective-permute-done
  6.7 1.1 collective-permute-start.3
  7.8 0.3 collective-permute-start.2
  8.2 1.9 %collective-permute-start.1 = (bf16[224,512]{1,0:T(8,128)(2,1)S(1)}, bf16[224,512]{1,0:T(8,128)(2,1)S(1)}, u32[]{:S(2)}, u32[]{:S(2)}) collective-permute-start(bf16[224,512]{1,0:T(8,128)(2,1)S(1)} %bitcast_add_fusion), channel_id=1, source_target_pairs={{0,2},{1,3},{2,0},{3,1},{4,6},{5,7},{6,4},{7,5},{8,10},{9,11},{10,... | collective-permute-start | bytes 688136 | tf_op jit(solution)/shard_map/ppermute | solution.py:203
  10.1 1.3 %collective-permute-start.11 = (bf16[224,256]{1,0:T(8,128)(2,1)S(1)}, bf16[224,256]{1,0:T(8,128)(2,1)S(1)}, u32[]{:S(2)}, u32[]{:S(2)}) collective-permute-start(bf16[224,256]{1,0:T(8,128)(2,1)S(1)} %get-tuple-element.7), channel_id=1, source_target_pairs={{0,1},{1,0},{2,3},{3,2},{4,5},{5,4},{6,7},{7,6},{8,9},{9,8},{10,11... | collective-permute-start | bytes 344072 | tf_op jit(solution)/shard_map/ppermute | solution.py:203
  11.4 8.4 %collective-permute-done.3 = bf16[224,512]{1,0:T(8,128)(2,1)S(1)} collective-permute-done((bf16[224,512]{1,0:T(8,128)(2,1)S(1)}, bf16[224,512]{1,0:T(8,128)(2,1)S(1)}, u32[]{:S(2)}, u32[]{:S(2)}) %collective-permute-start.3) | collective-permute-done | bytes 229408 | tf_op jit(solution)/shard_map/ppermute | solution.py:203
  19.7 0.3 collective-permute-done.1
  20.2 1.1 %convolution_convert_fusion = bf16[2,256,512]{2,1,0:T(8,128)(2,1)} fusion(bf16[1,224,256]{2,1,0:T(8,128)(2,1)S(1)} %bitcast.64, bf16[1,224,256]{2,1,0:T(8,128)(2,1)S(1)} %get-tuple-element.6, bf16[224,512]{1,0:T(8,128)(2,1)S(1)} %add_convert_fusion), kind=kOutput, calls=%fused_computation | convolution fusion | flops 117817344 | bytes 983040 | tf_op jit(solution)/shard_map/hrc,rk->hck/dot_general | solution.py:261
  21.4 9.6 %all-to-all-start = ((bf16[32,16,512]{2,1,0:T(8,128)(2,1)}), bf16[32,16,512]{2,1,0:T(8,128)(2,1)S(1)}, u32[]{:S(2)}, u32[]{:S(2)}) async-start(bf16[32,16,512]{2,1,0:T(8,128)(2,1)} %bitcast.11), calls=%async_computation | async-start | bytes 1048576 | tf_op jit(solution)/shard_map/all_to_all | solution.py:195
  31.3 2.6 %collective-permute-start.6 = (f32[32,384]{1,0:T(8,128)S(1)}, f32[32,384]{1,0:T(8,128)S(1)}, u32[]{:S(2)}, u32[]{:S(2)}) collective-permute-start(f32[32,384]{1,0:T(8,128)S(1)} %get-tuple-element.10), channel_id=1, source_target_pairs={{0,192},{8,200},{16,208},{24,216},{32,224},{40,232},{48,240},{56,2... | collective-permute-start | bytes 147464 | tf_op jit(solution)/shard_map/ppermute | solution.py:203
  33.9 0.5 collective-permute-start.5
  34.6 1.1 collective-permute-done.6
  35.7 3.0 %collective-permute-done.5 = f32[32,384]{1,0:T(8,128)S(1)} collective-permute-done((f32[32,384]{1,0:T(8,128)S(1)}, f32[32,384]{1,0:T(8,128)S(1)}, u32[]{:S(2)}, u32[]{:S(2)}) %collective-permute-start.5) | collective-permute-done | bytes 49184 | tf_op jit(solution)/shard_map/ppermute | solution.py:203
  38.7 6.3 %collective-permute-start.7 = (f32[32,384]{1,0:T(8,128)S(1)}, f32[32,384]{1,0:T(8,128)S(1)}, u32[]{:S(2)}, u32[]{:S(2)}) collective-permute-start(f32[32,384]{1,0:T(8,128)S(1)} %fusion.19), channel_id=1, source_target_pairs={{0,32},{8,40},{16,48},{24,56},{32,0},{40,8},{48,16},{56,24},{64,96... | collective-permute-start | bytes 147464 | tf_op jit(solution)/shard_map/ppermute | solution.py:203
  45.0 4.0 %collective-permute-done.7 = f32[32,384]{1,0:T(8,128)S(1)} collective-permute-done((f32[32,384]{1,0:T(8,128)S(1)}, f32[32,384]{1,0:T(8,128)S(1)}, u32[]{:S(2)}, u32[]{:S(2)}) %collective-permute-start.7) | collective-permute-done | bytes 49184 | tf_op jit(solution)/shard_map/ppermute | solution.py:203
  49.0 1.3 %collective-permute-start.10 = (f32[32,384]{1,0:T(8,128)S(1)}, f32[32,384]{1,0:T(8,128)S(1)}, u32[]{:S(2)}, u32[]{:S(2)}) collective-permute-start(f32[32,384]{1,0:T(8,128)S(1)} %add.50.refs_0_), channel_id=1, source_target_pairs={{0,24},{8,16},{16,8},{24,0},{32,56},{40,48},{48,40},{56,32},{64,88... | collective-permute-start | bytes 147464 | tf_op jit(solution)/shard_map/ppermute | solution.py:203
  50.3 2.3 %collective-permute-start.8 = (f32[32,384]{1,0:T(8,128)S(1)}, f32[32,384]{1,0:T(8,128)S(1)}, u32[]{:S(2)}, u32[]{:S(2)}) collective-permute-start(f32[32,384]{1,0:T(8,128)S(1)} %add.50.refs_0_), channel_id=1, source_target_pairs={{0,8},{8,0},{16,24},{24,16},{32,40},{40,32},{48,56},{56,48},{64,72... | collective-permute-start | bytes 147464 | tf_op jit(solution)/shard_map/ppermute | solution.py:203
  52.7 0.7 reduce_sum.21.refs_4_
  53.4 0.6 collective-permute-done.10.refs_3_
  53.9 1.3 %collective-permute-done.9.refs_2_ = f32[32,384]{1,0:T(8,128)S(1)} collective-permute-done((f32[32,384]{1,0:T(8,128)S(1)}, f32[32,384]{1,0:T(8,128)S(1)}, u32[]{:S(2)}, u32[]{:S(2)}) %collective-permute-start.9) | collective-permute-done | bytes 49184 | tf_op jit(solution)/shard_map/ppermute | solution.py:203
  55.2 0.6 copy-done.6
  55.8 0.6 copy-done.7
  56.5 1.5 %shard_map.50 = f32[32,384]{1,0:T(8,128)} custom-call(f32[32,384]{1,0:T(8,128)} %copy-done.3, f32[32,384]{1,0:T(8,128)} %copy-done.7, f32[32,384]{1,0:T(8,128)} %copy-done.6, f32[32,384]{1,0:T(8,128)} %copy-done.5, bf16[16,512]{1,0:T(8,128)(2,1)} %reduce_sum.21.refs_4_), custom_call_target="tpu_custom_call" | custom-call | tf_op jit(solution)/shard_map/pallas_call | solution.py:186
  58.2 2.6 %collective-permute-start.13 = (f32[32,384]{1,0:T(8,128)}, f32[32,384]{1,0:T(8,128)S(1)}, u32[]{:S(2)}, u32[]{:S(2)}) collective-permute-start(f32[32,384]{1,0:T(8,128)} %shard_map.50), channel_id=1, source_target_pairs={{0,128},{8,136},{16,144},{24,152},{32,160},{40,168},{48,176},{56,1... | collective-permute-start | bytes 147464 | tf_op jit(solution)/shard_map/ppermute | solution.py:203
  60.8 1.0 collective-permute-start.14
  61.8 0.8 select_bitcast_fusion.5
  62.7 0.4 collective-permute-done.13
  63.1 2.1 %collective-permute-done.14 = f32[32,384]{1,0:T(8,128)S(1)} collective-permute-done((f32[32,384]{1,0:T(8,128)}, f32[32,384]{1,0:T(8,128)S(1)}, u32[]{:S(2)}, u32[]{:S(2)}) %collective-permute-start.14) | collective-permute-done | bytes 49184 | tf_op jit(solution)/shard_map/ppermute | solution.py:203
  65.3 2.3 %collective-permute-start.17 = (f32[128,384]{1,0:T(8,128)S(1)}, f32[128,384]{1,0:T(8,128)S(1)}, u32[]{:S(2)}, u32[]{:S(2)}) collective-permute-start(f32[128,384]{1,0:T(8,128)S(1)} %bitcast.52), channel_id=1, source_target_pairs={{0,6},{1,7},{2,0},{3,1},{4,2},{5,3},{6,4},{7,5},{8,14},{9,15},{10,... | collective-permute-start | bytes 589832 | tf_op jit(solution)/shard_map/ppermute | solution.py:271
  67.5 0.3 collective-permute-start.16
  67.9 0.7 collective-permute-start.15
  68.6 0.9 broadcast_in_dim.4
  69.4 5.0 %all-to-all-start.1 = ((bf16[32,16,512]{2,1,0:T(8,128)(2,1)}), bf16[32,16,512]{2,1,0:T(8,128)(2,1)S(1)}, u32[]{:S(2)}, u32[]{:S(2)}) async-start(bf16[32,16,512]{2,1,0:T(8,128)(2,1)} %broadcast_in_dim.4), calls=%async_computation.1 | async-start | bytes 1048576 | tf_op jit(solution)/shard_map/all_to_all | solution.py:195
  74.5 1.2 %collective-permute-done.15.one_ref = f32[128,384]{1,0:T(8,128)S(1)} collective-permute-done((f32[128,384]{1,0:T(8,128)S(1)}, f32[128,384]{1,0:T(8,128)S(1)}, u32[]{:S(2)}, u32[]{:S(2)}) %collective-permute-start.15) | collective-permute-done | bytes 196640 | tf_op jit(solution)/shard_map/ppermute | solution.py:271
  75.7 19.0 %shard_map.51 = bf16[512,512]{1,0:T(8,128)(2,1)S(1)} custom-call(s32[1]{0:T(128)} %bitcast.2.where_ref, f32[128,384]{1,0:T(8,128)S(1)} %bitcast.55, f32[128,384]{1,0:T(8,128)S(1)} %collective-permute-done.15.one_ref, f32[128,384]{1,0:T(8,128)S(1)} %collective-permute-done.16.two_ref, f32[128,384]{1,0:T(8,128)S(1)} %collective-permute-done.17.three_ref), custom_call_target="tpu_custom_call" | custom-call | flops 20000000000 | tf_op jit(solution)/shard_map/pallas_call | solution.py:166
  94.7 0.3 convolution_convert_fusion.2
  95.0 0.5 multiply_reduce_fusion
  95.5 0.9 collective-permute-start.21
  96.4 1.4 %collective-permute-start.20 = (f32[1,512]{1,0:T(1,128)S(1)}, f32[1,512]{1,0:T(1,128)S(1)}, u32[]{:S(2)}, u32[]{:S(2)}) collective-permute-start(f32[1,512]{1,0:T(1,128)S(1)} %bitcast.60), channel_id=1, source_target_pairs={{0,4},{1,5},{2,6},{3,7},{4,0},{5,1},{6,2},{7,3},{8,12},{9,13},{10,... | collective-permute-start | bytes 6152 | tf_op jit(solution)/shard_map/ppermute | solution.py:203
  97.9 1.0 collective-permute-start.19
  98.9 0.3 fusion.2
  99.2 7.8 %collective-permute-start.18 = (bf16[224,256]{1,0:T(8,128)(2,1)S(1)}, bf16[224,256]{1,0:T(8,128)(2,1)S(1)}, u32[]{:S(2)}, u32[]{:S(2)}) collective-permute-start(bf16[224,256]{1,0:T(8,128)(2,1)S(1)} %fusion.9), channel_id=1, source_target_pairs={{0,1},{1,0},{2,3},{3,2},{4,5},{5,4},{6,7},{7,6},{8,9},{9,8},{10,11... | collective-permute-start | bytes 344072 | tf_op jit(solution)/shard_map/ppermute | solution.py:203
  107.0 0.3 fusion
  107.4 3.0 %collective-permute-start.22 = (bf16[224,256]{1,0:T(8,128)(2,1)S(1)}, bf16[224,256]{1,0:T(8,128)(2,1)S(1)}, u32[]{:S(2)}, u32[]{:S(2)}) collective-permute-start(bf16[224,256]{1,0:T(8,128)(2,1)S(1)} %fusion.7), channel_id=1, source_target_pairs={{0,1},{1,0},{2,3},{3,2},{4,5},{5,4},{6,7},{7,6},{8,9},{9,8},{10,11... | collective-permute-start | bytes 344072 | tf_op jit(solution)/shard_map/ppermute | solution.py:203
  110.5 0.8 maximum_subtract_fusion
  111.5 0.7 pad_maximum_fusion
  (50 shorter events, 1.7 us)
Async XLA Ops:
  0.6 1.3 %copy-start = (bf16[2,256,512]{2,1,0:T(8,128)(2,1)S(1)}, bf16[2,256,512]{2,1,0:T(8,128)(2,1)}, u32[]{:S(2)}) copy-start(bf16[2,256,512]{2,1,0:T(8,128)(2,1)} %param.5) | copy-start | bytes 1572868
  2.2 4.4 %collective-permute-start = (bf16[224,512]{1,0:T(8,128)(2,1)S(1)}, bf16[224,512]{1,0:T(8,128)(2,1)S(1)}, u32[]{:S(2)}, u32[]{:S(2)}) collective-permute-start(bf16[224,512]{1,0:T(8,128)(2,1)S(1)} %dynamic-slice_bitcast_fusion), channel_id=1, source_target_pairs={{0,1},{1,0},{2,3},{3,2},{4,5},{5,4},{6,7},{7,6},{8,9},{9,8},{10,11... | collective-permute-start | bytes 688136 | tf_op jit(solution)/shard_map/ppermute | solution.py:203
  6.7 13.0 %collective-permute-start.3 = (bf16[224,512]{1,0:T(8,128)(2,1)S(1)}, bf16[224,512]{1,0:T(8,128)(2,1)S(1)}, u32[]{:S(2)}, u32[]{:S(2)}) collective-permute-start(bf16[224,512]{1,0:T(8,128)(2,1)S(1)} %bitcast_add_fusion), channel_id=1, source_target_pairs={{0,6},{1,7},{2,4},{3,5},{4,2},{5,3},{6,0},{7,1},{8,14},{9,15},{10,... | collective-permute-start | bytes 688136 | tf_op jit(solution)/shard_map/ppermute | solution.py:203
  7.8 11.9 %collective-permute-start.2 = (bf16[224,512]{1,0:T(8,128)(2,1)S(1)}, bf16[224,512]{1,0:T(8,128)(2,1)S(1)}, u32[]{:S(2)}, u32[]{:S(2)}) collective-permute-start(bf16[224,512]{1,0:T(8,128)(2,1)S(1)} %bitcast_add_fusion), channel_id=1, source_target_pairs={{0,4},{1,5},{2,6},{3,7},{4,0},{5,1},{6,2},{7,3},{8,12},{9,13},{10,... | collective-permute-start | bytes 688136 | tf_op jit(solution)/shard_map/ppermute | solution.py:203
  8.2 11.9 %collective-permute-start.1 = (bf16[224,512]{1,0:T(8,128)(2,1)S(1)}, bf16[224,512]{1,0:T(8,128)(2,1)S(1)}, u32[]{:S(2)}, u32[]{:S(2)}) collective-permute-start(bf16[224,512]{1,0:T(8,128)(2,1)S(1)} %bitcast_add_fusion), channel_id=1, source_target_pairs={{0,2},{1,3},{2,0},{3,1},{4,6},{5,7},{6,4},{7,5},{8,10},{9,11},{10,... | collective-permute-start | bytes 688136 | tf_op jit(solution)/shard_map/ppermute | solution.py:203
  10.1 10.1 %collective-permute-start.11 = (bf16[224,256]{1,0:T(8,128)(2,1)S(1)}, bf16[224,256]{1,0:T(8,128)(2,1)S(1)}, u32[]{:S(2)}, u32[]{:S(2)}) collective-permute-start(bf16[224,256]{1,0:T(8,128)(2,1)S(1)} %get-tuple-element.7), channel_id=1, source_target_pairs={{0,1},{1,0},{2,3},{3,2},{4,5},{5,4},{6,7},{7,6},{8,9},{9,8},{10,11... | collective-permute-start | bytes 344072 | tf_op jit(solution)/shard_map/ppermute | solution.py:203
  21.4 31.3 %all-to-all-start = ((bf16[32,16,512]{2,1,0:T(8,128)(2,1)}), bf16[32,16,512]{2,1,0:T(8,128)(2,1)S(1)}, u32[]{:S(2)}, u32[]{:S(2)}) async-start(bf16[32,16,512]{2,1,0:T(8,128)(2,1)} %bitcast.11), calls=%async_computation | async-start | bytes 1048576 | tf_op jit(solution)/shard_map/all_to_all | solution.py:195
  31.3 4.4 %collective-permute-start.6 = (f32[32,384]{1,0:T(8,128)S(1)}, f32[32,384]{1,0:T(8,128)S(1)}, u32[]{:S(2)}, u32[]{:S(2)}) collective-permute-start(f32[32,384]{1,0:T(8,128)S(1)} %get-tuple-element.10), channel_id=1, source_target_pairs={{0,192},{8,200},{16,208},{24,216},{32,224},{40,232},{48,240},{56,2... | collective-permute-start | bytes 147464 | tf_op jit(solution)/shard_map/ppermute | solution.py:203
  33.9 4.8 %collective-permute-start.5 = (f32[32,384]{1,0:T(8,128)S(1)}, f32[32,384]{1,0:T(8,128)S(1)}, u32[]{:S(2)}, u32[]{:S(2)}) collective-permute-start(f32[32,384]{1,0:T(8,128)S(1)} %get-tuple-element.11), channel_id=1, source_target_pairs={{0,128},{8,136},{16,144},{24,152},{32,160},{40,168},{48,176},{56,1... | collective-permute-start | bytes 147464 | tf_op jit(solution)/shard_map/ppermute | solution.py:203
  34.4 4.3 %collective-permute-start.4 = (f32[32,384]{1,0:T(8,128)S(1)}, f32[32,384]{1,0:T(8,128)S(1)}, u32[]{:S(2)}, u32[]{:S(2)}) collective-permute-start(f32[32,384]{1,0:T(8,128)S(1)} %get-tuple-element.12), channel_id=1, source_target_pairs={{0,64},{8,72},{16,80},{24,88},{32,96},{40,104},{48,112},{56,120},{... | collective-permute-start | bytes 147464 | tf_op jit(solution)/shard_map/ppermute | solution.py:203
  38.7 10.3 %collective-permute-start.7 = (f32[32,384]{1,0:T(8,128)S(1)}, f32[32,384]{1,0:T(8,128)S(1)}, u32[]{:S(2)}, u32[]{:S(2)}) collective-permute-start(f32[32,384]{1,0:T(8,128)S(1)} %fusion.19), channel_id=1, source_target_pairs={{0,32},{8,40},{16,48},{24,56},{32,0},{40,8},{48,16},{56,24},{64,96... | collective-permute-start | bytes 147464 | tf_op jit(solution)/shard_map/ppermute | solution.py:203
  49.0 4.3 %copy-start.3 = (f32[32,384]{1,0:T(8,128)}, f32[32,384]{1,0:T(8,128)S(1)}, u32[]{:S(2)}) copy-start(f32[32,384]{1,0:T(8,128)S(1)} %add.50.refs_0_) | copy-start | bytes 147460
  49.0 4.9 %collective-permute-start.10 = (f32[32,384]{1,0:T(8,128)S(1)}, f32[32,384]{1,0:T(8,128)S(1)}, u32[]{:S(2)}, u32[]{:S(2)}) collective-permute-start(f32[32,384]{1,0:T(8,128)S(1)} %add.50.refs_0_), channel_id=1, source_target_pairs={{0,24},{8,16},{16,8},{24,0},{32,56},{40,48},{48,40},{56,32},{64,88... | collective-permute-start | bytes 147464 | tf_op jit(solution)/shard_map/ppermute | solution.py:203
  50.3 4.9 %collective-permute-start.9 = (f32[32,384]{1,0:T(8,128)S(1)}, f32[32,384]{1,0:T(8,128)S(1)}, u32[]{:S(2)}, u32[]{:S(2)}) collective-permute-start(f32[32,384]{1,0:T(8,128)S(1)} %add.50.refs_0_), channel_id=1, source_target_pairs={{0,16},{8,24},{16,0},{24,8},{32,48},{40,56},{48,32},{56,40},{64,80... | collective-permute-start | bytes 147464 | tf_op jit(solution)/shard_map/ppermute | solution.py:203
  50.3 4.9 %collective-permute-start.8 = (f32[32,384]{1,0:T(8,128)S(1)}, f32[32,384]{1,0:T(8,128)S(1)}, u32[]{:S(2)}, u32[]{:S(2)}) collective-permute-start(f32[32,384]{1,0:T(8,128)S(1)} %add.50.refs_0_), channel_id=1, source_target_pairs={{0,8},{8,0},{16,24},{24,16},{32,40},{40,32},{48,56},{56,48},{64,72... | collective-permute-start | bytes 147464 | tf_op jit(solution)/shard_map/ppermute | solution.py:203
  53.9 1.3 %copy-start.5 = (f32[32,384]{1,0:T(8,128)}, f32[32,384]{1,0:T(8,128)S(1)}, u32[]{:S(2)}) copy-start(f32[32,384]{1,0:T(8,128)S(1)} %collective-permute-done.10.refs_3_) | copy-start | bytes 147460
  55.2 0.6 copy-start.6
  55.8 0.6 copy-start.7
  58.0 3.9 %collective-permute-start.12 = (f32[32,384]{1,0:T(8,128)}, f32[32,384]{1,0:T(8,128)S(1)}, u32[]{:S(2)}, u32[]{:S(2)}) collective-permute-start(f32[32,384]{1,0:T(8,128)} %shard_map.50), channel_id=1, source_target_pairs={{0,64},{8,72},{16,80},{24,88},{32,96},{40,104},{48,112},{56,120},{... | collective-permute-start | bytes 147464 | tf_op jit(solution)/shard_map/ppermute | solution.py:203
  58.2 4.8 %collective-permute-start.13 = (f32[32,384]{1,0:T(8,128)}, f32[32,384]{1,0:T(8,128)S(1)}, u32[]{:S(2)}, u32[]{:S(2)}) collective-permute-start(f32[32,384]{1,0:T(8,128)} %shard_map.50), channel_id=1, source_target_pairs={{0,128},{8,136},{16,144},{24,152},{32,160},{40,168},{48,176},{56,1... | collective-permute-start | bytes 147464 | tf_op jit(solution)/shard_map/ppermute | solution.py:203
  60.8 4.4 %collective-permute-start.14 = (f32[32,384]{1,0:T(8,128)}, f32[32,384]{1,0:T(8,128)S(1)}, u32[]{:S(2)}, u32[]{:S(2)}) collective-permute-start(f32[32,384]{1,0:T(8,128)} %shard_map.50), channel_id=1, source_target_pairs={{0,192},{8,200},{16,208},{24,216},{32,224},{40,232},{48,240},{56,2... | collective-permute-start | bytes 147464 | tf_op jit(solution)/shard_map/ppermute | solution.py:203
  65.2 3.3 %copy-start.4 = (bf16[16,512]{1,0:T(8,128)(2,1)S(1)}, bf16[16,512]{1,0:T(8,128)(2,1)}, u32[]{:S(2)}) copy-start(bf16[16,512]{1,0:T(8,128)(2,1)} %reduce_sum.21.refs_4_) | copy-start | bytes 49156
  65.3 9.2 %collective-permute-start.17 = (f32[128,384]{1,0:T(8,128)S(1)}, f32[128,384]{1,0:T(8,128)S(1)}, u32[]{:S(2)}, u32[]{:S(2)}) collective-permute-start(f32[128,384]{1,0:T(8,128)S(1)} %bitcast.52), channel_id=1, source_target_pairs={{0,6},{1,7},{2,0},{3,1},{4,2},{5,3},{6,4},{7,5},{8,14},{9,15},{10,... | collective-permute-start | bytes 589832 | tf_op jit(solution)/shard_map/ppermute | solution.py:271
  67.5 6.9 %collective-permute-start.16 = (f32[128,384]{1,0:T(8,128)S(1)}, f32[128,384]{1,0:T(8,128)S(1)}, u32[]{:S(2)}, u32[]{:S(2)}) collective-permute-start(f32[128,384]{1,0:T(8,128)S(1)} %bitcast.53), channel_id=1, source_target_pairs={{0,4},{1,5},{2,6},{3,7},{4,0},{5,1},{6,2},{7,3},{8,12},{9,13},{10,... | collective-permute-start | bytes 589832 | tf_op jit(solution)/shard_map/ppermute | solution.py:271
  67.9 7.8 %collective-permute-start.15 = (f32[128,384]{1,0:T(8,128)S(1)}, f32[128,384]{1,0:T(8,128)S(1)}, u32[]{:S(2)}, u32[]{:S(2)}) collective-permute-start(f32[128,384]{1,0:T(8,128)S(1)} %bitcast.54), channel_id=1, source_target_pairs={{0,2},{1,3},{2,4},{3,5},{4,6},{5,7},{6,0},{7,1},{8,10},{9,11},{10,... | collective-permute-start | bytes 589832 | tf_op jit(solution)/shard_map/ppermute | solution.py:271
  69.4 25.6 %all-to-all-start.1 = ((bf16[32,16,512]{2,1,0:T(8,128)(2,1)}), bf16[32,16,512]{2,1,0:T(8,128)(2,1)S(1)}, u32[]{:S(2)}, u32[]{:S(2)}) async-start(bf16[32,16,512]{2,1,0:T(8,128)(2,1)} %broadcast_in_dim.4), calls=%async_computation.1 | async-start | bytes 1048576 | tf_op jit(solution)/shard_map/all_to_all | solution.py:195
  95.5 11.5 %collective-permute-start.21 = (f32[1,512]{1,0:T(1,128)S(1)}, f32[1,512]{1,0:T(1,128)S(1)}, u32[]{:S(2)}, u32[]{:S(2)}) collective-permute-start(f32[1,512]{1,0:T(1,128)S(1)} %bitcast.59), channel_id=1, source_target_pairs={{0,6},{1,7},{2,4},{3,5},{4,2},{5,3},{6,0},{7,1},{8,14},{9,15},{10,... | collective-permute-start | bytes 6152 | tf_op jit(solution)/shard_map/ppermute | solution.py:203
  96.4 10.6 %collective-permute-start.20 = (f32[1,512]{1,0:T(1,128)S(1)}, f32[1,512]{1,0:T(1,128)S(1)}, u32[]{:S(2)}, u32[]{:S(2)}) collective-permute-start(f32[1,512]{1,0:T(1,128)S(1)} %bitcast.60), channel_id=1, source_target_pairs={{0,4},{1,5},{2,6},{3,7},{4,0},{5,1},{6,2},{7,3},{8,12},{9,13},{10,... | collective-permute-start | bytes 6152 | tf_op jit(solution)/shard_map/ppermute | solution.py:203
  97.9 9.2 %collective-permute-start.19 = (f32[1,512]{1,0:T(1,128)S(1)}, f32[1,512]{1,0:T(1,128)S(1)}, u32[]{:S(2)}, u32[]{:S(2)}) collective-permute-start(f32[1,512]{1,0:T(1,128)S(1)} %bitcast.61), channel_id=1, source_target_pairs={{0,2},{1,3},{2,0},{3,1},{4,6},{5,7},{6,4},{7,5},{8,10},{9,11},{10,... | collective-permute-start | bytes 6152 | tf_op jit(solution)/shard_map/ppermute | solution.py:203
  99.2 11.2 %collective-permute-start.18 = (bf16[224,256]{1,0:T(8,128)(2,1)S(1)}, bf16[224,256]{1,0:T(8,128)(2,1)S(1)}, u32[]{:S(2)}, u32[]{:S(2)}) collective-permute-start(bf16[224,256]{1,0:T(8,128)(2,1)S(1)} %fusion.9), channel_id=1, source_target_pairs={{0,1},{1,0},{2,3},{3,2},{4,5},{5,4},{6,7},{7,6},{8,9},{9,8},{10,11... | collective-permute-start | bytes 344072 | tf_op jit(solution)/shard_map/ppermute | solution.py:203
  107.4 3.1 %copy-start.1 = (f32[2,224,256]{2,1,0:T(8,128)S(1)}, f32[2,224,256]{2,1,0:T(8,128)}, u32[]{:S(2)}) copy-start(f32[2,224,256]{2,1,0:T(8,128)} %param.3) | copy-start | bytes 1376260
  107.4 3.1 %copy-start.2 = (bf16[2,224,256]{2,1,0:T(8,128)(2,1)S(1)}, bf16[2,224,256]{2,1,0:T(8,128)(2,1)}, u32[]{:S(2)}) copy-start(bf16[2,224,256]{2,1,0:T(8,128)(2,1)} %param.4) | copy-start | bytes 688132
  107.4 4.0 %collective-permute-start.22 = (bf16[224,256]{1,0:T(8,128)(2,1)S(1)}, bf16[224,256]{1,0:T(8,128)(2,1)S(1)}, u32[]{:S(2)}, u32[]{:S(2)}) collective-permute-start(bf16[224,256]{1,0:T(8,128)(2,1)S(1)} %fusion.7), channel_id=1, source_target_pairs={{0,1},{1,0},{2,3},{3,2},{4,5},{5,4},{6,7},{7,6},{8,9},{9,8},{10,11... | collective-permute-start | bytes 344072 | tf_op jit(solution)/shard_map/ppermute | solution.py:203

commit v3 on v2

--- a/solution.py
+++ b/solution.py
@@ -1,3 +1,4 @@
+import functools
 import math
 
 import jax
@@ -44,7 +45,6 @@
         a, b, c = row_of(left, j), row_of(right, j), row_of(right, j + 1)
         root = lax.rsqrt(a * c - b * b)
         inv = root * root
-        ia, ib, ic = c * inv, -(b * inv), a * inv
         root_a = lax.rsqrt(a)
         ratio = b * (root_a * root_a)
         root_c = lax.rsqrt(c - b * ratio)
@@ -55,15 +55,15 @@
                 continue
             top, low = row_of(cols[k], j), row_of(cols[k], j + 1)
             rest = jnp.where(both, 0.0, cols[k])
-            cols[k] = rest - (left_m * (ia * top + ib * low) + right_m * (ib * top + ic * low))
+            cols[k] = rest - inv * (left_m * (c * top - b * low) + right_m * (a * low - b * top))
             if k < j:
                 factor[k] = jnp.where(
                     first, top * root_a, jnp.where(second, (low - ratio * top) * root_c, factor[k])
                 )
         factor[j] = jnp.where(first, root_a, jnp.where(second, -(ratio * root_c), factor[j]))
         factor[j + 1] = jnp.where(second, root_c, factor[j + 1])
-        cols[j] = -(left_m * ia + right_m * ib)
-        cols[j + 1] = -(left_m * ib + right_m * ic)
+        cols[j] = inv * (right_m * b - left_m * c)
+        cols[j + 1] = inv * (left_m * b - right_m * a)
     return cols, factor
 
 
@@ -71,7 +71,7 @@
     return added([cols[j] * row_of(value, j) for j in range(PANEL)])
 
 
-def block_inverse_factor(groups):
+def block_inverse_factor(groups, tasks):
     row = lax.broadcasted_iota(jnp.int32, (PANEL, BLOCK), 0)
     lane = lax.broadcasted_iota(jnp.int32, (PANEL, BLOCK), 1)
     block = [lanes_of(groups[0], j) for j in range(PANEL)]
@@ -93,6 +93,8 @@
                 change = added([lanes_of(old, base + j) * rows[j] for j in range(PANEL)])
                 groups[i] = jnp.where(inside, 0.0, old) - change
         groups[k] = jnp.where(lane <= row + base, combine(factor, panel), 0.0)
+        if k < len(tasks):
+            tasks[k]()
     return groups
 
 
@@ -102,13 +104,53 @@
     return high, low
 
 
-def product(left, right, left_axis):
-    return lax.dot_general(
-        jnp.concatenate([left[0], left[0], left[1]], axis=left_axis),
-        jnp.concatenate([right[0], right[1], right[0]], axis=0),
-        (((left_axis,), (0,)), ((), ())),
-        preferred_element_type=jnp.float32,
+def wide_terms(value):
+    high, low = split_halves(value)
+    return jnp.concatenate([high, high, low], axis=1)
+
+
+def product(terms, right):
+    high, low = split_halves(right)
+    return jnp.dot(
+        terms, jnp.concatenate([high, low, high], axis=0), preferred_element_type=jnp.float32
     )
+
+
+def later_products(work_ref, k, inverse, columns):
+    before, through = slice(0, k * BLOCK), slice(0, (k + 1) * BLOCK)
+    lefts = {}
+
+    def solve(j):
+        upper = product(inverse, work_ref[k, :, columns(j)])
+        work_ref[k, :, columns(j)] = upper
+        lefts[j] = wide_terms(upper.T)
+
+    def solve_before():
+        work_ref[k, :, before] = product(inverse, work_ref[k, :, before])
+
+    def update(i, j):
+        work_ref[i, :, columns(j)] -= product(lefts[i], work_ref[k, :, columns(j)])
+
+    def update_before(i):
+        change = product(lefts[i], work_ref[k, :, through])
+        if k > 0:
+            work_ref[i, :, before] -= change[:, before]
+        work_ref[i, :, columns(k)] = -change[:, columns(k)]
+
+    rest = range(k + 1, BLOCKS)
+    tasks = [functools.partial(solve, j) for j in rest[1:]]
+    if k > 0:
+        tasks.append(solve_before)
+    for i in rest:
+        tasks += [functools.partial(update, i, j) for j in range(i, BLOCKS) if j > k + 1]
+        tasks.append(functools.partial(update_before, i))
+    if k + 1 < BLOCKS:
+        solve(k + 1)
+        update(k + 1, k + 1)
+        return tasks
+    for task in tasks:
+        task()
+    return []
 
 
 def factor_kernel(where_ref, own_ref, one_ref, two_ref, three_ref, out_ref, slab_ref, work_ref):
@@ -131,28 +173,16 @@
             work_ref[i, :, j * BLOCK : (j + 1) * BLOCK] = block(i, j) * scale
     back_scale = lax.rsqrt(most)
 
+    def columns(j):
+        return slice(j * BLOCK, (j + 1) * BLOCK)
+
+    tasks = []
     for k in range(BLOCKS):
         at, to = k * BLOCK, (k + 1) * BLOCK
         groups = [work_ref[k, i * PANEL : (i + 1) * PANEL, at:to] for i in range(PANELS)]
-        inverse = jnp.concatenate(block_inverse_factor(groups), axis=0)
+        inverse = jnp.concatenate(block_inverse_factor(groups, tasks), axis=0)
         work_ref[k, :, at:to] = inverse
-        pair = split_halves(inverse)
-        if k > 0:
-            work_ref[k, :, :at] = product(pair, split_halves(work_ref[k, :, :at]), 1)
-        if k + 1 < BLOCKS:
-            upper = product(pair, split_halves(work_ref[k, :, to:]), 1)
-            work_ref[k, :, to:] = upper
-            upper = split_halves(upper)
-            whole = split_halves(work_ref[k])
-            for i in range(k + 1, BLOCKS):
-                left = tuple(part[:, (i - k - 1) * BLOCK : (i - k) * BLOCK] for part in upper)
-                work_ref[i, :, i * BLOCK :] -= product(
-                    left, tuple(part[:, i * BLOCK :] for part in whole), 0
-                )
-                change = product(left, tuple(part[:, :to] for part in whole), 0)
-                if k > 0:
-                    work_ref[i, :, :at] -= change[:, :at]
-                work_ref[i, :, at:to] = -change[:, at:]
+        tasks = later_products(work_ref, k, wide_terms(inverse), columns)
     for i in range(BLOCKS):
         to = (i + 1) * BLOCK
         rows = slice(i * BLOCK, to)
@@ -177,18 +207,38 @@
     )(where, *slabs)
 
 
-def sum_kernel(*refs):
-    refs[-1][...] = added([ref[...] for ref in refs[:-2]])
-
-
-def summed(terms, after):
+def place_kernel(where_ref, *refs):
+    parts, out_ref = refs[:X_SIZE], refs[-1]
+    for step, ref in enumerate(parts):
+        out_ref[lax.bitwise_xor(where_ref[0], step)] = ref[...]
+
+
+def placed_parts(where, parts, after):
     vmem = pl.BlockSpec(memory_space=pltpu.VMEM)
     return pl.pallas_call(
-        sum_kernel,
-        out_shape=jax.ShapeDtypeStruct(terms[0].shape, terms[0].dtype),
-        in_specs=[vmem] * len(terms) + [pl.BlockSpec(memory_space=pl.ANY)],
+        place_kernel,
+        out_shape=jax.ShapeDtypeStruct((X_SIZE,) + parts[0].shape, parts[0].dtype),
+        in_specs=[pl.BlockSpec(memory_space=pltpu.SMEM)] + [vmem] * (X_SIZE + 1),
         out_specs=vmem,
-    )(*terms, after)
+    )(where, *parts, after)
+
+
+def wide_kernel(own_ref, other_ref, right_ref, _, out_ref):
+    for i, ref in enumerate((own_ref, other_ref)):
+        out_ref[i] = lax.dot_general(
+            ref[...], right_ref[...], (((0,), (0,)), ((), ())), preferred_element_type=jnp.float32
+        ).astype(out_ref.dtype)
+
+
+def wide_product(own, other, right, after):
+    vmem = pl.BlockSpec(memory_space=pltpu.VMEM)
+    return pl.pallas_call(
+        wide_kernel,
+        out_shape=jax.ShapeDtypeStruct((2, own.shape[1], right.shape[1]), jnp.bfloat16),
+        in_specs=[vmem] * 4,
+        out_specs=vmem,
+        compiler_params=pltpu.CompilerParams(vmem_limit_bytes=24 * 1024 * 1024),
+    )(own, other, right, after)
 
 
 def spread(chunks, axis):
@@ -208,29 +258,23 @@
 
 
 def make_local(row_count, col_count):
-    def bit(index, mask):
-        return lax.convert_element_type(lax.bitwise_and(index, np.uint32(mask)) != 0, jnp.uint32)
-
     def item(stack, index):
         return lax.dynamic_index_in_dim(stack, index, 0, keepdims=False)
 
     def quad(value, axis, count, low):
         return [value] + [swap(value, axis, count, step * low) for step in (1, 2, 3)]
 
-    def row_sum(value, row, after):
+    def x_sum(value, plane):
         pieces = value.reshape(X_SIZE, value.shape[0] // X_SIZE, value.shape[1])
-        plane = lax.div(row, np.uint32(Z_SIZE))
         terms = [item(pieces, plane)]
         for step in range(1, X_SIZE):
             send = item(pieces, lax.bitwise_xor(plane, np.uint32(step)))
             terms.append(swap(send, "row", row_count, step * Z_SIZE))
-        value = added(terms)
+        return added(terms)
+
+    def z_sum(value):
         value = value + swap(value, "row", row_count, 4)
-        value = summed(quad(value, "row", row_count, 1), after)
-        parts = quad(value, "row", row_count, Z_SIZE)
-        low = bit(plane, 1) == 0
-        both = pick(bit(plane, 2) == 0, pick(low, parts[0], parts[1]), pick(low, parts[2], parts[3]))
-        return both.reshape(X_SIZE * value.shape[0], value.shape[1])
+        return added(quad(value, "row", row_count, 1))
 
     def local(momentum, gradient, basis_in):
         experts, rows, cols = momentum.shape
@@ -240,7 +284,7 @@
         expert = lax.rem(col, np.uint32(experts))
         place = lax.div(col, np.uint32(experts))
         first = expert == 0
-        buffer = momentum + gradient.astype(jnp.float32)
+        buffer = lax.optimization_barrier(momentum + gradient.astype(jnp.float32))
         half = buffer.astype(jnp.bfloat16)
         partial = jnp.einsum(
             "erc,eck->erk", half, basis_in, preferred_element_type=jnp.float32
@@ -255,16 +299,19 @@
             KEPT * BLOCK,
             axis=1,
         )
-        whole = jnp.stack(
-            [item(half, expert), swap(item(half, 1 - expert), "col", col_count, 1)]
-        )
-        wide = jnp.einsum("hrc,rk->hck", whole, projected, preferred_element_type=jnp.float32)
-        wide = wide.astype(jnp.bfloat16).reshape(row_count, 2 * cols // row_count, rank)
+        gram = jnp.einsum("rk,rl->kl", turned[:, :BLOCK], turned, preferred_element_type=jnp.float32)
+        plane = lax.div(row, np.uint32(Z_SIZE))
+        gram = x_sum(gram, plane)
+        left = swap(item(half, 1 - expert), "col", col_count, 1)
+        wide = wide_product(item(half, expert), left, projected, gram[:PANEL, :BLOCK])
+        wide = wide.reshape(row_count, 2 * cols // row_count, rank)
         wide = jnp.sum(spread(wide, "row").astype(jnp.float32), axis=0).astype(jnp.bfloat16)
-
-        slab = row_sum(
-            jnp.einsum("rk,rl->kl", turned[:, :BLOCK], turned, preferred_element_type=jnp.float32), row, wide
-        )
+        gram = z_sum(gram)
+        slab = placed_parts(
+            jnp.reshape(plane, (1,)).astype(jnp.int32),
+            quad(gram, "row", row_count, Z_SIZE),
+            wide[: 2 * PANEL, :BLOCK],
+        ).reshape(BLOCK, KEPT * BLOCK)
         slabs = [slab]
         for step in range(1, BLOCKS):
             turn = [(i, (i + step * experts) % col_count) for i in range(col_count)]

time: 113 us -> 116 us (1.027)
  waiting for transfers between devices: 23.6 us -> 30.1 us
  other arithmetic: 4.66 us -> 3.22 us
    ppermute x20, waiting for transfers between devices: 22.4 us -> 28.2 us  [swap(): return lax.ppermute(value, axis, [(i, i ^ mask) for i in range(count)])]
    pallas_call x1 -> x2, Pallas kernels: 1.5 us -> 2.7 us  [the longest x1 1.56 us: placed_parts(): pl.pallas_call(place_kernel, out_shape=jax.ShapeDtypeStruct((X_SIZE,) + p...]
    add x1 -> x2, other arithmetic: 0.01 us -> 1.19 us  [the longest x1 1.18 us: local(): buffer = lax.optimization_barrier(momentum + gradient.astype(jnp.float32))]
  transfers between devices with their start and end apart: 25 -> 25, of which waited for: 12 -> 11; matrix products, arithmetic and copies ran while one was open for 4% -> 3% of each run, Pallas kernels for 17% -> 16%
where the time goes in v3:
time: 116 us
  starting transfers between devices  56.5 us (49%)
  waiting for transfers between devices  30.1 us (26%)
  Pallas kernels  21.1 us (18%)
  other arithmetic  3.22 us (3%)
  local copies, waits for them, and re-layouts  2.22 us (2%)
  matrix products  1.97 us (2%)
    ppermute x20, starting transfers between devices, swap(): return lax.ppermute(value, axis, [(i, i ^ mask) for i in range(count)])  39 us
    ppermute x20, waiting for transfers between devices, swap(): return lax.ppermute(value, axis, [(i, i ^ mask) for i in range(count)])  28.2 us
    pallas_call x1, Pallas kernels, inverse_factor(): pl.pallas_call(factor_kernel, out_shape=jax.ShapeDtypeStruct((RANK, RANK)...  18.4 us
    all_to_all x2, starting transfers between devices, spread(): return lax.all_to_all(chunks, axis, split_axis=0, concat_axis=0, tiled=True)  13.9 us
    ppermute x3, starting transfers between devices, local(): slabs.append(lax.ppermute(slab, 'col', turn))  3.63 us
  transfers between devices with their start and end apart: 25, of which 11 were waited for; matrix products, arithmetic and copies ran while one was open for 3% of the time, Pallas kernels for 16%

profile of v3, /device:TPU:1, one launch (start us, length us, event | category | flops | bytes accessed | tf_op | source)
XLA Modules:
  0.0 116.1 jit_solution(15599538916713775091)
XLA Ops:
  0.7 1.2 %convert_add_fusion = f32[2,224,256]{2,1,0:T(8,128)S(1)} fusion(f32[2,224,256]{2,1,0:T(8,128)} %param.3, bf16[2,224,256]{2,1,0:T(8,128)(2,1)} %param.4), kind=kLoop, calls=%fused_computation.10 | loop fusion | flops 229376 | bytes 1146880 | tf_op jit(solution)/shard_map/add | solution.py:287
  1.9 0.3 convolution_convert_fusion
  2.2 3.3 %collective-permute-start = (bf16[224,512]{1,0:T(8,128)(2,1)S(1)}, bf16[224,512]{1,0:T(8,128)(2,1)S(1)}, u32[]{:S(2)}, u32[]{:S(2)}) collective-permute-start(bf16[224,512]{1,0:T(8,128)(2,1)S(1)} %dynamic-slice_bitcast_fusion), channel_id=1, source_target_pairs={{0,1},{1,0},{2,3},{3,2},{4,5},{5,4},{6,7},{7,6},{8,9},{9,8},{10,11... | collective-permute-start | bytes 688136 | tf_op jit(solution)/shard_map/ppermute | solution.py:253
  5.6 1.1 collective-permute-done
  6.7 1.1 collective-permute-start.3
  7.8 0.3 collective-permute-start.2
  8.2 1.9 %collective-permute-start.1 = (bf16[224,512]{1,0:T(8,128)(2,1)S(1)}, bf16[224,512]{1,0:T(8,128)(2,1)S(1)}, u32[]{:S(2)}, u32[]{:S(2)}) collective-permute-start(bf16[224,512]{1,0:T(8,128)(2,1)S(1)} %bitcast_add_fusion), channel_id=1, source_target_pairs={{0,2},{1,3},{2,0},{3,1},{4,6},{5,7},{6,4},{7,5},{8,10},{9,11},{10,... | collective-permute-start | bytes 688136 | tf_op jit(solution)/shard_map/ppermute | solution.py:253
  10.1 9.7 %collective-permute-done.3 = bf16[224,512]{1,0:T(8,128)(2,1)S(1)} collective-permute-done((bf16[224,512]{1,0:T(8,128)(2,1)S(1)}, bf16[224,512]{1,0:T(8,128)(2,1)S(1)}, u32[]{:S(2)}, u32[]{:S(2)}) %collective-permute-start.3) | collective-permute-done | bytes 229408 | tf_op jit(solution)/shard_map/ppermute | solution.py:253
  19.8 0.3 collective-permute-done.1
  20.6 1.1 collective-permute-start.6
  21.7 0.5 collective-permute-start.5
  22.2 1.7 %collective-permute-start.4 = (f32[32,384]{1,0:T(8,128)S(1)}, f32[32,384]{1,0:T(8,128)S(1)}, u32[]{:S(2)}, u32[]{:S(2)}) collective-permute-start(f32[32,384]{1,0:T(8,128)S(1)} %get-tuple-element.10), channel_id=1, source_target_pairs={{0,64},{8,72},{16,80},{24,88},{32,96},{40,104},{48,112},{56,120},{... | collective-permute-start | bytes 147464 | tf_op jit(solution)/shard_map/ppermute | solution.py:253
  23.9 2.4 %collective-permute-start.14 = (bf16[224,256]{1,0:T(8,128)(2,1)S(1)}, bf16[224,256]{1,0:T(8,128)(2,1)S(1)}, u32[]{:S(2)}, u32[]{:S(2)}) collective-permute-start(bf16[224,256]{1,0:T(8,128)(2,1)S(1)} %get-tuple-element.6), channel_id=1, source_target_pairs={{0,1},{1,0},{2,3},{3,2},{4,5},{5,4},{6,7},{7,6},{8,9},{9,8},{10,11... | collective-permute-start | bytes 344072 | tf_op jit(solution)/shard_map/ppermute | solution.py:253
  26.4 0.9 collective-permute-done.14.other_ref
  27.3 1.1 shard_map.50
  28.4 9.5 %all-to-all-start = ((bf16[32,16,512]{2,1,0:T(8,128)(2,1)}), bf16[32,16,512]{2,1,0:T(8,128)(2,1)S(1)}, u32[]{:S(2)}, u32[]{:S(2)}) async-start(bf16[32,16,512]{2,1,0:T(8,128)(2,1)} %bitcast.11), calls=%async_computation | async-start | bytes 1048576 | tf_op jit(solution)/shard_map/all_to_all | solution.py:245
  37.9 5.2 %collective-permute-start.7 = (f32[32,384]{1,0:T(8,128)S(1)}, f32[32,384]{1,0:T(8,128)S(1)}, u32[]{:S(2)}, u32[]{:S(2)}) collective-permute-start(f32[32,384]{1,0:T(8,128)S(1)} %fusion.12), channel_id=1, source_target_pairs={{0,32},{8,40},{16,48},{24,56},{32,0},{40,8},{48,16},{56,24},{64,96... | collective-permute-start | bytes 147464 | tf_op jit(solution)/shard_map/ppermute | solution.py:253
  43.1 10.8 %collective-permute-done.7 = f32[32,384]{1,0:T(8,128)S(1)} collective-permute-done((f32[32,384]{1,0:T(8,128)S(1)}, f32[32,384]{1,0:T(8,128)S(1)}, u32[]{:S(2)}, u32[]{:S(2)}) %collective-permute-start.7) | collective-permute-done | bytes 49184 | tf_op jit(solution)/shard_map/ppermute | solution.py:253
  54.0 2.2 %collective-permute-start.9 = (f32[32,384]{1,0:T(8,128)S(1)}, f32[32,384]{1,0:T(8,128)S(1)}, u32[]{:S(2)}, u32[]{:S(2)}) collective-permute-start(f32[32,384]{1,0:T(8,128)S(1)} %add.59), channel_id=1, source_target_pairs={{0,16},{8,24},{16,0},{24,8},{32,48},{40,56},{48,32},{56,40},{64,80... | collective-permute-start | bytes 147464 | tf_op jit(solution)/shard_map/ppermute | solution.py:253
  56.2 1.3 %collective-permute-start.8 = (f32[32,384]{1,0:T(8,128)S(1)}, f32[32,384]{1,0:T(8,128)S(1)}, u32[]{:S(2)}, u32[]{:S(2)}) collective-permute-start(f32[32,384]{1,0:T(8,128)S(1)} %add.59), channel_id=1, source_target_pairs={{0,8},{8,0},{16,24},{24,16},{32,40},{40,32},{48,56},{56,48},{64,72... | collective-permute-start | bytes 147464 | tf_op jit(solution)/shard_map/ppermute | solution.py:253
  57.5 1.2 %collective-permute-done.10 = f32[32,384]{1,0:T(8,128)S(1)} collective-permute-done((f32[32,384]{1,0:T(8,128)S(1)}, f32[32,384]{1,0:T(8,128)S(1)}, u32[]{:S(2)}, u32[]{:S(2)}) %collective-permute-start.10) | collective-permute-done | bytes 49184 | tf_op jit(solution)/shard_map/ppermute | solution.py:253
  58.7 1.0 collective-permute-done.9
  59.8 2.6 %collective-permute-start.13 = (f32[32,384]{1,0:T(8,128)S(1)}, f32[32,384]{1,0:T(8,128)S(1)}, u32[]{:S(2)}, u32[]{:S(2)}) collective-permute-start(f32[32,384]{1,0:T(8,128)S(1)} %add_add_fusion.refs_0_), channel_id=1, source_target_pairs={{0,192},{8,200},{16,208},{24,216},{32,224},{40,232},{48,240},{56,2... | collective-permute-start | bytes 147464 | tf_op jit(solution)/shard_map/ppermute | solution.py:253
  62.4 0.5 collective-permute-start.12
  62.9 0.3 collective-permute-start.11
  63.2 0.6 slice.35.refs_4_
  63.8 0.4 collective-permute-done.13.refs_3_
  64.2 2.6 %collective-permute-done.12.refs_2_ = f32[32,384]{1,0:T(8,128)S(1)} collective-permute-done((f32[32,384]{1,0:T(8,128)S(1)}, f32[32,384]{1,0:T(8,128)S(1)}, u32[]{:S(2)}, u32[]{:S(2)}) %collective-permute-start.12) | collective-permute-done | bytes 49184 | tf_op jit(solution)/shard_map/ppermute | solution.py:253
  66.8 0.6 copy-done.4
  67.4 1.6 %shard_map.51 = f32[4,32,384]{2,1,0:T(8,128)} custom-call(s32[1]{0:T(128)} %bitcast.3.where_ref, f32[32,384]{1,0:T(8,128)} %copy-done.2, f32[32,384]{1,0:T(8,128)} %copy-done.5, f32[32,384]{1,0:T(8,128)} %copy-done.4, f32[32,384]{1,0:T(8,128)} %copy-done.3, bf16[16,128]{1,0:T(8,128)(2,1)} %slice.35.refs_4_), custom_call_target="tpu_custom_call" | custom-call | tf_op jit(solution)/shard_map/pallas_call | solution.py:218
  69.0 2.6 %collective-permute-start.17 = (f32[128,384]{1,0:T(8,128)}, f32[128,384]{1,0:T(8,128)S(1)}, u32[]{:S(2)}, u32[]{:S(2)}) collective-permute-start(f32[128,384]{1,0:T(8,128)} %bitcast.43), channel_id=1, source_target_pairs={{0,6},{1,7},{2,0},{3,1},{4,2},{5,3},{6,4},{7,5},{8,14},{9,15},{10,... | collective-permute-start | bytes 589832 | tf_op jit(solution)/shard_map/ppermute | solution.py:318
  71.6 0.3 collective-permute-start.16
  71.9 0.7 collective-permute-start.15
  72.6 0.9 broadcast_in_dim.4
  73.5 4.4 %all-to-all-start.1 = ((bf16[32,16,512]{2,1,0:T(8,128)(2,1)}), bf16[32,16,512]{2,1,0:T(8,128)(2,1)S(1)}, u32[]{:S(2)}, u32[]{:S(2)}) async-start(bf16[32,16,512]{2,1,0:T(8,128)(2,1)} %broadcast_in_dim.4), calls=%async_computation.1 | async-start | bytes 1048576 | tf_op jit(solution)/shard_map/all_to_all | solution.py:245
  78.0 2.0 %collective-permute-done.15.one_ref = f32[128,384]{1,0:T(8,128)S(1)} collective-permute-done((f32[128,384]{1,0:T(8,128)}, f32[128,384]{1,0:T(8,128)S(1)}, u32[]{:S(2)}, u32[]{:S(2)}) %collective-permute-start.15) | collective-permute-done | bytes 196640 | tf_op jit(solution)/shard_map/ppermute | solution.py:318
  79.9 18.4 %shard_map.52 = bf16[512,512]{1,0:T(8,128)(2,1)S(1)} custom-call(s32[1]{0:T(128)} %bitcast.2.where_ref, f32[128,384]{1,0:T(8,128)S(1)} %bitcast.46, f32[128,384]{1,0:T(8,128)S(1)} %collective-permute-done.15.one_ref, f32[128,384]{1,0:T(8,128)S(1)} %collective-permute-done.16.two_ref, f32[128,384]{1,0:T(8,128)S(1)} %collective-permute-done.17.three_ref), custom_call_target="tpu_custom_call" | custom-call | flops 20000000000 | tf_op jit(solution)/shard_map/pallas_call | solution.py:196
  98.4 0.3 convolution_convert_fusion.1
  98.7 0.5 multiply_reduce_fusion
  99.2 0.4 collective-permute-start.21
  99.6 1.1 collective-permute-start.20
  100.7 1.8 %collective-permute-start.19 = (f32[1,512]{1,0:T(1,128)S(1)}, f32[1,512]{1,0:T(1,128)S(1)}, u32[]{:S(2)}, u32[]{:S(2)}) collective-permute-start(f32[1,512]{1,0:T(1,128)S(1)} %bitcast.52), channel_id=1, source_target_pairs={{0,2},{1,3},{2,0},{3,1},{4,6},{5,7},{6,4},{7,5},{8,10},{9,11},{10,... | collective-permute-start | bytes 6152 | tf_op jit(solution)/shard_map/ppermute | solution.py:253
  102.5 0.3 fusion.2
  102.9 9.2 %collective-permute-start.18 = (bf16[224,256]{1,0:T(8,128)(2,1)S(1)}, bf16[224,256]{1,0:T(8,128)(2,1)S(1)}, u32[]{:S(2)}, u32[]{:S(2)}) collective-permute-start(bf16[224,256]{1,0:T(8,128)(2,1)S(1)} %fusion.8), channel_id=1, source_target_pairs={{0,1},{1,0},{2,3},{3,2},{4,5},{5,4},{6,7},{7,6},{8,9},{9,8},{10,11... | collective-permute-start | bytes 344072 | tf_op jit(solution)/shard_map/ppermute | solution.py:253
  112.1 0.3 fusion
  112.5 1.9 %collective-permute-start.22 = (bf16[224,256]{1,0:T(8,128)(2,1)S(1)}, bf16[224,256]{1,0:T(8,128)(2,1)S(1)}, u32[]{:S(2)}, u32[]{:S(2)}) collective-permute-start(bf16[224,256]{1,0:T(8,128)(2,1)S(1)} %fusion.6), channel_id=1, source_target_pairs={{0,1},{1,0},{2,3},{3,2},{4,5},{5,4},{6,7},{7,6},{8,9},{9,8},{10,11... | collective-permute-start | bytes 344072 | tf_op jit(solution)/shard_map/ppermute | solution.py:253
  114.4 0.8 maximum_subtract_fusion
  115.4 0.7 pad_maximum_fusion
  (46 shorter events, 1.1 us)
Async XLA Ops:
  0.6 1.3 %copy-start = (bf16[2,256,512]{2,1,0:T(8,128)(2,1)S(1)}, bf16[2,256,512]{2,1,0:T(8,128)(2,1)}, u32[]{:S(2)}) copy-start(bf16[2,256,512]{2,1,0:T(8,128)(2,1)} %param.5) | copy-start | bytes 1572868
  2.2 4.4 %collective-permute-start = (bf16[224,512]{1,0:T(8,128)(2,1)S(1)}, bf16[224,512]{1,0:T(8,128)(2,1)S(1)}, u32[]{:S(2)}, u32[]{:S(2)}) collective-permute-start(bf16[224,512]{1,0:T(8,128)(2,1)S(1)} %dynamic-slice_bitcast_fusion), channel_id=1, source_target_pairs={{0,1},{1,0},{2,3},{3,2},{4,5},{5,4},{6,7},{7,6},{8,9},{9,8},{10,11... | collective-permute-start | bytes 688136 | tf_op jit(solution)/shard_map/ppermute | solution.py:253
  6.7 13.0 %collective-permute-start.3 = (bf16[224,512]{1,0:T(8,128)(2,1)S(1)}, bf16[224,512]{1,0:T(8,128)(2,1)S(1)}, u32[]{:S(2)}, u32[]{:S(2)}) collective-permute-start(bf16[224,512]{1,0:T(8,128)(2,1)S(1)} %bitcast_add_fusion), channel_id=1, source_target_pairs={{0,6},{1,7},{2,4},{3,5},{4,2},{5,3},{6,0},{7,1},{8,14},{9,15},{10,... | collective-permute-start | bytes 688136 | tf_op jit(solution)/shard_map/ppermute | solution.py:253
  7.8 11.9 %collective-permute-start.2 = (bf16[224,512]{1,0:T(8,128)(2,1)S(1)}, bf16[224,512]{1,0:T(8,128)(2,1)S(1)}, u32[]{:S(2)}, u32[]{:S(2)}) collective-permute-start(bf16[224,512]{1,0:T(8,128)(2,1)S(1)} %bitcast_add_fusion), channel_id=1, source_target_pairs={{0,4},{1,5},{2,6},{3,7},{4,0},{5,1},{6,2},{7,3},{8,12},{9,13},{10,... | collective-permute-start | bytes 688136 | tf_op jit(solution)/shard_map/ppermute | solution.py:253
  8.2 11.9 %collective-permute-start.1 = (bf16[224,512]{1,0:T(8,128)(2,1)S(1)}, bf16[224,512]{1,0:T(8,128)(2,1)S(1)}, u32[]{:S(2)}, u32[]{:S(2)}) collective-permute-start(bf16[224,512]{1,0:T(8,128)(2,1)S(1)} %bitcast_add_fusion), channel_id=1, source_target_pairs={{0,2},{1,3},{2,0},{3,1},{4,6},{5,7},{6,4},{7,5},{8,10},{9,11},{10,... | collective-permute-start | bytes 688136 | tf_op jit(solution)/shard_map/ppermute | solution.py:253
  20.6 5.8 %collective-permute-start.6 = (f32[32,384]{1,0:T(8,128)S(1)}, f32[32,384]{1,0:T(8,128)S(1)}, u32[]{:S(2)}, u32[]{:S(2)}) collective-permute-start(f32[32,384]{1,0:T(8,128)S(1)} %get-tuple-element.8), channel_id=1, source_target_pairs={{0,192},{8,200},{16,208},{24,216},{32,224},{40,232},{48,240},{56,2... | collective-permute-start | bytes 147464 | tf_op jit(solution)/shard_map/ppermute | solution.py:253
  21.7 4.7 %collective-permute-start.5 = (f32[32,384]{1,0:T(8,128)S(1)}, f32[32,384]{1,0:T(8,128)S(1)}, u32[]{:S(2)}, u32[]{:S(2)}) collective-permute-start(f32[32,384]{1,0:T(8,128)S(1)} %get-tuple-element.9), channel_id=1, source_target_pairs={{0,128},{8,136},{16,144},{24,152},{32,160},{40,168},{48,176},{56,1... | collective-permute-start | bytes 147464 | tf_op jit(solution)/shard_map/ppermute | solution.py:253
  22.2 4.1 %collective-permute-start.4 = (f32[32,384]{1,0:T(8,128)S(1)}, f32[32,384]{1,0:T(8,128)S(1)}, u32[]{:S(2)}, u32[]{:S(2)}) collective-permute-start(f32[32,384]{1,0:T(8,128)S(1)} %get-tuple-element.10), channel_id=1, source_target_pairs={{0,64},{8,72},{16,80},{24,88},{32,96},{40,104},{48,112},{56,120},{... | collective-permute-start | bytes 147464 | tf_op jit(solution)/shard_map/ppermute | solution.py:253
  23.9 3.4 %collective-permute-start.14 = (bf16[224,256]{1,0:T(8,128)(2,1)S(1)}, bf16[224,256]{1,0:T(8,128)(2,1)S(1)}, u32[]{:S(2)}, u32[]{:S(2)}) collective-permute-start(bf16[224,256]{1,0:T(8,128)(2,1)S(1)} %get-tuple-element.6), channel_id=1, source_target_pairs={{0,1},{1,0},{2,3},{3,2},{4,5},{5,4},{6,7},{7,6},{8,9},{9,8},{10,11... | collective-permute-start | bytes 344072 | tf_op jit(solution)/shard_map/ppermute | solution.py:253
  28.4 34.7 %all-to-all-start = ((bf16[32,16,512]{2,1,0:T(8,128)(2,1)}), bf16[32,16,512]{2,1,0:T(8,128)(2,1)S(1)}, u32[]{:S(2)}, u32[]{:S(2)}) async-start(bf16[32,16,512]{2,1,0:T(8,128)(2,1)} %bitcast.11), calls=%async_computation | async-start | bytes 1048576 | tf_op jit(solution)/shard_map/all_to_all | solution.py:245
  37.9 16.0 %collective-permute-start.7 = (f32[32,384]{1,0:T(8,128)S(1)}, f32[32,384]{1,0:T(8,128)S(1)}, u32[]{:S(2)}, u32[]{:S(2)}) collective-permute-start(f32[32,384]{1,0:T(8,128)S(1)} %fusion.12), channel_id=1, source_target_pairs={{0,32},{8,40},{16,48},{24,56},{32,0},{40,8},{48,16},{56,24},{64,96... | collective-permute-start | bytes 147464 | tf_op jit(solution)/shard_map/ppermute | solution.py:253
  53.9 4.8 %collective-permute-start.10 = (f32[32,384]{1,0:T(8,128)S(1)}, f32[32,384]{1,0:T(8,128)S(1)}, u32[]{:S(2)}, u32[]{:S(2)}) collective-permute-start(f32[32,384]{1,0:T(8,128)S(1)} %add.59), channel_id=1, source_target_pairs={{0,24},{8,16},{16,8},{24,0},{32,56},{40,48},{48,40},{56,32},{64,88... | collective-permute-start | bytes 147464 | tf_op jit(solution)/shard_map/ppermute | solution.py:253
  54.0 5.8 %collective-permute-start.9 = (f32[32,384]{1,0:T(8,128)S(1)}, f32[32,384]{1,0:T(8,128)S(1)}, u32[]{:S(2)}, u32[]{:S(2)}) collective-permute-start(f32[32,384]{1,0:T(8,128)S(1)} %add.59), channel_id=1, source_target_pairs={{0,16},{8,24},{16,0},{24,8},{32,48},{40,56},{48,32},{56,40},{64,80... | collective-permute-start | bytes 147464 | tf_op jit(solution)/shard_map/ppermute | solution.py:253
  56.2 3.6 %collective-permute-start.8 = (f32[32,384]{1,0:T(8,128)S(1)}, f32[32,384]{1,0:T(8,128)S(1)}, u32[]{:S(2)}, u32[]{:S(2)}) collective-permute-start(f32[32,384]{1,0:T(8,128)S(1)} %add.59), channel_id=1, source_target_pairs={{0,8},{8,0},{16,24},{24,16},{32,40},{40,32},{48,56},{56,48},{64,72... | collective-permute-start | bytes 147464 | tf_op jit(solution)/shard_map/ppermute | solution.py:253
  59.8 3.4 %copy-start.2 = (f32[32,384]{1,0:T(8,128)}, f32[32,384]{1,0:T(8,128)S(1)}, u32[]{:S(2)}) copy-start(f32[32,384]{1,0:T(8,128)S(1)} %add_add_fusion.refs_0_) | copy-start | bytes 147460
  59.8 4.4 %collective-permute-start.13 = (f32[32,384]{1,0:T(8,128)S(1)}, f32[32,384]{1,0:T(8,128)S(1)}, u32[]{:S(2)}, u32[]{:S(2)}) collective-permute-start(f32[32,384]{1,0:T(8,128)S(1)} %add_add_fusion.refs_0_), channel_id=1, source_target_pairs={{0,192},{8,200},{16,208},{24,216},{32,224},{40,232},{48,240},{56,2... | collective-permute-start | bytes 147464 | tf_op jit(solution)/shard_map/ppermute | solution.py:253
  62.4 4.4 %collective-permute-start.12 = (f32[32,384]{1,0:T(8,128)S(1)}, f32[32,384]{1,0:T(8,128)S(1)}, u32[]{:S(2)}, u32[]{:S(2)}) collective-permute-start(f32[32,384]{1,0:T(8,128)S(1)} %add_add_fusion.refs_0_), channel_id=1, source_target_pairs={{0,128},{8,136},{16,144},{24,152},{32,160},{40,168},{48,176},{56,1... | collective-permute-start | bytes 147464 | tf_op jit(solution)/shard_map/ppermute | solution.py:253
  62.9 3.9 %collective-permute-start.11 = (f32[32,384]{1,0:T(8,128)S(1)}, f32[32,384]{1,0:T(8,128)S(1)}, u32[]{:S(2)}, u32[]{:S(2)}) collective-permute-start(f32[32,384]{1,0:T(8,128)S(1)} %add_add_fusion.refs_0_), channel_id=1, source_target_pairs={{0,64},{8,72},{16,80},{24,88},{32,96},{40,104},{48,112},{56,120},{... | collective-permute-start | bytes 147464 | tf_op jit(solution)/shard_map/ppermute | solution.py:253
  64.2 2.6 %copy-start.3 = (f32[32,384]{1,0:T(8,128)}, f32[32,384]{1,0:T(8,128)S(1)}, u32[]{:S(2)}) copy-start(f32[32,384]{1,0:T(8,128)S(1)} %collective-permute-done.13.refs_3_) | copy-start | bytes 147460
  66.8 0.6 copy-start.4
  66.8 0.6 copy-start.5
  69.0 8.9 %collective-permute-start.17 = (f32[128,384]{1,0:T(8,128)}, f32[128,384]{1,0:T(8,128)S(1)}, u32[]{:S(2)}, u32[]{:S(2)}) collective-permute-start(f32[128,384]{1,0:T(8,128)} %bitcast.43), channel_id=1, source_target_pairs={{0,6},{1,7},{2,0},{3,1},{4,2},{5,3},{6,4},{7,5},{8,14},{9,15},{10,... | collective-permute-start | bytes 589832 | tf_op jit(solution)/shard_map/ppermute | solution.py:318
  71.6 6.4 %collective-permute-start.16 = (f32[128,384]{1,0:T(8,128)}, f32[128,384]{1,0:T(8,128)S(1)}, u32[]{:S(2)}, u32[]{:S(2)}) collective-permute-start(f32[128,384]{1,0:T(8,128)} %bitcast.44), channel_id=1, source_target_pairs={{0,4},{1,5},{2,6},{3,7},{4,0},{5,1},{6,2},{7,3},{8,12},{9,13},{10,... | collective-permute-start | bytes 589832 | tf_op jit(solution)/shard_map/ppermute | solution.py:318
  71.9 8.0 %collective-permute-start.15 = (f32[128,384]{1,0:T(8,128)}, f32[128,384]{1,0:T(8,128)S(1)}, u32[]{:S(2)}, u32[]{:S(2)}) collective-permute-start(f32[128,384]{1,0:T(8,128)} %bitcast.45), channel_id=1, source_target_pairs={{0,2},{1,3},{2,4},{3,5},{4,6},{5,7},{6,0},{7,1},{8,10},{9,11},{10,... | collective-permute-start | bytes 589832 | tf_op jit(solution)/shard_map/ppermute | solution.py:318
  73.5 6.4 %copy-start.1 = (f32[4,32,384]{2,1,0:T(8,128)S(1)}, f32[4,32,384]{2,1,0:T(8,128)}, u32[]{:S(2)}) copy-start(f32[4,32,384]{2,1,0:T(8,128)} %shard_map.51) | copy-start | bytes 589828
  73.5 25.2 %all-to-all-start.1 = ((bf16[32,16,512]{2,1,0:T(8,128)(2,1)}), bf16[32,16,512]{2,1,0:T(8,128)(2,1)S(1)}, u32[]{:S(2)}, u32[]{:S(2)}) async-start(bf16[32,16,512]{2,1,0:T(8,128)(2,1)} %broadcast_in_dim.4), calls=%async_computation.1 | async-start | bytes 1048576 | tf_op jit(solution)/shard_map/all_to_all | solution.py:245
  99.2 12.9 %collective-permute-start.21 = (f32[1,512]{1,0:T(1,128)S(1)}, f32[1,512]{1,0:T(1,128)S(1)}, u32[]{:S(2)}, u32[]{:S(2)}) collective-permute-start(f32[1,512]{1,0:T(1,128)S(1)} %bitcast.50), channel_id=1, source_target_pairs={{0,6},{1,7},{2,4},{3,5},{4,2},{5,3},{6,0},{7,1},{8,14},{9,15},{10,... | collective-permute-start | bytes 6152 | tf_op jit(solution)/shard_map/ppermute | solution.py:253
  99.6 12.5 %collective-permute-start.20 = (f32[1,512]{1,0:T(1,128)S(1)}, f32[1,512]{1,0:T(1,128)S(1)}, u32[]{:S(2)}, u32[]{:S(2)}) collective-permute-start(f32[1,512]{1,0:T(1,128)S(1)} %bitcast.51), channel_id=1, source_target_pairs={{0,4},{1,5},{2,6},{3,7},{4,0},{5,1},{6,2},{7,3},{8,12},{9,13},{10,... | collective-permute-start | bytes 6152 | tf_op jit(solution)/shard_map/ppermute | solution.py:253
  100.7 11.4 %collective-permute-start.19 = (f32[1,512]{1,0:T(1,128)S(1)}, f32[1,512]{1,0:T(1,128)S(1)}, u32[]{:S(2)}, u32[]{:S(2)}) collective-permute-start(f32[1,512]{1,0:T(1,128)S(1)} %bitcast.52), channel_id=1, source_target_pairs={{0,2},{1,3},{2,0},{3,1},{4,6},{5,7},{6,4},{7,5},{8,10},{9,11},{10,... | collective-permute-start | bytes 6152 | tf_op jit(solution)/shard_map/ppermute | solution.py:253
  102.9 11.5 %collective-permute-start.18 = (bf16[224,256]{1,0:T(8,128)(2,1)S(1)}, bf16[224,256]{1,0:T(8,128)(2,1)S(1)}, u32[]{:S(2)}, u32[]{:S(2)}) collective-permute-start(bf16[224,256]{1,0:T(8,128)(2,1)S(1)} %fusion.8), channel_id=1, source_target_pairs={{0,1},{1,0},{2,3},{3,2},{4,5},{5,4},{6,7},{7,6},{8,9},{9,8},{10,11... | collective-permute-start | bytes 344072 | tf_op jit(solution)/shard_map/ppermute | solution.py:253
  112.5 2.8 %collective-permute-start.22 = (bf16[224,256]{1,0:T(8,128)(2,1)S(1)}, bf16[224,256]{1,0:T(8,128)(2,1)S(1)}, u32[]{:S(2)}, u32[]{:S(2)}) collective-permute-start(bf16[224,256]{1,0:T(8,128)(2,1)S(1)} %fusion.6), channel_id=1, source_target_pairs={{0,1},{1,0},{2,3},{3,2},{4,5},{5,4},{6,7},{7,6},{8,9},{9,8},{10,11... | collective-permute-start | bytes 344072 | tf_op jit(solution)/shard_map/ppermute | solution.py:253

commit v4 on v3

--- a/solution.py
+++ b/solution.py
@@ -7,6 +7,7 @@
 from jax import lax
 from jax.experimental import pallas as pl
 from jax.experimental.pallas import tpu as pltpu
+from jax.sharding import Mesh
 from jax.sharding import PartitionSpec as P
 
 ROWS = 7168
@@ -213,14 +214,14 @@
         out_ref[lax.bitwise_xor(where_ref[0], step)] = ref[...]
 
 
-def placed_parts(where, parts, after):
+def placed_parts(where, parts):
     vmem = pl.BlockSpec(memory_space=pltpu.VMEM)
     return pl.pallas_call(
         place_kernel,
         out_shape=jax.ShapeDtypeStruct((X_SIZE,) + parts[0].shape, parts[0].dtype),
-        in_specs=[pl.BlockSpec(memory_space=pltpu.SMEM)] + [vmem] * (X_SIZE + 1),
+        in_specs=[pl.BlockSpec(memory_space=pltpu.SMEM)] + [vmem] * X_SIZE,
         out_specs=vmem,
-    )(where, *parts, after)
+    )(where, *parts)
 
 
 def wide_kernel(own_ref, other_ref, right_ref, _, out_ref):
@@ -241,116 +242,152 @@
     )(own, other, right, after)
 
 
+def solve_kernel(where_ref, inverse_ref, wide_ref, out_ref, squares_ref):
+    squares = jnp.zeros(squares_ref.shape, jnp.float32)
+    for step in range(X_SIZE):
+        rows = wide_ref[:, step].reshape(out_ref.shape[1:])
+        value = lax.dot_general(
+            rows, inverse_ref[...], (((1,), (1,)), ((), ())), preferred_element_type=jnp.float32
+        )
+        out_ref[lax.bitwise_xor(where_ref[0], step)] = value
+        squares += jnp.sum(value * value, axis=0, keepdims=True)
+    squares_ref[...] = squares
+
+
+def solved_rows(where, inverse, wide):
+    vmem = pl.BlockSpec(memory_space=pltpu.VMEM)
+    return pl.pallas_call(
+        solve_kernel,
+        out_shape=(
+            jax.ShapeDtypeStruct((X_SIZE, Z_SIZE * wide.shape[2], RANK), jnp.float32),
+            jax.ShapeDtypeStruct((1, RANK), jnp.float32),
+        ),
+        in_specs=[pl.BlockSpec(memory_space=pltpu.SMEM), vmem, vmem],
+        out_specs=(vmem, vmem),
+        compiler_params=pltpu.CompilerParams(vmem_limit_bytes=24 * 1024 * 1024),
+    )(where, inverse, wide)
+
+
+def sum_kernel(*refs):
+    terms = [ref[...].astype(jnp.float32) for ref in refs[:-2]]
+    refs[-1][...] = added(terms).astype(refs[-1].dtype)
+
+
+def summed(terms, after):
+    vmem = pl.BlockSpec(memory_space=pltpu.VMEM)
+    return pl.pallas_call(
+        sum_kernel,
+        out_shape=jax.ShapeDtypeStruct(terms[0].shape, terms[0].dtype),
+        in_specs=[vmem] * (len(terms) + 1),
+        out_specs=vmem,
+    )(*terms, after)
+
+
+SIZES = {"x": X_SIZE, "z": Z_SIZE, "y": BLOCKS, "core": 2}
+
+
 def spread(chunks, axis):
     return lax.all_to_all(chunks, axis, split_axis=0, concat_axis=0, tiled=True)
 
 
-def share(value, axis, count):
-    return spread(jnp.broadcast_to(value[None], (count,) + value.shape), axis)
-
-
-def swap(value, axis, count, mask):
-    return lax.ppermute(value, axis, [(i, i ^ mask) for i in range(count)])
+def swap(value, axis, mask=1):
+    return lax.ppermute(value, axis, [(i, i ^ mask) for i in range(SIZES[axis])])
+
+
+def quad(value, axis):
+    return [value] + [swap(value, axis, step) for step in (1, 2, 3)]
 
 
 def pick(first, value, other):
     return jnp.stack([jnp.where(first, value, other), jnp.where(first, other, value)])
 
 
-def make_local(row_count, col_count):
-    def item(stack, index):
-        return lax.dynamic_index_in_dim(stack, index, 0, keepdims=False)
-
-    def quad(value, axis, count, low):
-        return [value] + [swap(value, axis, count, step * low) for step in (1, 2, 3)]
-
-    def x_sum(value, plane):
-        pieces = value.reshape(X_SIZE, value.shape[0] // X_SIZE, value.shape[1])
-        terms = [item(pieces, plane)]
-        for step in range(1, X_SIZE):
-            send = item(pieces, lax.bitwise_xor(plane, np.uint32(step)))
-            terms.append(swap(send, "row", row_count, step * Z_SIZE))
-        return added(terms)
-
-    def z_sum(value):
-        value = value + swap(value, "row", row_count, 4)
-        return added(quad(value, "row", row_count, 1))
-
-    def local(momentum, gradient, basis_in):
-        experts, rows, cols = momentum.shape
-        rank = basis_in.shape[-1]
-        row = lax.axis_index("row").astype(jnp.uint32)
-        col = lax.axis_index("col").astype(jnp.uint32)
-        expert = lax.rem(col, np.uint32(experts))
-        place = lax.div(col, np.uint32(experts))
-        first = expert == 0
-        buffer = lax.optimization_barrier(momentum + gradient.astype(jnp.float32))
-        half = buffer.astype(jnp.bfloat16)
-        partial = jnp.einsum(
-            "erc,eck->erk", half, basis_in, preferred_element_type=jnp.float32
-        ).astype(jnp.bfloat16)
-        term = item(partial, expert) + swap(item(partial, 1 - expert), "col", col_count, 1)
-        terms = [part.astype(jnp.float32) for part in quad(term, "col", col_count, experts)]
-        projected = added(terms).astype(jnp.bfloat16)
-
-        turned = lax.dynamic_slice_in_dim(
-            jnp.concatenate([projected, projected[:, : (KEPT - 1) * BLOCK]], axis=1),
-            place * np.uint32(BLOCK),
-            KEPT * BLOCK,
-            axis=1,
-        )
-        gram = jnp.einsum("rk,rl->kl", turned[:, :BLOCK], turned, preferred_element_type=jnp.float32)
-        plane = lax.div(row, np.uint32(Z_SIZE))
-        gram = x_sum(gram, plane)
-        left = swap(item(half, 1 - expert), "col", col_count, 1)
-        wide = wide_product(item(half, expert), left, projected, gram[:PANEL, :BLOCK])
-        wide = wide.reshape(row_count, 2 * cols // row_count, rank)
-        wide = jnp.sum(spread(wide, "row").astype(jnp.float32), axis=0).astype(jnp.bfloat16)
-        gram = z_sum(gram)
-        slab = placed_parts(
-            jnp.reshape(plane, (1,)).astype(jnp.int32),
-            quad(gram, "row", row_count, Z_SIZE),
-            wide[: 2 * PANEL, :BLOCK],
-        ).reshape(BLOCK, KEPT * BLOCK)
-        slabs = [slab]
-        for step in range(1, BLOCKS):
-            turn = [(i, (i + step * experts) % col_count) for i in range(col_count)]
-            slabs.append(lax.ppermute(slab, "col", turn))
-        wide = share(wide, "row", row_count).reshape(2 * cols, rank)
-
-        inverse = inverse_factor(jnp.reshape(place, (1,)).astype(jnp.int32), slabs)
-
-        def solve(value):
-            return jnp.einsum("rk,lk->rl", value, inverse, preferred_element_type=jnp.float32)
-
-        reduced = solve(wide)
-        squares = jnp.sum(reduced * reduced, axis=0, keepdims=True)
-        squares = added(quad(squares, "col", col_count, experts))
-        orthonormal = solve(projected).astype(jnp.bfloat16)
-
-        def outer(right):
-            value = jnp.einsum("rk,ck->rc", orthonormal, right, preferred_element_type=jnp.float32)
-            return value[:, :cols], value[:, cols:]
-
-        own, other = outer(reduced.astype(jnp.bfloat16))
-        other = swap((0.1 * other).astype(jnp.bfloat16), "col", col_count, 1)
-        momentum_new = buffer - pick(first, 0.1 * own, other.astype(jnp.float32))
-        new_basis = (reduced * lax.rsqrt(squares + 1e-06)).astype(jnp.bfloat16)
-        update_scale = math.sqrt(ROWS * COLS / RANK)
-        own, other = outer(new_basis)
-        own = (update_scale * own).astype(jnp.bfloat16)
-        other = swap((update_scale * other).astype(jnp.bfloat16), "col", col_count, 1)
-        return (momentum_new, pick(first, own, other))
-
-    return local
+def item(stack, index):
+    return lax.dynamic_index_in_dim(stack, index, 0, keepdims=False)
+
+
+def x_terms(value, plane):
+    pieces = value.reshape(X_SIZE, value.shape[0] // X_SIZE, value.shape[1])
+    terms = [item(pieces, plane)]
+    for step in range(1, X_SIZE):
+        send = item(pieces, lax.bitwise_xor(plane, np.uint32(step)))
+        terms.append(swap(send, "x", step))
+    return terms
+
+
+def local(momentum, gradient, basis_in):
+    experts, rows, cols = momentum.shape
+    rank = basis_in.shape[-1]
+    expert = lax.axis_index("core").astype(jnp.uint32)
+    place = lax.axis_index("y").astype(jnp.uint32)
+    plane = lax.axis_index("x").astype(jnp.uint32)
+    where_y = jnp.reshape(place, (1,)).astype(jnp.int32)
+    where_x = jnp.reshape(plane, (1,)).astype(jnp.int32)
+    first = expert == 0
+    buffer = lax.optimization_barrier(momentum + gradient.astype(jnp.float32))
+    half = buffer.astype(jnp.bfloat16)
+    partial = jnp.einsum(
+        "erc,eck->erk", half, basis_in, preferred_element_type=jnp.float32
+    ).astype(jnp.bfloat16)
+    term = item(partial, expert) + swap(item(partial, 1 - expert), "core")
+    projected = added([part.astype(jnp.float32) for part in quad(term, "y")]).astype(jnp.bfloat16)
+
+    turned = lax.dynamic_slice_in_dim(
+        jnp.concatenate([projected, projected[:, : (KEPT - 1) * BLOCK]], axis=1),
+        place * np.uint32(BLOCK),
+        KEPT * BLOCK,
+        axis=1,
+    )
+    gram = jnp.einsum("rk,rl->kl", turned[:, :BLOCK], turned, preferred_element_type=jnp.float32)
+    gram = added(x_terms(gram, plane))
+
+    left = swap(item(half, 1 - expert), "core")
+    wide = wide_product(item(half, expert), left, projected, gram[:PANEL, :BLOCK])
+    terms = x_terms(wide.reshape(2 * cols, rank), plane)
+
+    gram = gram + swap(gram, "z", 4)
+    gram = added(quad(gram, "z"))
+    wide = summed(terms, gram[:PANEL, :BLOCK])
+    wide = spread(wide.reshape(Z_SIZE, 2 * cols // (X_SIZE * Z_SIZE), rank), "z")
+    wide = jnp.sum(wide.astype(jnp.float32), axis=0).astype(jnp.bfloat16)
+    wide = jnp.stack(quad(wide, "x"))
+    wide = spread(jnp.broadcast_to(wide[None], (Z_SIZE,) + wide.shape), "z")
+
+    slab = placed_parts(where_x, quad(gram, "x")).reshape(BLOCK, KEPT * BLOCK)
+    slabs = [slab]
+    for step in range(1, BLOCKS):
+        slabs.append(lax.ppermute(slab, "y", [(i, (i + step) % BLOCKS) for i in range(BLOCKS)]))
+
+    inverse = inverse_factor(where_y, slabs)
+    reduced, squares = solved_rows(where_x, inverse, wide)
+    reduced = reduced.reshape(2 * cols, rank)
+    squares = added(quad(squares, "y"))
+    orthonormal = jnp.einsum(
+        "rk,lk->rl", projected, inverse, preferred_element_type=jnp.float32
+    ).astype(jnp.bfloat16)
+
+    def outer(right):
+        value = jnp.einsum("rk,ck->rc", orthonormal, right, preferred_element_type=jnp.float32)
+        return value[:, :cols], value[:, cols:]
+
+    own, other = outer(reduced.astype(jnp.bfloat16))
+    other = swap((0.1 * other).astype(jnp.bfloat16), "core")
+    momentum_new = buffer - pick(first, 0.1 * own, other.astype(jnp.float32))
+    new_basis = (reduced * lax.rsqrt(squares + 1e-06)).astype(jnp.bfloat16)
+    update_scale = math.sqrt(ROWS * COLS / RANK)
+    own, other = outer(new_basis)
+    own = (update_scale * own).astype(jnp.bfloat16)
+    other = swap((update_scale * other).astype(jnp.bfloat16), "core")
+    return (momentum_new, pick(first, own, other))
 
 
 def solution(mesh):
-    placed = (P(None, "row", "col"), P(None, "row", "col"), P(None, "col", None))
+    lines = Mesh(mesh.devices.reshape(X_SIZE, Z_SIZE, BLOCKS, 2), ("x", "z", "y", "core"))
+    placed = P(None, ("x", "z"), ("y", "core"))
     return jax.shard_map(
-        make_local(mesh.shape["row"], mesh.shape["col"]),
-        mesh=mesh,
-        in_specs=placed,
-        out_specs=(P(None, "row", "col"), P(None, "row", "col")),
+        local,
+        mesh=lines,
+        in_specs=(placed, placed, P(None, ("y", "core"), None)),
+        out_specs=(placed, placed),
         check_vma=False,
     )

time: 116 us -> 122 us (1.052)
  starting transfers between devices: 56.5 us -> 67.4 us
  waiting for transfers between devices: 30.1 us -> 22.3 us
  Pallas kernels: 21.1 us -> 23 us
  local copies, waits for them, and re-layouts: 2.22 us -> 3.56 us
    ppermute x23 -> x29, starting transfers between devices: 42.6 us -> 54.3 us  [the longest x26 50.6 us: swap(): lax.ppermute(value, axis, [(i, i ^ mask) for i in range(SIZES[axis])])]
    ppermute x23 -> x29, waiting for transfers between devices: 30.1 us -> 22.2 us  [the longest x26 22.2 us: swap(): lax.ppermute(value, axis, [(i, i ^ mask) for i in range(SIZES[axis])])]
    pallas_call x0 -> x2, Pallas kernels: none -> 2.62 us  [the longest x1 1.8 us: summed(): pl.pallas_call(sum_kernel, out_shape=jax.ShapeDtypeStruct(terms[0].shape,...]
  transfers between devices with their start and end apart: 25 -> 31, of which waited for: 11 -> 13; matrix products, arithmetic and copies ran while one was open for 3% -> 4% of each run, Pallas kernels for 16% -> 17%
where the time goes in v4:
time: 122 us
  starting transfers between devices  67.4 us (55%)
  Pallas kernels  23 us (19%)
  waiting for transfers between devices  22.3 us (18%)
  local copies, waits for them, and re-layouts  3.56 us (3%)
  other arithmetic  3.33 us (3%)
  matrix products  1.46 us (1%)
    ppermute x26, starting transfers between devices, swap(): lax.ppermute(value, axis, [(i, i ^ mask) for i in range(SIZES[axis])])  50.6 us
    ppermute x26, waiting for transfers between devices, swap(): lax.ppermute(value, axis, [(i, i ^ mask) for i in range(SIZES[axis])])  22.2 us
    pallas_call x1, Pallas kernels, inverse_factor(): pl.pallas_call(factor_kernel, out_shape=jax.ShapeDtypeStruct((RANK, RANK)...  18.5 us
    all_to_all x2, starting transfers between devices, spread(): return lax.all_to_all(chunks, axis, split_axis=0, concat_axis=0, tiled=True)  13.1 us
    ppermute x3, starting transfers between devices, local(): lax.ppermute(slab, 'y', [(i, (i + step) % BLOCKS) for i in range(BLOCKS)])  3.62 us
  transfers between devices with their start and end apart: 31, of which 13 were waited for; matrix products, arithmetic and copies ran while one was open for 4% of the time, Pallas kernels for 17%

profile of v4, /device:TPU:1, one launch (start us, length us, event | category | flops | bytes accessed | tf_op | source)
XLA Modules:
  0.0 121.9 jit_solution(8157929153450242520)
XLA Ops:
  0.7 1.2 convert_add_fusion
  2.2 3.3 %collective-permute-start = (bf16[224,512]{1,0:T(8,128)(2,1)S(1)}, bf16[224,512]{1,0:T(8,128)(2,1)S(1)}, u32[]{:S(2)}, u32[]{:S(2)}) collective-permute-start(bf16[224,512]{1,0:T(8,128)(2,1)S(1)} %dynamic-slice_bitcast_fusion), channel_id=1, source_target_pairs={{0,1},{1,0},{2,3},{3,2},{4,5},{5,4},{6,7},{7,6},{8,9},{9,8},{10,11... | collective-permute-start | bytes 688136 | tf_op jit(solution)/shard_map/ppermute | solution.py:294
  5.6 1.1 collective-permute-done
  6.7 1.1 collective-permute-start.3
  8.2 1.9 %collective-permute-start.1 = (bf16[224,512]{1,0:T(8,128)(2,1)S(1)}, bf16[224,512]{1,0:T(8,128)(2,1)S(1)}, u32[]{:S(2)}, u32[]{:S(2)}) collective-permute-start(bf16[224,512]{1,0:T(8,128)(2,1)S(1)} %bitcast_add_fusion), channel_id=1, source_target_pairs={{0,2},{2,0},{4,6},{6,4},{1,3},{3,1},{5,7},{7,5},{8,10},{10,8},{12,... | collective-permute-start | bytes 688136 | tf_op jit(solution)/shard_map/ppermute | solution.py:294
  10.1 9.7 %collective-permute-done.3 = bf16[224,512]{1,0:T(8,128)(2,1)S(1)} collective-permute-done((bf16[224,512]{1,0:T(8,128)(2,1)S(1)}, bf16[224,512]{1,0:T(8,128)(2,1)S(1)}, u32[]{:S(2)}, u32[]{:S(2)}) %collective-permute-start.3) | collective-permute-done | bytes 229408 | tf_op jit(solution)/shard_map/ppermute | solution.py:294
  20.6 1.1 collective-permute-start.6
  22.2 1.7 %collective-permute-start.4 = (f32[32,384]{1,0:T(8,128)S(1)}, f32[32,384]{1,0:T(8,128)S(1)}, u32[]{:S(2)}, u32[]{:S(2)}) collective-permute-start(f32[32,384]{1,0:T(8,128)S(1)} %get-tuple-element.18), channel_id=1, source_target_pairs={{0,64},{64,0},{128,192},{192,128},{1,65},{65,1},{129,193},{193,129... | collective-permute-start | bytes 147464 | tf_op jit(solution)/shard_map/ppermute | solution.py:294
  23.9 2.4 %collective-permute-start.17 = (bf16[224,256]{1,0:T(8,128)(2,1)S(1)}, bf16[224,256]{1,0:T(8,128)(2,1)S(1)}, u32[]{:S(2)}, u32[]{:S(2)}) collective-permute-start(bf16[224,256]{1,0:T(8,128)(2,1)S(1)} %get-tuple-element.14), channel_id=1, source_target_pairs={{0,1},{1,0},{2,3},{3,2},{4,5},{5,4},{6,7},{7,6},{8,9},{9,8},{10,11... | collective-permute-start | bytes 344072 | tf_op jit(solution)/shard_map/ppermute | solution.py:294
  26.4 6.8 %collective-permute-start.7 = (f32[32,384]{1,0:T(8,128)S(1)}, f32[32,384]{1,0:T(8,128)S(1)}, u32[]{:S(2)}, u32[]{:S(2)}) collective-permute-start(f32[32,384]{1,0:T(8,128)S(1)} %fusion.9), channel_id=1, source_target_pairs={{0,32},{8,40},{16,48},{24,56},{32,0},{40,8},{48,16},{56,24},{1,33}... | collective-permute-start | bytes 147464 | tf_op jit(solution)/shard_map/ppermute | solution.py:294
  33.5 1.1 collective-permute-done.7
  34.6 2.9 %collective-permute-start.10 = (f32[32,384]{1,0:T(8,128)S(1)}, f32[32,384]{1,0:T(8,128)S(1)}, u32[]{:S(2)}, u32[]{:S(2)}) collective-permute-start(f32[32,384]{1,0:T(8,128)S(1)} %add.59), channel_id=1, source_target_pairs={{0,24},{8,16},{16,8},{24,0},{32,56},{40,48},{48,40},{56,32},{1,25}... | collective-permute-start | bytes 147464 | tf_op jit(solution)/shard_map/ppermute | solution.py:294
  37.5 0.7 collective-permute-start.8
  38.3 0.7 dynamic-slice_bitcast_fusion.1
  39.0 1.1 collective-permute-start.20
  40.1 0.6 collective-permute-start.19
  40.7 1.5 %collective-permute-start.18 = (bf16[128,512]{1,0:T(8,128)(2,1)S(1)}, bf16[128,512]{1,0:T(8,128)(2,1)S(1)}, u32[]{:S(2)}, u32[]{:S(2)}) collective-permute-start(bf16[128,512]{1,0:T(8,128)(2,1)S(1)} %get-tuple-element.12), channel_id=1, source_target_pairs={{0,64},{64,0},{128,192},{192,128},{1,65},{65,1},{129,193},{193,129... | collective-permute-start | bytes 393224 | tf_op jit(solution)/shard_map/ppermute | solution.py:294
  42.2 0.6 slice.35.refs_4_
  42.8 1.1 collective-permute-done.20.refs_3_
  44.0 1.4 %collective-permute-done.19.refs_2_ = bf16[128,512]{1,0:T(8,128)(2,1)S(1)} collective-permute-done((bf16[128,512]{1,0:T(8,128)(2,1)S(1)}, bf16[128,512]{1,0:T(8,128)(2,1)S(1)}, u32[]{:S(2)}, u32[]{:S(2)}) %collective-permute-start.19) | collective-permute-done | bytes 131104 | tf_op jit(solution)/shard_map/ppermute | solution.py:294
  45.4 0.9 collective-permute-done.18.refs_1_
  46.3 0.6 copy-done.5
  46.9 1.8 %shard_map.53 = bf16[128,512]{1,0:T(8,128)(2,1)} custom-call(bf16[128,512]{1,0:T(8,128)(2,1)} %get-tuple-element.13.refs_0_, bf16[128,512]{1,0:T(8,128)(2,1)} %copy-done.5, bf16[128,512]{1,0:T(8,128)(2,1)} %copy-done.4, bf16[128,512]{1,0:T(8,128)(2,1)} %copy-done.3, f32[8,128]{1,0:T(8,128)} %slice.35.refs_4_), custom_call_target="tpu_custom_call" | custom-call | tf_op jit(solution)/shard_map/pallas_call | solution.py:278
  48.7 6.3 %all-to-all-start = ((bf16[8,16,512]{2,1,0:T(8,128)(2,1)}), bf16[8,16,512]{2,1,0:T(8,128)(2,1)S(1)}, u32[]{:S(2)}, u32[]{:S(2)}) async-start(bf16[8,16,512]{2,1,0:T(8,128)(2,1)} %bitcast.66), calls=%async_computation | async-start | bytes 262144 | tf_op jit(solution)/shard_map/all_to_all | solution.py:290
  55.1 1.1 collective-permute-start.13
  56.2 0.7 collective-permute-start.12
  56.9 1.4 %collective-permute-start.11 = (f32[32,384]{1,0:T(8,128)S(1)}, f32[32,384]{1,0:T(8,128)S(1)}, u32[]{:S(2)}, u32[]{:S(2)}) collective-permute-start(f32[32,384]{1,0:T(8,128)S(1)} %add_add_fusion.refs_0_), channel_id=1, source_target_pairs={{0,64},{64,0},{128,192},{192,128},{1,65},{65,1},{129,193},{193,129... | collective-permute-start | bytes 147464 | tf_op jit(solution)/shard_map/ppermute | solution.py:294
  58.3 0.9 collective-permute-done.13.refs_3_
  59.2 1.4 %collective-permute-done.12.refs_2_ = f32[32,384]{1,0:T(8,128)S(1)} collective-permute-done((f32[32,384]{1,0:T(8,128)S(1)}, f32[32,384]{1,0:T(8,128)S(1)}, u32[]{:S(2)}, u32[]{:S(2)}) %collective-permute-start.12) | collective-permute-done | bytes 49184 | tf_op jit(solution)/shard_map/ppermute | solution.py:294
  60.6 0.6 copy-done.7
  61.3 1.6 %shard_map.50 = f32[4,32,384]{2,1,0:T(8,128)} custom-call(s32[1]{0:T(128)} %bitcast.3.where_ref, f32[32,384]{1,0:T(8,128)} %copy-done.2, f32[32,384]{1,0:T(8,128)} %copy-done.8, f32[32,384]{1,0:T(8,128)} %copy-done.7, f32[32,384]{1,0:T(8,128)} %copy-done.6), custom_call_target="tpu_custom_call" | custom-call | tf_op jit(solution)/shard_map/pallas_call | solution.py:219
  62.8 2.6 %collective-permute-start.16 = (f32[128,384]{1,0:T(8,128)}, f32[128,384]{1,0:T(8,128)S(1)}, u32[]{:S(2)}, u32[]{:S(2)}) collective-permute-start(f32[128,384]{1,0:T(8,128)} %bitcast.60), channel_id=1, source_target_pairs={{0,6},{2,0},{4,2},{6,4},{1,7},{3,1},{5,3},{7,5},{8,14},{10,8},{12,... | collective-permute-start | bytes 589832 | tf_op jit(solution)/shard_map/ppermute | solution.py:359
  65.8 0.7 collective-permute-start.14
  66.5 1.5 %collective-permute-start.23 = (bf16[16,512]{1,0:T(8,128)(2,1)S(1)}, bf16[16,512]{1,0:T(8,128)(2,1)S(1)}, u32[]{:S(2)}, u32[]{:S(2)}) collective-permute-start(bf16[16,512]{1,0:T(8,128)(2,1)S(1)} %reduce_sum.12), channel_id=1, source_target_pairs={{0,192},{64,128},{128,64},{192,0},{1,193},{65,129},{129,65},{193,1... | collective-permute-start | bytes 49160 | tf_op jit(solution)/shard_map/ppermute | solution.py:294
  68.0 0.8 collective-permute-start.22
  68.8 1.5 %collective-permute-done.23 = bf16[16,512]{1,0:T(8,128)(2,1)S(1)} collective-permute-done((bf16[16,512]{1,0:T(8,128)(2,1)S(1)}, bf16[16,512]{1,0:T(8,128)(2,1)S(1)}, u32[]{:S(2)}, u32[]{:S(2)}) %collective-permute-start.23) | collective-permute-done | bytes 16416 | tf_op jit(solution)/shard_map/ppermute | solution.py:294
  70.4 1.7 %collective-permute-done.22 = bf16[16,512]{1,0:T(8,128)(2,1)S(1)} collective-permute-done((bf16[16,512]{1,0:T(8,128)(2,1)S(1)}, bf16[16,512]{1,0:T(8,128)(2,1)S(1)}, u32[]{:S(2)}, u32[]{:S(2)}) %collective-permute-start.22) | collective-permute-done | bytes 16416 | tf_op jit(solution)/shard_map/ppermute | solution.py:294
  72.1 0.9 collective-permute-done.21
  73.0 0.9 broadcast_in_dim.2
  73.8 6.8 %all-to-all-start.1 = ((bf16[8,4,16,512]{3,2,1,0:T(8,128)(2,1)}), bf16[8,4,16,512]{3,2,1,0:T(8,128)(2,1)S(1)}, u32[]{:S(2)}, u32[]{:S(2)}) async-start(bf16[8,4,16,512]{3,2,1,0:T(8,128)(2,1)} %broadcast_in_dim.2), calls=%async_computation.1 | async-start | bytes 1048576 | tf_op jit(solution)/shard_map/all_to_all | solution.py:290
  80.6 18.5 %shard_map.51.inverse_ref = bf16[512,512]{1,0:T(8,128)(2,1)S(1)} custom-call(s32[1]{0:T(128)} %bitcast.2.where_ref, f32[128,384]{1,0:T(8,128)S(1)} %bitcast.63, f32[128,384]{1,0:T(8,128)S(1)} %collective-permute-done.14.one_ref, f32[128,384]{1,0:T(8,128)S(1)} %collective-permute-done.15.two_ref, f32[128,384]{1,0:T(8,128)S(1)} %collective-permute-done.16.three_ref), custom_call_target="tpu_custom_call" | custom-call | flops 20000000000 | tf_op jit(solution)/shard_map/pallas_call | solution.py:197
  99.5 0.8 shard_map.54
  100.3 2.1 %collective-permute-start.27 = (f32[1,512]{1,0:T(1,128)S(1)}, f32[1,512]{1,0:T(1,128)S(1)}, u32[]{:S(2)}, u32[]{:S(2)}) collective-permute-start(f32[1,512]{1,0:T(1,128)S(1)} %get-tuple-element.5), channel_id=1, source_target_pairs={{0,6},{2,4},{4,2},{6,0},{1,7},{3,5},{5,3},{7,1},{8,14},{10,12},{12... | collective-permute-start | bytes 6152 | tf_op jit(solution)/shard_map/ppermute | solution.py:294
  102.4 1.4 %collective-permute-start.26 = (f32[1,512]{1,0:T(1,128)S(1)}, f32[1,512]{1,0:T(1,128)S(1)}, u32[]{:S(2)}, u32[]{:S(2)}) collective-permute-start(f32[1,512]{1,0:T(1,128)S(1)} %get-tuple-element.5), channel_id=1, source_target_pairs={{0,4},{2,6},{4,0},{6,2},{1,5},{3,7},{5,1},{7,3},{8,12},{10,14},{12... | collective-permute-start | bytes 6152 | tf_op jit(solution)/shard_map/ppermute | solution.py:294
  104.2 12.4 %collective-permute-start.24 = (bf16[224,256]{1,0:T(8,128)(2,1)S(1)}, bf16[224,256]{1,0:T(8,128)(2,1)S(1)}, u32[]{:S(2)}, u32[]{:S(2)}) collective-permute-start(bf16[224,256]{1,0:T(8,128)(2,1)S(1)} %fusion.5), channel_id=1, source_target_pairs={{0,1},{1,0},{2,3},{3,2},{4,5},{5,4},{6,7},{7,6},{8,9},{9,8},{10,11... | collective-permute-start | bytes 344072 | tf_op jit(solution)/shard_map/ppermute | solution.py:294
  117.2 3.0 %collective-permute-start.28 = (bf16[224,256]{1,0:T(8,128)(2,1)S(1)}, bf16[224,256]{1,0:T(8,128)(2,1)S(1)}, u32[]{:S(2)}, u32[]{:S(2)}) collective-permute-start(bf16[224,256]{1,0:T(8,128)(2,1)S(1)} %fusion.3), channel_id=1, source_target_pairs={{0,1},{1,0},{2,3},{3,2},{4,5},{5,4},{6,7},{7,6},{8,9},{9,8},{10,11... | collective-permute-start | bytes 344072 | tf_op jit(solution)/shard_map/ppermute | solution.py:294
  120.2 0.8 maximum_subtract_fusion
  121.2 0.7 pad_maximum_fusion
  (69 shorter events, 4.3 us)
Async XLA Ops:
  0.6 1.3 %copy-start = (bf16[2,256,512]{2,1,0:T(8,128)(2,1)S(1)}, bf16[2,256,512]{2,1,0:T(8,128)(2,1)}, u32[]{:S(2)}) copy-start(bf16[2,256,512]{2,1,0:T(8,128)(2,1)} %param.5) | copy-start | bytes 1572868
  2.2 4.4 %collective-permute-start = (bf16[224,512]{1,0:T(8,128)(2,1)S(1)}, bf16[224,512]{1,0:T(8,128)(2,1)S(1)}, u32[]{:S(2)}, u32[]{:S(2)}) collective-permute-start(bf16[224,512]{1,0:T(8,128)(2,1)S(1)} %dynamic-slice_bitcast_fusion), channel_id=1, source_target_pairs={{0,1},{1,0},{2,3},{3,2},{4,5},{5,4},{6,7},{7,6},{8,9},{9,8},{10,11... | collective-permute-start | bytes 688136 | tf_op jit(solution)/shard_map/ppermute | solution.py:294
  6.7 13.0 %collective-permute-start.3 = (bf16[224,512]{1,0:T(8,128)(2,1)S(1)}, bf16[224,512]{1,0:T(8,128)(2,1)S(1)}, u32[]{:S(2)}, u32[]{:S(2)}) collective-permute-start(bf16[224,512]{1,0:T(8,128)(2,1)S(1)} %bitcast_add_fusion), channel_id=1, source_target_pairs={{0,6},{2,4},{4,2},{6,0},{1,7},{3,5},{5,3},{7,1},{8,14},{10,12},{12... | collective-permute-start | bytes 688136 | tf_op jit(solution)/shard_map/ppermute | solution.py:294
  7.8 11.9 %collective-permute-start.2 = (bf16[224,512]{1,0:T(8,128)(2,1)S(1)}, bf16[224,512]{1,0:T(8,128)(2,1)S(1)}, u32[]{:S(2)}, u32[]{:S(2)}) collective-permute-start(bf16[224,512]{1,0:T(8,128)(2,1)S(1)} %bitcast_add_fusion), channel_id=1, source_target_pairs={{0,4},{2,6},{4,0},{6,2},{1,5},{3,7},{5,1},{7,3},{8,12},{10,14},{12... | collective-permute-start | bytes 688136 | tf_op jit(solution)/shard_map/ppermute | solution.py:294
  8.2 11.9 %collective-permute-start.1 = (bf16[224,512]{1,0:T(8,128)(2,1)S(1)}, bf16[224,512]{1,0:T(8,128)(2,1)S(1)}, u32[]{:S(2)}, u32[]{:S(2)}) collective-permute-start(bf16[224,512]{1,0:T(8,128)(2,1)S(1)} %bitcast_add_fusion), channel_id=1, source_target_pairs={{0,2},{2,0},{4,6},{6,4},{1,3},{3,1},{5,7},{7,5},{8,10},{10,8},{12,... | collective-permute-start | bytes 688136 | tf_op jit(solution)/shard_map/ppermute | solution.py:294
  20.6 5.8 %collective-permute-start.6 = (f32[32,384]{1,0:T(8,128)S(1)}, f32[32,384]{1,0:T(8,128)S(1)}, u32[]{:S(2)}, u32[]{:S(2)}) collective-permute-start(f32[32,384]{1,0:T(8,128)S(1)} %get-tuple-element.16), channel_id=1, source_target_pairs={{0,192},{64,128},{128,64},{192,0},{1,193},{65,129},{129,65},{193,1... | collective-permute-start | bytes 147464 | tf_op jit(solution)/shard_map/ppermute | solution.py:294
  21.7 4.7 %collective-permute-start.5 = (f32[32,384]{1,0:T(8,128)S(1)}, f32[32,384]{1,0:T(8,128)S(1)}, u32[]{:S(2)}, u32[]{:S(2)}) collective-permute-start(f32[32,384]{1,0:T(8,128)S(1)} %get-tuple-element.17), channel_id=1, source_target_pairs={{0,128},{64,192},{128,0},{192,64},{1,129},{65,193},{129,1},{193,65... | collective-permute-start | bytes 147464 | tf_op jit(solution)/shard_map/ppermute | solution.py:294
  22.2 4.1 %collective-permute-start.4 = (f32[32,384]{1,0:T(8,128)S(1)}, f32[32,384]{1,0:T(8,128)S(1)}, u32[]{:S(2)}, u32[]{:S(2)}) collective-permute-start(f32[32,384]{1,0:T(8,128)S(1)} %get-tuple-element.18), channel_id=1, source_target_pairs={{0,64},{64,0},{128,192},{192,128},{1,65},{65,1},{129,193},{193,129... | collective-permute-start | bytes 147464 | tf_op jit(solution)/shard_map/ppermute | solution.py:294
  23.9 9.2 %collective-permute-start.17 = (bf16[224,256]{1,0:T(8,128)(2,1)S(1)}, bf16[224,256]{1,0:T(8,128)(2,1)S(1)}, u32[]{:S(2)}, u32[]{:S(2)}) collective-permute-start(bf16[224,256]{1,0:T(8,128)(2,1)S(1)} %get-tuple-element.14), channel_id=1, source_target_pairs={{0,1},{1,0},{2,3},{3,2},{4,5},{5,4},{6,7},{7,6},{8,9},{9,8},{10,11... | collective-permute-start | bytes 344072 | tf_op jit(solution)/shard_map/ppermute | solution.py:294
  26.4 8.3 %collective-permute-start.7 = (f32[32,384]{1,0:T(8,128)S(1)}, f32[32,384]{1,0:T(8,128)S(1)}, u32[]{:S(2)}, u32[]{:S(2)}) collective-permute-start(f32[32,384]{1,0:T(8,128)S(1)} %fusion.9), channel_id=1, source_target_pairs={{0,32},{8,40},{16,48},{24,56},{32,0},{40,8},{48,16},{56,24},{1,33}... | collective-permute-start | bytes 147464 | tf_op jit(solution)/shard_map/ppermute | solution.py:294
  34.6 6.1 %collective-permute-start.10 = (f32[32,384]{1,0:T(8,128)S(1)}, f32[32,384]{1,0:T(8,128)S(1)}, u32[]{:S(2)}, u32[]{:S(2)}) collective-permute-start(f32[32,384]{1,0:T(8,128)S(1)} %add.59), channel_id=1, source_target_pairs={{0,24},{8,16},{16,8},{24,0},{32,56},{40,48},{48,40},{56,32},{1,25}... | collective-permute-start | bytes 147464 | tf_op jit(solution)/shard_map/ppermute | solution.py:294
  37.5 4.7 %collective-permute-start.9 = (f32[32,384]{1,0:T(8,128)S(1)}, f32[32,384]{1,0:T(8,128)S(1)}, u32[]{:S(2)}, u32[]{:S(2)}) collective-permute-start(f32[32,384]{1,0:T(8,128)S(1)} %add.59), channel_id=1, source_target_pairs={{0,16},{8,24},{16,0},{24,8},{32,48},{40,56},{48,32},{56,40},{1,17}... | collective-permute-start | bytes 147464 | tf_op jit(solution)/shard_map/ppermute | solution.py:294
  37.5 4.7 %collective-permute-start.8 = (f32[32,384]{1,0:T(8,128)S(1)}, f32[32,384]{1,0:T(8,128)S(1)}, u32[]{:S(2)}, u32[]{:S(2)}) collective-permute-start(f32[32,384]{1,0:T(8,128)S(1)} %add.59), channel_id=1, source_target_pairs={{0,8},{8,0},{16,24},{24,16},{32,40},{40,32},{48,56},{56,48},{1,9},... | collective-permute-start | bytes 147464 | tf_op jit(solution)/shard_map/ppermute | solution.py:294
  39.0 5.0 %collective-permute-start.20 = (bf16[128,512]{1,0:T(8,128)(2,1)S(1)}, bf16[128,512]{1,0:T(8,128)(2,1)S(1)}, u32[]{:S(2)}, u32[]{:S(2)}) collective-permute-start(bf16[128,512]{1,0:T(8,128)(2,1)S(1)} %get-tuple-element.10), channel_id=1, source_target_pairs={{0,192},{64,128},{128,64},{192,0},{1,193},{65,129},{129,65},{193,1... | collective-permute-start | bytes 393224 | tf_op jit(solution)/shard_map/ppermute | solution.py:294
  40.1 5.3 %collective-permute-start.19 = (bf16[128,512]{1,0:T(8,128)(2,1)S(1)}, bf16[128,512]{1,0:T(8,128)(2,1)S(1)}, u32[]{:S(2)}, u32[]{:S(2)}) collective-permute-start(bf16[128,512]{1,0:T(8,128)(2,1)S(1)} %get-tuple-element.11), channel_id=1, source_target_pairs={{0,128},{64,192},{128,0},{192,64},{1,129},{65,193},{129,1},{193,65... | collective-permute-start | bytes 393224 | tf_op jit(solution)/shard_map/ppermute | solution.py:294
  40.7 5.6 %collective-permute-start.18 = (bf16[128,512]{1,0:T(8,128)(2,1)S(1)}, bf16[128,512]{1,0:T(8,128)(2,1)S(1)}, u32[]{:S(2)}, u32[]{:S(2)}) collective-permute-start(bf16[128,512]{1,0:T(8,128)(2,1)S(1)} %get-tuple-element.12), channel_id=1, source_target_pairs={{0,64},{64,0},{128,192},{192,128},{1,65},{65,1},{129,193},{193,129... | collective-permute-start | bytes 393224 | tf_op jit(solution)/shard_map/ppermute | solution.py:294
  42.2 14.7 %copy-start.2 = (f32[32,384]{1,0:T(8,128)}, f32[32,384]{1,0:T(8,128)S(1)}, u32[]{:S(2)}) copy-start(f32[32,384]{1,0:T(8,128)S(1)} %add_add_fusion.refs_0_) | copy-start | bytes 147460
  44.0 2.3 %copy-start.3 = (bf16[128,512]{1,0:T(8,128)(2,1)}, bf16[128,512]{1,0:T(8,128)(2,1)S(1)}, u32[]{:S(2)}) copy-start(bf16[128,512]{1,0:T(8,128)(2,1)S(1)} %collective-permute-done.20.refs_3_) | copy-start | bytes 393220
  45.4 0.9 copy-start.4
  46.3 0.7 copy-start.5
  48.7 17.7 %all-to-all-start = ((bf16[8,16,512]{2,1,0:T(8,128)(2,1)}), bf16[8,16,512]{2,1,0:T(8,128)(2,1)S(1)}, u32[]{:S(2)}, u32[]{:S(2)}) async-start(bf16[8,16,512]{2,1,0:T(8,128)(2,1)} %bitcast.66), calls=%async_computation | async-start | bytes 262144 | tf_op jit(solution)/shard_map/all_to_all | solution.py:290
  55.1 4.2 %collective-permute-start.13 = (f32[32,384]{1,0:T(8,128)S(1)}, f32[32,384]{1,0:T(8,128)S(1)}, u32[]{:S(2)}, u32[]{:S(2)}) collective-permute-start(f32[32,384]{1,0:T(8,128)S(1)} %add_add_fusion.refs_0_), channel_id=1, source_target_pairs={{0,192},{64,128},{128,64},{192,0},{1,193},{65,129},{129,65},{193,1... | collective-permute-start | bytes 147464 | tf_op jit(solution)/shard_map/ppermute | solution.py:294
  56.2 4.4 %collective-permute-start.12 = (f32[32,384]{1,0:T(8,128)S(1)}, f32[32,384]{1,0:T(8,128)S(1)}, u32[]{:S(2)}, u32[]{:S(2)}) collective-permute-start(f32[32,384]{1,0:T(8,128)S(1)} %add_add_fusion.refs_0_), channel_id=1, source_target_pairs={{0,128},{64,192},{128,0},{192,64},{1,129},{65,193},{129,1},{193,65... | collective-permute-start | bytes 147464 | tf_op jit(solution)/shard_map/ppermute | solution.py:294
  56.9 3.7 %collective-permute-start.11 = (f32[32,384]{1,0:T(8,128)S(1)}, f32[32,384]{1,0:T(8,128)S(1)}, u32[]{:S(2)}, u32[]{:S(2)}) collective-permute-start(f32[32,384]{1,0:T(8,128)S(1)} %add_add_fusion.refs_0_), channel_id=1, source_target_pairs={{0,64},{64,0},{128,192},{192,128},{1,65},{65,1},{129,193},{193,129... | collective-permute-start | bytes 147464 | tf_op jit(solution)/shard_map/ppermute | solution.py:294
  59.2 1.4 %copy-start.6 = (f32[32,384]{1,0:T(8,128)}, f32[32,384]{1,0:T(8,128)S(1)}, u32[]{:S(2)}) copy-start(f32[32,384]{1,0:T(8,128)S(1)} %collective-permute-done.13.refs_3_) | copy-start | bytes 147460
  60.6 0.6 copy-start.7
  60.6 0.6 copy-start.8
  62.8 17.8 %collective-permute-start.16 = (f32[128,384]{1,0:T(8,128)}, f32[128,384]{1,0:T(8,128)S(1)}, u32[]{:S(2)}, u32[]{:S(2)}) collective-permute-start(f32[128,384]{1,0:T(8,128)} %bitcast.60), channel_id=1, source_target_pairs={{0,6},{2,0},{4,2},{6,4},{1,7},{3,1},{5,3},{7,5},{8,14},{10,8},{12,... | collective-permute-start | bytes 589832 | tf_op jit(solution)/shard_map/ppermute | solution.py:359
  65.4 15.2 %collective-permute-start.15 = (f32[128,384]{1,0:T(8,128)}, f32[128,384]{1,0:T(8,128)S(1)}, u32[]{:S(2)}, u32[]{:S(2)}) collective-permute-start(f32[128,384]{1,0:T(8,128)} %bitcast.61), channel_id=1, source_target_pairs={{0,4},{2,6},{4,0},{6,2},{1,5},{3,7},{5,1},{7,3},{8,12},{10,14},{12... | collective-permute-start | bytes 589832 | tf_op jit(solution)/shard_map/ppermute | solution.py:359
  65.8 14.9 %collective-permute-start.14 = (f32[128,384]{1,0:T(8,128)}, f32[128,384]{1,0:T(8,128)S(1)}, u32[]{:S(2)}, u32[]{:S(2)}) collective-permute-start(f32[128,384]{1,0:T(8,128)} %bitcast.62), channel_id=1, source_target_pairs={{0,2},{2,4},{4,6},{6,0},{1,3},{3,5},{5,7},{7,1},{8,10},{10,12},{12... | collective-permute-start | bytes 589832 | tf_op jit(solution)/shard_map/ppermute | solution.py:359
  66.5 3.9 %collective-permute-start.23 = (bf16[16,512]{1,0:T(8,128)(2,1)S(1)}, bf16[16,512]{1,0:T(8,128)(2,1)S(1)}, u32[]{:S(2)}, u32[]{:S(2)}) collective-permute-start(bf16[16,512]{1,0:T(8,128)(2,1)S(1)} %reduce_sum.12), channel_id=1, source_target_pairs={{0,192},{64,128},{128,64},{192,0},{1,193},{65,129},{129,65},{193,1... | collective-permute-start | bytes 49160 | tf_op jit(solution)/shard_map/ppermute | solution.py:294
  68.0 4.1 %collective-permute-start.22 = (bf16[16,512]{1,0:T(8,128)(2,1)S(1)}, bf16[16,512]{1,0:T(8,128)(2,1)S(1)}, u32[]{:S(2)}, u32[]{:S(2)}) collective-permute-start(bf16[16,512]{1,0:T(8,128)(2,1)S(1)} %reduce_sum.12), channel_id=1, source_target_pairs={{0,128},{64,192},{128,0},{192,64},{1,129},{65,193},{129,1},{193,65... | collective-permute-start | bytes 49160 | tf_op jit(solution)/shard_map/ppermute | solution.py:294
  70.4 2.6 %collective-permute-start.21 = (bf16[16,512]{1,0:T(8,128)(2,1)S(1)}, bf16[16,512]{1,0:T(8,128)(2,1)S(1)}, u32[]{:S(2)}, u32[]{:S(2)}) collective-permute-start(bf16[16,512]{1,0:T(8,128)(2,1)S(1)} %reduce_sum.12), channel_id=1, source_target_pairs={{0,64},{64,0},{128,192},{192,128},{1,65},{65,1},{129,193},{193,129... | collective-permute-start | bytes 49160 | tf_op jit(solution)/shard_map/ppermute | solution.py:294
  73.8 6.8 %copy-start.1 = (f32[4,32,384]{2,1,0:T(8,128)S(1)}, f32[4,32,384]{2,1,0:T(8,128)}, u32[]{:S(2)}) copy-start(f32[4,32,384]{2,1,0:T(8,128)} %shard_map.50) | copy-start | bytes 589828
  73.8 25.6 %all-to-all-start.1 = ((bf16[8,4,16,512]{3,2,1,0:T(8,128)(2,1)}), bf16[8,4,16,512]{3,2,1,0:T(8,128)(2,1)S(1)}, u32[]{:S(2)}, u32[]{:S(2)}) async-start(bf16[8,4,16,512]{3,2,1,0:T(8,128)(2,1)} %broadcast_in_dim.2), calls=%async_computation.1 | async-start | bytes 1048576 | tf_op jit(solution)/shard_map/all_to_all | solution.py:290
  100.3 16.4 %collective-permute-start.27 = (f32[1,512]{1,0:T(1,128)S(1)}, f32[1,512]{1,0:T(1,128)S(1)}, u32[]{:S(2)}, u32[]{:S(2)}) collective-permute-start(f32[1,512]{1,0:T(1,128)S(1)} %get-tuple-element.5), channel_id=1, source_target_pairs={{0,6},{2,4},{4,2},{6,0},{1,7},{3,5},{5,3},{7,1},{8,14},{10,12},{12... | collective-permute-start | bytes 6152 | tf_op jit(solution)/shard_map/ppermute | solution.py:294
  102.4 14.3 %collective-permute-start.26 = (f32[1,512]{1,0:T(1,128)S(1)}, f32[1,512]{1,0:T(1,128)S(1)}, u32[]{:S(2)}, u32[]{:S(2)}) collective-permute-start(f32[1,512]{1,0:T(1,128)S(1)} %get-tuple-element.5), channel_id=1, source_target_pairs={{0,4},{2,6},{4,0},{6,2},{1,5},{3,7},{5,1},{7,3},{8,12},{10,14},{12... | collective-permute-start | bytes 6152 | tf_op jit(solution)/shard_map/ppermute | solution.py:294
  103.8 12.9 %collective-permute-start.25 = (f32[1,512]{1,0:T(1,128)S(1)}, f32[1,512]{1,0:T(1,128)S(1)}, u32[]{:S(2)}, u32[]{:S(2)}) collective-permute-start(f32[1,512]{1,0:T(1,128)S(1)} %get-tuple-element.5), channel_id=1, source_target_pairs={{0,2},{2,0},{4,6},{6,4},{1,3},{3,1},{5,7},{7,5},{8,10},{10,8},{12,... | collective-permute-start | bytes 6152 | tf_op jit(solution)/shard_map/ppermute | solution.py:294
  104.2 16.0 %collective-permute-start.24 = (bf16[224,256]{1,0:T(8,128)(2,1)S(1)}, bf16[224,256]{1,0:T(8,128)(2,1)S(1)}, u32[]{:S(2)}, u32[]{:S(2)}) collective-permute-start(bf16[224,256]{1,0:T(8,128)(2,1)S(1)} %fusion.5), channel_id=1, source_target_pairs={{0,1},{1,0},{2,3},{3,2},{4,5},{5,4},{6,7},{7,6},{8,9},{9,8},{10,11... | collective-permute-start | bytes 344072 | tf_op jit(solution)/shard_map/ppermute | solution.py:294
  117.2 4.0 %collective-permute-start.28 = (bf16[224,256]{1,0:T(8,128)(2,1)S(1)}, bf16[224,256]{1,0:T(8,128)(2,1)S(1)}, u32[]{:S(2)}, u32[]{:S(2)}) collective-permute-start(bf16[224,256]{1,0:T(8,128)(2,1)S(1)} %fusion.3), channel_id=1, source_target_pairs={{0,1},{1,0},{2,3},{3,2},{4,5},{5,4},{6,7},{7,6},{8,9},{9,8},{10,11... | collective-permute-start | bytes 344072 | tf_op jit(solution)/shard_map/ppermute | solution.py:294

commit v5 on v4

--- a/solution.py
+++ b/solution.py
@@ -208,81 +208,6 @@
     )(where, *slabs)
 
 
-def place_kernel(where_ref, *refs):
-    parts, out_ref = refs[:X_SIZE], refs[-1]
-    for step, ref in enumerate(parts):
-        out_ref[lax.bitwise_xor(where_ref[0], step)] = ref[...]
-
-
-def placed_parts(where, parts):
-    vmem = pl.BlockSpec(memory_space=pltpu.VMEM)
-    return pl.pallas_call(
-        place_kernel,
-        out_shape=jax.ShapeDtypeStruct((X_SIZE,) + parts[0].shape, parts[0].dtype),
-        in_specs=[pl.BlockSpec(memory_space=pltpu.SMEM)] + [vmem] * X_SIZE,
-        out_specs=vmem,
-    )(where, *parts)
-
-
-def wide_kernel(own_ref, other_ref, right_ref, _, out_ref):
-    for i, ref in enumerate((own_ref, other_ref)):
-        out_ref[i] = lax.dot_general(
-            ref[...], right_ref[...], (((0,), (0,)), ((), ())), preferred_element_type=jnp.float32
-        ).astype(out_ref.dtype)
-
-
-def wide_product(own, other, right, after):
-    vmem = pl.BlockSpec(memory_space=pltpu.VMEM)
-    return pl.pallas_call(
-        wide_kernel,
-        out_shape=jax.ShapeDtypeStruct((2, own.shape[1], right.shape[1]), jnp.bfloat16),
-        in_specs=[vmem] * 4,
-        out_specs=vmem,
-        compiler_params=pltpu.CompilerParams(vmem_limit_bytes=24 * 1024 * 1024),
-    )(own, other, right, after)
-
-
-def solve_kernel(where_ref, inverse_ref, wide_ref, out_ref, squares_ref):
-    squares = jnp.zeros(squares_ref.shape, jnp.float32)
-    for step in range(X_SIZE):
-        rows = wide_ref[:, step].reshape(out_ref.shape[1:])
-        value = lax.dot_general(
-            rows, inverse_ref[...], (((1,), (1,)), ((), ())), preferred_element_type=jnp.float32
-        )
-        out_ref[lax.bitwise_xor(where_ref[0], step)] = value
-        squares += jnp.sum(value * value, axis=0, keepdims=True)
-    squares_ref[...] = squares
-
-
-def solved_rows(where, inverse, wide):
-    vmem = pl.BlockSpec(memory_space=pltpu.VMEM)
-    return pl.pallas_call(
-        solve_kernel,
-        out_shape=(
-            jax.ShapeDtypeStruct((X_SIZE, Z_SIZE * wide.shape[2], RANK), jnp.float32),
-            jax.ShapeDtypeStruct((1, RANK), jnp.float32),
-        ),
-        in_specs=[pl.BlockSpec(memory_space=pltpu.SMEM), vmem, vmem],
-        out_specs=(vmem, vmem),
-        compiler_params=pltpu.CompilerParams(vmem_limit_bytes=24 * 1024 * 1024),
-    )(where, inverse, wide)
-
-
-def sum_kernel(*refs):
-    terms = [ref[...].astype(jnp.float32) for ref in refs[:-2]]
-    refs[-1][...] = added(terms).astype(refs[-1].dtype)
-
-
-def summed(terms, after):
-    vmem = pl.BlockSpec(memory_space=pltpu.VMEM)
-    return pl.pallas_call(
-        sum_kernel,
-        out_shape=jax.ShapeDtypeStruct(terms[0].shape, terms[0].dtype),
-        in_specs=[vmem] * (len(terms) + 1),
-        out_specs=vmem,
-    )(*terms, after)
-
-
 SIZES = {"x": X_SIZE, "z": Z_SIZE, "y": BLOCKS, "core": 2}
 
 
@@ -321,8 +246,6 @@
     expert = lax.axis_index("core").astype(jnp.uint32)
     place = lax.axis_index("y").astype(jnp.uint32)
     plane = lax.axis_index("x").astype(jnp.uint32)
-    where_y = jnp.reshape(place, (1,)).astype(jnp.int32)
-    where_x = jnp.reshape(plane, (1,)).astype(jnp.int32)
     first = expert == 0
     buffer = lax.optimization_barrier(momentum + gradient.astype(jnp.float32))
     half = buffer.astype(jnp.bfloat16)
@@ -330,7 +253,10 @@
         "erc,eck->erk", half, basis_in, preferred_element_type=jnp.float32
     ).astype(jnp.bfloat16)
     term = item(partial, expert) + swap(item(partial, 1 - expert), "core")
-    projected = added([part.astype(jnp.float32) for part in quad(term, "y")]).astype(jnp.bfloat16)
+    upper, lower = term[: rows // 2], term[rows // 2 :]
+    upper, lower = upper + swap(upper, "y", 1), lower + swap(lower, "y", 3)
+    upper, lower = upper + swap(upper, "y", 3), lower + swap(lower, "y", 1)
+    projected = jnp.concatenate([upper, lower], axis=0)
 
     turned = lax.dynamic_slice_in_dim(
         jnp.concatenate([projected, projected[:, : (KEPT - 1) * BLOCK]], axis=1),
@@ -341,30 +267,32 @@
     gram = jnp.einsum("rk,rl->kl", turned[:, :BLOCK], turned, preferred_element_type=jnp.float32)
     gram = added(x_terms(gram, plane))
 
-    left = swap(item(half, 1 - expert), "core")
-    wide = wide_product(item(half, expert), left, projected, gram[:PANEL, :BLOCK])
-    terms = x_terms(wide.reshape(2 * cols, rank), plane)
-
     gram = gram + swap(gram, "z", 4)
     gram = added(quad(gram, "z"))
-    wide = summed(terms, gram[:PANEL, :BLOCK])
-    wide = spread(wide.reshape(Z_SIZE, 2 * cols // (X_SIZE * Z_SIZE), rank), "z")
-    wide = jnp.sum(wide.astype(jnp.float32), axis=0).astype(jnp.bfloat16)
-    wide = jnp.stack(quad(wide, "x"))
-    wide = spread(jnp.broadcast_to(wide[None], (Z_SIZE,) + wide.shape), "z")
-
-    slab = placed_parts(where_x, quad(gram, "x")).reshape(BLOCK, KEPT * BLOCK)
+    parts = quad(gram, "x")
+    low = lax.bitwise_and(plane, np.uint32(1)) == 0
+    slab = pick(
+        plane < np.uint32(2), pick(low, parts[0], parts[1]), pick(low, parts[2], parts[3])
+    ).reshape(BLOCK, KEPT * BLOCK)
     slabs = [slab]
     for step in range(1, BLOCKS):
         slabs.append(lax.ppermute(slab, "y", [(i, (i + step) % BLOCKS) for i in range(BLOCKS)]))
 
-    inverse = inverse_factor(where_y, slabs)
-    reduced, squares = solved_rows(where_x, inverse, wide)
-    reduced = reduced.reshape(2 * cols, rank)
-    squares = added(quad(squares, "y"))
-    orthonormal = jnp.einsum(
-        "rk,lk->rl", projected, inverse, preferred_element_type=jnp.float32
-    ).astype(jnp.bfloat16)
+    whole = jnp.stack([item(half, expert), swap(item(half, 1 - expert), "core")])
+    wide = jnp.einsum("hrc,rk->hck", whole, projected, preferred_element_type=jnp.float32)
+    row_count = X_SIZE * Z_SIZE
+    wide = wide.astype(jnp.bfloat16).reshape(row_count, 2 * cols // row_count, rank)
+    wide = jnp.sum(spread(wide, ("x", "z")).astype(jnp.float32), axis=0).astype(jnp.bfloat16)
+    wide = spread(jnp.broadcast_to(wide[None], (row_count,) + wide.shape), ("x", "z"))
+
+    inverse = inverse_factor(jnp.reshape(place, (1,)).astype(jnp.int32), slabs)
+
+    def solve(value):
+        return jnp.einsum("rk,lk->rl", value, inverse, preferred_element_type=jnp.float32)
+
+    reduced = solve(wide.reshape(2 * cols, rank))
+    squares = added(quad(jnp.sum(reduced * reduced, axis=0, keepdims=True), "y"))
+    orthonormal = solve(projected).astype(jnp.bfloat16)
 
     def outer(right):
         value = jnp.einsum("rk,ck->rc", orthonormal, right, preferred_element_type=jnp.float32)

time: 122 us -> 104 us (0.85)
  starting transfers between devices: 67.4 us -> 61.1 us
  waiting for transfers between devices: 22.3 us -> 16 us
  Pallas kernels: 23 us -> 18.4 us
  local copies, waits for them, and re-layouts: 3.56 us -> 0.99 us
  matrix products: 1.46 us -> 3.08 us
    ppermute x26 -> x21, starting transfers between devices: 50.6 us -> 42.8 us  [swap(): lax.ppermute(value, axis, [(i, i ^ mask) for i in range(SIZES[axis])])]
    ppermute x26 -> x21, waiting for transfers between devices: 22.2 us -> 15 us  [swap(): lax.ppermute(value, axis, [(i, i ^ mask) for i in range(SIZES[axis])])]
    pallas_call x4 -> x0, Pallas kernels: 4.51 us -> none  [the longest x1 1.8 us: summed(): pl.pallas_call(sum_kernel, out_shape=jax.ShapeDtypeStruct(terms[0].shape,...]
    all_to_all x2, starting transfers between devices: 13.1 us -> 16.1 us  [spread(): return lax.all_to_all(chunks, axis, split_axis=0, concat_axis=0, tiled=True)]
    dot_general x1 -> x3, matrix products: 0.33 us -> 1.93 us  [the longest x1 1.12 us: local(): jnp.einsum('hrc,rk->hck', whole, projected, preferred_element_type=jnp.fl...]
    ppermute x3, starting transfers between devices: 3.62 us -> 2.12 us  [local(): lax.ppermute(slab, 'y', [(i, (i + step) % BLOCKS) for i in range(BLOCKS)])]
    unnamed x18 -> x2, local copies, waits for them, and re-layouts: 1.36 us -> 0.06 us
  transfers between devices with their start and end apart: 31 -> 26, of which waited for: 13 -> 9; matrix products, arithmetic and copies ran while one was open for 4% -> 4% of each run, Pallas kernels for 17% -> 18%
where the time goes in v5:
time: 104 us
  starting transfers between devices  61.1 us (59%)
  Pallas kernels  18.4 us (18%)
  waiting for transfers between devices  16 us (15%)
  other arithmetic  3.39 us (3%)
  matrix products  3.08 us (3%)
    ppermute x21, starting transfers between devices, swap(): lax.ppermute(value, axis, [(i, i ^ mask) for i in range(SIZES[axis])])  42.8 us
    pallas_call x1, Pallas kernels, inverse_factor(): pl.pallas_call(factor_kernel, out_shape=jax.ShapeDtypeStruct((RANK, RANK)...  18.4 us
    all_to_all x2, starting transfers between devices, spread(): return lax.all_to_all(chunks, axis, split_axis=0, concat_axis=0, tiled=True)  16.1 us
    ppermute x21, waiting for transfers between devices, swap(): lax.ppermute(value, axis, [(i, i ^ mask) for i in range(SIZES[axis])])  15 us
    ppermute x3, starting transfers between devices, local(): lax.ppermute(slab, 'y', [(i, (i + step) % BLOCKS) for i in range(BLOCKS)])  2.12 us
  transfers between devices with their start and end apart: 26, of which 9 were waited for; matrix products, arithmetic and copies ran while one was open for 4% of the time, Pallas kernels for 18%

profile of v5, /device:TPU:1, one launch (start us, length us, event | category | flops | bytes accessed | tf_op | source)
XLA Modules:
  0.0 103.9 jit_solution(14009173801011065145)
XLA Ops:
  0.6 0.0 copy-start
  0.7 1.2 %convert_add_fusion = f32[2,224,256]{2,1,0:T(8,128)S(1)} fusion(f32[2,224,256]{2,1,0:T(8,128)} %param.3, bf16[2,224,256]{2,1,0:T(8,128)(2,1)} %param.4), kind=kLoop, calls=%fused_computation.10 | loop fusion | flops 229376 | bytes 1146880 | tf_op jit(solution)/shard_map/add | solution.py:250
  1.9 0.1 copy-done
  1.9 0.3 convolution_convert_fusion.1
  2.2 3.3 %collective-permute-start = (bf16[224,512]{1,0:T(8,128)(2,1)S(1)}, bf16[224,512]{1,0:T(8,128)(2,1)S(1)}, u32[]{:S(2)}, u32[]{:S(2)}) collective-permute-start(bf16[224,512]{1,0:T(8,128)(2,1)S(1)} %dynamic-slice_bitcast_fusion), channel_id=1, source_target_pairs={{0,1},{1,0},{2,3},{3,2},{4,5},{5,4},{6,7},{7,6},{8,9},{9,8},{10,11... | collective-permute-start | bytes 688136 | tf_op jit(solution)/shard_map/ppermute | solution.py:219
  5.6 1.1 %collective-permute-done = bf16[224,512]{1,0:T(8,128)(2,1)S(1)} collective-permute-done((bf16[224,512]{1,0:T(8,128)(2,1)S(1)}, bf16[224,512]{1,0:T(8,128)(2,1)S(1)}, u32[]{:S(2)}, u32[]{:S(2)}) %collective-permute-start) | collective-permute-done | bytes 229408 | tf_op jit(solution)/shard_map/ppermute | solution.py:219
  6.7 1.1 %collective-permute-start.3 = (bf16[112,512]{1,0:T(8,128)(2,1)S(1)}, bf16[112,512]{1,0:T(8,128)(2,1)S(1)}, u32[]{:S(2)}, u32[]{:S(2)}) collective-permute-start(bf16[112,512]{1,0:T(8,128)(2,1)S(1)} %get-tuple-element.10), channel_id=1, source_target_pairs={{0,6},{2,4},{4,2},{6,0},{1,7},{3,5},{5,3},{7,1},{8,14},{10,12},{12... | collective-permute-start | bytes 344072 | tf_op jit(solution)/shard_map/ppermute | solution.py:219
  7.8 4.6 %collective-permute-done.3 = bf16[112,512]{1,0:T(8,128)(2,1)S(1)} collective-permute-done((bf16[112,512]{1,0:T(8,128)(2,1)S(1)}, bf16[112,512]{1,0:T(8,128)(2,1)S(1)}, u32[]{:S(2)}, u32[]{:S(2)}) %collective-permute-start.3) | collective-permute-done | bytes 114720 | tf_op jit(solution)/shard_map/ppermute | solution.py:219
  12.4 0.1 collective-permute-start.4
  12.5 1.5 %collective-permute-start.2 = (bf16[112,512]{1,0:T(8,128)(2,1)S(1)}, bf16[112,512]{1,0:T(8,128)(2,1)S(1)}, u32[]{:S(2)}, u32[]{:S(2)}) collective-permute-start(bf16[112,512]{1,0:T(8,128)(2,1)S(1)} %get-tuple-element.9), channel_id=1, source_target_pairs={{0,6},{2,4},{4,2},{6,0},{1,7},{3,5},{5,3},{7,1},{8,14},{10,12},{12... | collective-permute-start | bytes 344072 | tf_op jit(solution)/shard_map/ppermute | solution.py:219
  14.0 2.2 %collective-permute-done.4 = bf16[112,512]{1,0:T(8,128)(2,1)S(1)} collective-permute-done((bf16[112,512]{1,0:T(8,128)(2,1)S(1)}, bf16[112,512]{1,0:T(8,128)(2,1)S(1)}, u32[]{:S(2)}, u32[]{:S(2)}) %collective-permute-start.4) | collective-permute-done | bytes 114720 | tf_op jit(solution)/shard_map/ppermute | solution.py:219
  16.2 1.3 %collective-permute-done.2 = bf16[112,512]{1,0:T(8,128)(2,1)S(1)} collective-permute-done((bf16[112,512]{1,0:T(8,128)(2,1)S(1)}, bf16[112,512]{1,0:T(8,128)(2,1)S(1)}, u32[]{:S(2)}, u32[]{:S(2)}) %collective-permute-start.2) | collective-permute-done | bytes 114720 | tf_op jit(solution)/shard_map/ppermute | solution.py:219
  17.5 0.2 fusion.14
  17.8 0.2 fusion.18
  18.0 2.1 %collective-permute-start.7 = (f32[32,384]{1,0:T(8,128)S(1)}, f32[32,384]{1,0:T(8,128)S(1)}, u32[]{:S(2)}, u32[]{:S(2)}) collective-permute-start(f32[32,384]{1,0:T(8,128)S(1)} %get-tuple-element.14), channel_id=1, source_target_pairs={{0,192},{64,128},{128,64},{192,0},{1,193},{65,129},{129,65},{193,1... | collective-permute-start | bytes 147464 | tf_op jit(solution)/shard_map/ppermute | solution.py:219
  20.1 0.5 collective-permute-start.6
  20.6 0.7 collective-permute-start.5
  21.4 3.3 %collective-permute-start.18 = (bf16[224,256]{1,0:T(8,128)(2,1)S(1)}, bf16[224,256]{1,0:T(8,128)(2,1)S(1)}, u32[]{:S(2)}, u32[]{:S(2)}) collective-permute-start(bf16[224,256]{1,0:T(8,128)(2,1)S(1)} %get-tuple-element.7), channel_id=1, source_target_pairs={{0,1},{1,0},{2,3},{3,2},{4,5},{5,4},{6,7},{7,6},{8,9},{9,8},{10,11... | collective-permute-start | bytes 344072 | tf_op jit(solution)/shard_map/ppermute | solution.py:219
  24.7 7.0 %collective-permute-start.8 = (f32[32,384]{1,0:T(8,128)S(1)}, f32[32,384]{1,0:T(8,128)S(1)}, u32[]{:S(2)}, u32[]{:S(2)}) collective-permute-start(f32[32,384]{1,0:T(8,128)S(1)} %fusion.20), channel_id=1, source_target_pairs={{0,32},{8,40},{16,48},{24,56},{32,0},{40,8},{48,16},{56,24},{1,33}... | collective-permute-start | bytes 147464 | tf_op jit(solution)/shard_map/ppermute | solution.py:219
  31.6 1.5 %collective-permute-done.8 = f32[32,384]{1,0:T(8,128)S(1)} collective-permute-done((f32[32,384]{1,0:T(8,128)S(1)}, f32[32,384]{1,0:T(8,128)S(1)}, u32[]{:S(2)}, u32[]{:S(2)}) %collective-permute-start.8) | collective-permute-done | bytes 49184 | tf_op jit(solution)/shard_map/ppermute | solution.py:219
  33.1 2.9 %collective-permute-start.11 = (f32[32,384]{1,0:T(8,128)S(1)}, f32[32,384]{1,0:T(8,128)S(1)}, u32[]{:S(2)}, u32[]{:S(2)}) collective-permute-start(f32[32,384]{1,0:T(8,128)S(1)} %add.63), channel_id=1, source_target_pairs={{0,24},{8,16},{16,8},{24,0},{32,56},{40,48},{48,40},{56,32},{1,25}... | collective-permute-start | bytes 147464 | tf_op jit(solution)/shard_map/ppermute | solution.py:219
  36.0 0.7 collective-permute-start.9
  36.8 1.1 %convolution_convert_fusion = bf16[2,256,512]{2,1,0:T(8,128)(2,1)} fusion(bf16[1,224,256]{2,1,0:T(8,128)(2,1)S(1)} %bitcast.63, bf16[1,224,256]{2,1,0:T(8,128)(2,1)S(1)} %get-tuple-element.6, bf16[112,512]{1,0:T(8,128)(2,1)S(1)} %add.59, bf16[112,512]{1,0:T(8,128)(2,1)S(1)} %add.57), kind=kOutput, calls=%fused_computation | convolution fusion | flops 118276096 | bytes 983040 | tf_op jit(solution)/shard_map/hrc,rk->hck/dot_general | solution.py:282
  37.9 9.5 %all-to-all-start = ((bf16[32,16,512]{2,1,0:T(8,128)(2,1)}), bf16[32,16,512]{2,1,0:T(8,128)(2,1)S(1)}, u32[]{:S(2)}, u32[]{:S(2)}) async-start(bf16[32,16,512]{2,1,0:T(8,128)(2,1)} %bitcast.16), calls=%async_computation | async-start | bytes 1048576 | tf_op jit(solution)/shard_map/all_to_all | solution.py:215
  47.4 1.3 %collective-permute-start.12 = (f32[32,384]{1,0:T(8,128)S(1)}, f32[32,384]{1,0:T(8,128)S(1)}, u32[]{:S(2)}, u32[]{:S(2)}) collective-permute-start(f32[32,384]{1,0:T(8,128)S(1)} %add_add_fusion), channel_id=1, source_target_pairs={{0,64},{64,0},{128,192},{192,128},{1,65},{65,1},{129,193},{193,129... | collective-permute-start | bytes 147464 | tf_op jit(solution)/shard_map/ppermute | solution.py:219
  48.8 2.4 %collective-permute-start.13 = (f32[32,384]{1,0:T(8,128)S(1)}, f32[32,384]{1,0:T(8,128)S(1)}, u32[]{:S(2)}, u32[]{:S(2)}) collective-permute-start(f32[32,384]{1,0:T(8,128)S(1)} %add_add_fusion), channel_id=1, source_target_pairs={{0,128},{64,192},{128,0},{192,64},{1,129},{65,193},{129,1},{193,65... | collective-permute-start | bytes 147464 | tf_op jit(solution)/shard_map/ppermute | solution.py:219
  51.2 0.2 collective-permute-start.14
  51.4 2.0 %collective-permute-done.13 = f32[32,384]{1,0:T(8,128)S(1)} collective-permute-done((f32[32,384]{1,0:T(8,128)S(1)}, f32[32,384]{1,0:T(8,128)S(1)}, u32[]{:S(2)}, u32[]{:S(2)}) %collective-permute-start.13) | collective-permute-done | bytes 49184 | tf_op jit(solution)/shard_map/ppermute | solution.py:219
  53.4 2.3 %collective-permute-done.14 = f32[32,384]{1,0:T(8,128)S(1)} collective-permute-done((f32[32,384]{1,0:T(8,128)S(1)}, f32[32,384]{1,0:T(8,128)S(1)}, u32[]{:S(2)}, u32[]{:S(2)}) %collective-permute-start.14) | collective-permute-done | bytes 49184 | tf_op jit(solution)/shard_map/ppermute | solution.py:219
  55.7 1.1 %collective-permute-start.17 = (f32[128,384]{1,0:T(8,128)S(1)}, f32[128,384]{1,0:T(8,128)S(1)}, u32[]{:S(2)}, u32[]{:S(2)}) collective-permute-start(f32[128,384]{1,0:T(8,128)S(1)} %bitcast.51), channel_id=1, source_target_pairs={{0,6},{2,0},{4,2},{6,4},{1,7},{3,1},{5,3},{7,5},{8,14},{10,8},{12,... | collective-permute-start | bytes 589832 | tf_op jit(solution)/shard_map/ppermute | solution.py:279
  56.8 1.0 collective-permute-start.16
  57.9 0.0 collective-permute-start.15
  57.9 1.0 all-to-all-done
  58.8 0.1 reduce_sum.21
  58.9 0.9 broadcast_in_dim.4
  59.7 6.6 %all-to-all-start.1 = ((bf16[32,16,512]{2,1,0:T(8,128)(2,1)}), bf16[32,16,512]{2,1,0:T(8,128)(2,1)S(1)}, u32[]{:S(2)}, u32[]{:S(2)}) async-start(bf16[32,16,512]{2,1,0:T(8,128)(2,1)} %broadcast_in_dim.4), calls=%async_computation.1 | async-start | bytes 1048576 | tf_op jit(solution)/shard_map/all_to_all | solution.py:215
  66.4 18.4 %shard_map.50 = bf16[512,512]{1,0:T(8,128)(2,1)S(1)} custom-call(s32[1]{0:T(128)} %bitcast.2.where_ref, f32[128,384]{1,0:T(8,128)S(1)} %bitcast.54, f32[128,384]{1,0:T(8,128)S(1)} %collective-permute-done.15.one_ref, f32[128,384]{1,0:T(8,128)S(1)} %collective-permute-done.16.two_ref, f32[128,384]{1,0:T(8,128)S(1)} %collective-permute-done.17.three_ref), custom_call_target="tpu_custom_call" | custom-call | flops 20000000000 | tf_op jit(solution)/shard_map/pallas_call | solution.py:197
  84.8 0.3 convolution_convert_fusion.2
  85.2 0.5 multiply_reduce_fusion
  85.7 2.8 %collective-permute-start.22 = (f32[1,512]{1,0:T(1,128)S(1)}, f32[1,512]{1,0:T(1,128)S(1)}, u32[]{:S(2)}, u32[]{:S(2)}) collective-permute-start(f32[1,512]{1,0:T(1,128)S(1)} %bitcast.58), channel_id=1, source_target_pairs={{0,6},{2,4},{4,2},{6,0},{1,7},{3,5},{5,3},{7,1},{8,14},{10,12},{12... | collective-permute-start | bytes 6152 | tf_op jit(solution)/shard_map/ppermute | solution.py:219
  88.4 0.8 collective-permute-start.21
  89.2 0.3 fusion.2
  89.5 8.6 %collective-permute-start.19 = (bf16[224,256]{1,0:T(8,128)(2,1)S(1)}, bf16[224,256]{1,0:T(8,128)(2,1)S(1)}, u32[]{:S(2)}, u32[]{:S(2)}) collective-permute-start(bf16[224,256]{1,0:T(8,128)(2,1)S(1)} %fusion.8), channel_id=1, source_target_pairs={{0,1},{1,0},{2,3},{3,2},{4,5},{5,4},{6,7},{7,6},{8,9},{9,8},{10,11... | collective-permute-start | bytes 344072 | tf_op jit(solution)/shard_map/ppermute | solution.py:219
  98.2 0.3 fusion
  98.6 3.6 %collective-permute-start.23 = (bf16[224,256]{1,0:T(8,128)(2,1)S(1)}, bf16[224,256]{1,0:T(8,128)(2,1)S(1)}, u32[]{:S(2)}, u32[]{:S(2)}) collective-permute-start(bf16[224,256]{1,0:T(8,128)(2,1)S(1)} %fusion.6), channel_id=1, source_target_pairs={{0,1},{1,0},{2,3},{3,2},{4,5},{5,4},{6,7},{7,6},{8,9},{9,8},{10,11... | collective-permute-start | bytes 344072 | tf_op jit(solution)/shard_map/ppermute | solution.py:219
  102.2 0.8 maximum_subtract_fusion
  103.0 0.1 collective-permute-done.23
  103.2 0.7 pad_maximum_fusion.1
  (42 shorter events, 0.5 us)
Async XLA Ops:
  0.6 1.3 %copy-start = (bf16[2,256,512]{2,1,0:T(8,128)(2,1)S(1)}, bf16[2,256,512]{2,1,0:T(8,128)(2,1)}, u32[]{:S(2)}) copy-start(bf16[2,256,512]{2,1,0:T(8,128)(2,1)} %param.5) | copy-start | bytes 1572868
  2.2 4.4 %collective-permute-start = (bf16[224,512]{1,0:T(8,128)(2,1)S(1)}, bf16[224,512]{1,0:T(8,128)(2,1)S(1)}, u32[]{:S(2)}, u32[]{:S(2)}) collective-permute-start(bf16[224,512]{1,0:T(8,128)(2,1)S(1)} %dynamic-slice_bitcast_fusion), channel_id=1, source_target_pairs={{0,1},{1,0},{2,3},{3,2},{4,5},{5,4},{6,7},{7,6},{8,9},{9,8},{10,11... | collective-permute-start | bytes 688136 | tf_op jit(solution)/shard_map/ppermute | solution.py:219
  6.7 5.7 %collective-permute-start.3 = (bf16[112,512]{1,0:T(8,128)(2,1)S(1)}, bf16[112,512]{1,0:T(8,128)(2,1)S(1)}, u32[]{:S(2)}, u32[]{:S(2)}) collective-permute-start(bf16[112,512]{1,0:T(8,128)(2,1)S(1)} %get-tuple-element.10), channel_id=1, source_target_pairs={{0,6},{2,4},{4,2},{6,0},{1,7},{3,5},{5,3},{7,1},{8,14},{10,12},{12... | collective-permute-start | bytes 344072 | tf_op jit(solution)/shard_map/ppermute | solution.py:219
  7.8 4.6 %collective-permute-start.1 = (bf16[112,512]{1,0:T(8,128)(2,1)S(1)}, bf16[112,512]{1,0:T(8,128)(2,1)S(1)}, u32[]{:S(2)}, u32[]{:S(2)}) collective-permute-start(bf16[112,512]{1,0:T(8,128)(2,1)S(1)} %get-tuple-element.11), channel_id=1, source_target_pairs={{0,2},{2,0},{4,6},{6,4},{1,3},{3,1},{5,7},{7,5},{8,10},{10,8},{12,... | collective-permute-start | bytes 344072 | tf_op jit(solution)/shard_map/ppermute | solution.py:219
  12.4 3.7 %collective-permute-start.4 = (bf16[112,512]{1,0:T(8,128)(2,1)S(1)}, bf16[112,512]{1,0:T(8,128)(2,1)S(1)}, u32[]{:S(2)}, u32[]{:S(2)}) collective-permute-start(bf16[112,512]{1,0:T(8,128)(2,1)S(1)} %get-tuple-element.8), channel_id=1, source_target_pairs={{0,2},{2,0},{4,6},{6,4},{1,3},{3,1},{5,7},{7,5},{8,10},{10,8},{12,... | collective-permute-start | bytes 344072 | tf_op jit(solution)/shard_map/ppermute | solution.py:219
  12.5 4.9 %collective-permute-start.2 = (bf16[112,512]{1,0:T(8,128)(2,1)S(1)}, bf16[112,512]{1,0:T(8,128)(2,1)S(1)}, u32[]{:S(2)}, u32[]{:S(2)}) collective-permute-start(bf16[112,512]{1,0:T(8,128)(2,1)S(1)} %get-tuple-element.9), channel_id=1, source_target_pairs={{0,6},{2,4},{4,2},{6,0},{1,7},{3,5},{5,3},{7,1},{8,14},{10,12},{12... | collective-permute-start | bytes 344072 | tf_op jit(solution)/shard_map/ppermute | solution.py:219
  18.0 6.6 %collective-permute-start.7 = (f32[32,384]{1,0:T(8,128)S(1)}, f32[32,384]{1,0:T(8,128)S(1)}, u32[]{:S(2)}, u32[]{:S(2)}) collective-permute-start(f32[32,384]{1,0:T(8,128)S(1)} %get-tuple-element.14), channel_id=1, source_target_pairs={{0,192},{64,128},{128,64},{192,0},{1,193},{65,129},{129,65},{193,1... | collective-permute-start | bytes 147464 | tf_op jit(solution)/shard_map/ppermute | solution.py:219
  20.1 4.6 %collective-permute-start.6 = (f32[32,384]{1,0:T(8,128)S(1)}, f32[32,384]{1,0:T(8,128)S(1)}, u32[]{:S(2)}, u32[]{:S(2)}) collective-permute-start(f32[32,384]{1,0:T(8,128)S(1)} %get-tuple-element.15), channel_id=1, source_target_pairs={{0,128},{64,192},{128,0},{192,64},{1,129},{65,193},{129,1},{193,65... | collective-permute-start | bytes 147464 | tf_op jit(solution)/shard_map/ppermute | solution.py:219
  20.6 4.0 %collective-permute-start.5 = (f32[32,384]{1,0:T(8,128)S(1)}, f32[32,384]{1,0:T(8,128)S(1)}, u32[]{:S(2)}, u32[]{:S(2)}) collective-permute-start(f32[32,384]{1,0:T(8,128)S(1)} %get-tuple-element.16), channel_id=1, source_target_pairs={{0,64},{64,0},{128,192},{192,128},{1,65},{65,1},{129,193},{193,129... | collective-permute-start | bytes 147464 | tf_op jit(solution)/shard_map/ppermute | solution.py:219
  21.4 15.4 %collective-permute-start.18 = (bf16[224,256]{1,0:T(8,128)(2,1)S(1)}, bf16[224,256]{1,0:T(8,128)(2,1)S(1)}, u32[]{:S(2)}, u32[]{:S(2)}) collective-permute-start(bf16[224,256]{1,0:T(8,128)(2,1)S(1)} %get-tuple-element.7), channel_id=1, source_target_pairs={{0,1},{1,0},{2,3},{3,2},{4,5},{5,4},{6,7},{7,6},{8,9},{9,8},{10,11... | collective-permute-start | bytes 344072 | tf_op jit(solution)/shard_map/ppermute | solution.py:219
  24.7 8.4 %collective-permute-start.8 = (f32[32,384]{1,0:T(8,128)S(1)}, f32[32,384]{1,0:T(8,128)S(1)}, u32[]{:S(2)}, u32[]{:S(2)}) collective-permute-start(f32[32,384]{1,0:T(8,128)S(1)} %fusion.20), channel_id=1, source_target_pairs={{0,32},{8,40},{16,48},{24,56},{32,0},{40,8},{48,16},{56,24},{1,33}... | collective-permute-start | bytes 147464 | tf_op jit(solution)/shard_map/ppermute | solution.py:219
  33.1 14.3 %collective-permute-start.11 = (f32[32,384]{1,0:T(8,128)S(1)}, f32[32,384]{1,0:T(8,128)S(1)}, u32[]{:S(2)}, u32[]{:S(2)}) collective-permute-start(f32[32,384]{1,0:T(8,128)S(1)} %add.63), channel_id=1, source_target_pairs={{0,24},{8,16},{16,8},{24,0},{32,56},{40,48},{48,40},{56,32},{1,25}... | collective-permute-start | bytes 147464 | tf_op jit(solution)/shard_map/ppermute | solution.py:219
  36.0 11.4 %collective-permute-start.10 = (f32[32,384]{1,0:T(8,128)S(1)}, f32[32,384]{1,0:T(8,128)S(1)}, u32[]{:S(2)}, u32[]{:S(2)}) collective-permute-start(f32[32,384]{1,0:T(8,128)S(1)} %add.63), channel_id=1, source_target_pairs={{0,16},{8,24},{16,0},{24,8},{32,48},{40,56},{48,32},{56,40},{1,17}... | collective-permute-start | bytes 147464 | tf_op jit(solution)/shard_map/ppermute | solution.py:219
  36.0 11.4 %collective-permute-start.9 = (f32[32,384]{1,0:T(8,128)S(1)}, f32[32,384]{1,0:T(8,128)S(1)}, u32[]{:S(2)}, u32[]{:S(2)}) collective-permute-start(f32[32,384]{1,0:T(8,128)S(1)} %add.63), channel_id=1, source_target_pairs={{0,8},{8,0},{16,24},{24,16},{32,40},{40,32},{48,56},{56,48},{1,9},... | collective-permute-start | bytes 147464 | tf_op jit(solution)/shard_map/ppermute | solution.py:219
  37.9 20.9 %all-to-all-start = ((bf16[32,16,512]{2,1,0:T(8,128)(2,1)}), bf16[32,16,512]{2,1,0:T(8,128)(2,1)S(1)}, u32[]{:S(2)}, u32[]{:S(2)}) async-start(bf16[32,16,512]{2,1,0:T(8,128)(2,1)} %bitcast.16), calls=%async_computation | async-start | bytes 1048576 | tf_op jit(solution)/shard_map/all_to_all | solution.py:215
  47.4 3.9 %collective-permute-start.12 = (f32[32,384]{1,0:T(8,128)S(1)}, f32[32,384]{1,0:T(8,128)S(1)}, u32[]{:S(2)}, u32[]{:S(2)}) collective-permute-start(f32[32,384]{1,0:T(8,128)S(1)} %add_add_fusion), channel_id=1, source_target_pairs={{0,64},{64,0},{128,192},{192,128},{1,65},{65,1},{129,193},{193,129... | collective-permute-start | bytes 147464 | tf_op jit(solution)/shard_map/ppermute | solution.py:219
  48.8 4.6 %collective-permute-start.13 = (f32[32,384]{1,0:T(8,128)S(1)}, f32[32,384]{1,0:T(8,128)S(1)}, u32[]{:S(2)}, u32[]{:S(2)}) collective-permute-start(f32[32,384]{1,0:T(8,128)S(1)} %add_add_fusion), channel_id=1, source_target_pairs={{0,128},{64,192},{128,0},{192,64},{1,129},{65,193},{129,1},{193,65... | collective-permute-start | bytes 147464 | tf_op jit(solution)/shard_map/ppermute | solution.py:219
  51.2 4.5 %collective-permute-start.14 = (f32[32,384]{1,0:T(8,128)S(1)}, f32[32,384]{1,0:T(8,128)S(1)}, u32[]{:S(2)}, u32[]{:S(2)}) collective-permute-start(f32[32,384]{1,0:T(8,128)S(1)} %add_add_fusion), channel_id=1, source_target_pairs={{0,192},{64,128},{128,64},{192,0},{1,193},{65,129},{129,65},{193,1... | collective-permute-start | bytes 147464 | tf_op jit(solution)/shard_map/ppermute | solution.py:219
  55.7 10.6 %collective-permute-start.17 = (f32[128,384]{1,0:T(8,128)S(1)}, f32[128,384]{1,0:T(8,128)S(1)}, u32[]{:S(2)}, u32[]{:S(2)}) collective-permute-start(f32[128,384]{1,0:T(8,128)S(1)} %bitcast.51), channel_id=1, source_target_pairs={{0,6},{2,0},{4,2},{6,4},{1,7},{3,1},{5,3},{7,5},{8,14},{10,8},{12,... | collective-permute-start | bytes 589832 | tf_op jit(solution)/shard_map/ppermute | solution.py:279
  56.8 9.5 %collective-permute-start.16 = (f32[128,384]{1,0:T(8,128)S(1)}, f32[128,384]{1,0:T(8,128)S(1)}, u32[]{:S(2)}, u32[]{:S(2)}) collective-permute-start(f32[128,384]{1,0:T(8,128)S(1)} %bitcast.52), channel_id=1, source_target_pairs={{0,4},{2,6},{4,0},{6,2},{1,5},{3,7},{5,1},{7,3},{8,12},{10,14},{12... | collective-permute-start | bytes 589832 | tf_op jit(solution)/shard_map/ppermute | solution.py:279
  57.9 8.5 %collective-permute-start.15 = (f32[128,384]{1,0:T(8,128)S(1)}, f32[128,384]{1,0:T(8,128)S(1)}, u32[]{:S(2)}, u32[]{:S(2)}) collective-permute-start(f32[128,384]{1,0:T(8,128)S(1)} %bitcast.53), channel_id=1, source_target_pairs={{0,2},{2,4},{4,6},{6,0},{1,3},{3,5},{5,7},{7,1},{8,10},{10,12},{12... | collective-permute-start | bytes 589832 | tf_op jit(solution)/shard_map/ppermute | solution.py:279
  59.7 25.4 %all-to-all-start.1 = ((bf16[32,16,512]{2,1,0:T(8,128)(2,1)}), bf16[32,16,512]{2,1,0:T(8,128)(2,1)S(1)}, u32[]{:S(2)}, u32[]{:S(2)}) async-start(bf16[32,16,512]{2,1,0:T(8,128)(2,1)} %broadcast_in_dim.4), calls=%async_computation.1 | async-start | bytes 1048576 | tf_op jit(solution)/shard_map/all_to_all | solution.py:215
  85.7 12.5 %collective-permute-start.22 = (f32[1,512]{1,0:T(1,128)S(1)}, f32[1,512]{1,0:T(1,128)S(1)}, u32[]{:S(2)}, u32[]{:S(2)}) collective-permute-start(f32[1,512]{1,0:T(1,128)S(1)} %bitcast.58), channel_id=1, source_target_pairs={{0,6},{2,4},{4,2},{6,0},{1,7},{3,5},{5,3},{7,1},{8,14},{10,12},{12... | collective-permute-start | bytes 6152 | tf_op jit(solution)/shard_map/ppermute | solution.py:219
  88.4 9.8 %collective-permute-start.21 = (f32[1,512]{1,0:T(1,128)S(1)}, f32[1,512]{1,0:T(1,128)S(1)}, u32[]{:S(2)}, u32[]{:S(2)}) collective-permute-start(f32[1,512]{1,0:T(1,128)S(1)} %bitcast.59), channel_id=1, source_target_pairs={{0,4},{2,6},{4,0},{6,2},{1,5},{3,7},{5,1},{7,3},{8,12},{10,14},{12... | collective-permute-start | bytes 6152 | tf_op jit(solution)/shard_map/ppermute | solution.py:219
  89.2 9.0 %collective-permute-start.20 = (f32[1,512]{1,0:T(1,128)S(1)}, f32[1,512]{1,0:T(1,128)S(1)}, u32[]{:S(2)}, u32[]{:S(2)}) collective-permute-start(f32[1,512]{1,0:T(1,128)S(1)} %bitcast.60), channel_id=1, source_target_pairs={{0,2},{2,0},{4,6},{6,4},{1,3},{3,1},{5,7},{7,5},{8,10},{10,8},{12,... | collective-permute-start | bytes 6152 | tf_op jit(solution)/shard_map/ppermute | solution.py:219
  89.5 12.6 %collective-permute-start.19 = (bf16[224,256]{1,0:T(8,128)(2,1)S(1)}, bf16[224,256]{1,0:T(8,128)(2,1)S(1)}, u32[]{:S(2)}, u32[]{:S(2)}) collective-permute-start(bf16[224,256]{1,0:T(8,128)(2,1)S(1)} %fusion.8), channel_id=1, source_target_pairs={{0,1},{1,0},{2,3},{3,2},{4,5},{5,4},{6,7},{7,6},{8,9},{9,8},{10,11... | collective-permute-start | bytes 344072 | tf_op jit(solution)/shard_map/ppermute | solution.py:219
  98.6 4.5 %collective-permute-start.23 = (bf16[224,256]{1,0:T(8,128)(2,1)S(1)}, bf16[224,256]{1,0:T(8,128)(2,1)S(1)}, u32[]{:S(2)}, u32[]{:S(2)}) collective-permute-start(bf16[224,256]{1,0:T(8,128)(2,1)S(1)} %fusion.6), channel_id=1, source_target_pairs={{0,1},{1,0},{2,3},{3,2},{4,5},{5,4},{6,7},{7,6},{8,9},{9,8},{10,11... | collective-permute-start | bytes 344072 | tf_op jit(solution)/shard_map/ppermute | solution.py:219

commit v6 on v5

--- a/solution.py
+++ b/solution.py
@@ -18,6 +18,7 @@
 BLOCKS = RANK // BLOCK
 PANELS = BLOCK // PANEL
 KEPT = 3
+AHEAD = 4
 X_SIZE = 4
 Z_SIZE = 8
 
@@ -49,22 +50,22 @@
         root_a = lax.rsqrt(a)
         ratio = b * (root_a * root_a)
         root_c = lax.rsqrt(c - b * ratio)
-        left_m = jnp.where(first, -1.0, jnp.where(second, 0.0, left))
-        right_m = jnp.where(first, 0.0, jnp.where(second, -1.0, right))
+        left = jnp.where(first, -1.0, jnp.where(second, 0.0, left))
+        right = jnp.where(first, 0.0, jnp.where(second, -1.0, right))
+        alpha, beta = left * c - right * b, right * a - left * b
         for k in range(PANEL):
             if k in (j, j + 1):
                 continue
             top, low = row_of(cols[k], j), row_of(cols[k], j + 1)
-            rest = jnp.where(both, 0.0, cols[k])
-            cols[k] = rest - inv * (left_m * (c * top - b * low) + right_m * (a * low - b * top))
+            cols[k] = jnp.where(both, 0.0, cols[k]) - inv * (alpha * top + beta * low)
             if k < j:
                 factor[k] = jnp.where(
                     first, top * root_a, jnp.where(second, (low - ratio * top) * root_c, factor[k])
                 )
         factor[j] = jnp.where(first, root_a, jnp.where(second, -(ratio * root_c), factor[j]))
         factor[j + 1] = jnp.where(second, root_c, factor[j + 1])
-        cols[j] = inv * (right_m * b - left_m * c)
-        cols[j + 1] = inv * (left_m * b - right_m * a)
+        cols[j] = -(inv * alpha)
+        cols[j + 1] = -(inv * beta)
     return cols, factor
 
 
@@ -84,7 +85,7 @@
         if k + 1 < PANELS:
             down = [lanes_of(groups[k + 1], base + j) for j in range(PANEL)]
             block = []
-            for m in range(base + PANEL, base + 2 * PANEL):
+            for m in range(base + PANEL, base + PANEL + AHEAD):
                 column = combine(full, lanes_of(groups[k], m))
                 block.append(lanes_of(groups[k + 1], m) - combine(down, column))
             solved = combine(full, panel)
@@ -93,6 +94,8 @@
                 old = groups[i]
                 change = added([lanes_of(old, base + j) * rows[j] for j in range(PANEL)])
                 groups[i] = jnp.where(inside, 0.0, old) - change
+            for m in range(base + PANEL + AHEAD, base + 2 * PANEL):
+                block.append(lanes_of(groups[k + 1], m))
         groups[k] = jnp.where(lane <= row + base, combine(factor, panel), 0.0)
         if k < len(tasks):
             tasks[k]()

time: 104 us -> 104 us (level)
  no operation moved by 1% of the time
where the time goes in v6:
time: 104 us
  starting transfers between devices  61.1 us (59%)
  Pallas kernels  18.4 us (18%)
  waiting for transfers between devices  16 us (15%)
  other arithmetic  3.39 us (3%)
  matrix products  3.09 us (3%)
    ppermute x21, starting transfers between devices, swap(): lax.ppermute(value, axis, [(i, i ^ mask) for i in range(SIZES[axis])])  42.8 us
    pallas_call x1, Pallas kernels, inverse_factor(): pl.pallas_call(factor_kernel, out_shape=jax.ShapeDtypeStruct((RANK, RANK)...  18.4 us
    all_to_all x2, starting transfers between devices, spread(): return lax.all_to_all(chunks, axis, split_axis=0, concat_axis=0, tiled=True)  16.1 us
    ppermute x21, waiting for transfers between devices, swap(): lax.ppermute(value, axis, [(i, i ^ mask) for i in range(SIZES[axis])])  15 us
    ppermute x3, starting transfers between devices, local(): lax.ppermute(slab, 'y', [(i, (i + step) % BLOCKS) for i in range(BLOCKS)])  2.12 us
  transfers between devices with their start and end apart: 26, of which 9 were waited for; matrix products, arithmetic and copies ran while one was open for 4% of the time, Pallas kernels for 18%

profile of v6, /device:TPU:1, one launch (start us, length us, event | category | flops | bytes accessed | tf_op | source)
XLA Modules:
  0.0 103.8 jit_solution(7431683190418814390)
XLA Ops:
  0.6 0.0 copy-start
  0.7 1.2 %convert_add_fusion = f32[2,224,256]{2,1,0:T(8,128)S(1)} fusion(f32[2,224,256]{2,1,0:T(8,128)} %param.3, bf16[2,224,256]{2,1,0:T(8,128)(2,1)} %param.4), kind=kLoop, calls=%fused_computation.10 | loop fusion | flops 229376 | bytes 1146880 | tf_op jit(solution)/shard_map/add | solution.py:253
  1.9 0.1 copy-done
  1.9 0.3 convolution_convert_fusion.1
  2.2 3.3 %collective-permute-start = (bf16[224,512]{1,0:T(8,128)(2,1)S(1)}, bf16[224,512]{1,0:T(8,128)(2,1)S(1)}, u32[]{:S(2)}, u32[]{:S(2)}) collective-permute-start(bf16[224,512]{1,0:T(8,128)(2,1)S(1)} %dynamic-slice_bitcast_fusion), channel_id=1, source_target_pairs={{0,1},{1,0},{2,3},{3,2},{4,5},{5,4},{6,7},{7,6},{8,9},{9,8},{10,11... | collective-permute-start | bytes 688136 | tf_op jit(solution)/shard_map/ppermute | solution.py:222
  5.6 1.1 %collective-permute-done = bf16[224,512]{1,0:T(8,128)(2,1)S(1)} collective-permute-done((bf16[224,512]{1,0:T(8,128)(2,1)S(1)}, bf16[224,512]{1,0:T(8,128)(2,1)S(1)}, u32[]{:S(2)}, u32[]{:S(2)}) %collective-permute-start) | collective-permute-done | bytes 229408 | tf_op jit(solution)/shard_map/ppermute | solution.py:222
  6.7 1.1 %collective-permute-start.3 = (bf16[112,512]{1,0:T(8,128)(2,1)S(1)}, bf16[112,512]{1,0:T(8,128)(2,1)S(1)}, u32[]{:S(2)}, u32[]{:S(2)}) collective-permute-start(bf16[112,512]{1,0:T(8,128)(2,1)S(1)} %get-tuple-element.10), channel_id=1, source_target_pairs={{0,6},{2,4},{4,2},{6,0},{1,7},{3,5},{5,3},{7,1},{8,14},{10,12},{12... | collective-permute-start | bytes 344072 | tf_op jit(solution)/shard_map/ppermute | solution.py:222
  7.8 4.6 %collective-permute-done.3 = bf16[112,512]{1,0:T(8,128)(2,1)S(1)} collective-permute-done((bf16[112,512]{1,0:T(8,128)(2,1)S(1)}, bf16[112,512]{1,0:T(8,128)(2,1)S(1)}, u32[]{:S(2)}, u32[]{:S(2)}) %collective-permute-start.3) | collective-permute-done | bytes 114720 | tf_op jit(solution)/shard_map/ppermute | solution.py:222
  12.4 0.1 collective-permute-start.4
  12.5 1.5 %collective-permute-start.2 = (bf16[112,512]{1,0:T(8,128)(2,1)S(1)}, bf16[112,512]{1,0:T(8,128)(2,1)S(1)}, u32[]{:S(2)}, u32[]{:S(2)}) collective-permute-start(bf16[112,512]{1,0:T(8,128)(2,1)S(1)} %get-tuple-element.9), channel_id=1, source_target_pairs={{0,6},{2,4},{4,2},{6,0},{1,7},{3,5},{5,3},{7,1},{8,14},{10,12},{12... | collective-permute-start | bytes 344072 | tf_op jit(solution)/shard_map/ppermute | solution.py:222
  14.0 2.2 %collective-permute-done.4 = bf16[112,512]{1,0:T(8,128)(2,1)S(1)} collective-permute-done((bf16[112,512]{1,0:T(8,128)(2,1)S(1)}, bf16[112,512]{1,0:T(8,128)(2,1)S(1)}, u32[]{:S(2)}, u32[]{:S(2)}) %collective-permute-start.4) | collective-permute-done | bytes 114720 | tf_op jit(solution)/shard_map/ppermute | solution.py:222
  16.2 1.3 %collective-permute-done.2 = bf16[112,512]{1,0:T(8,128)(2,1)S(1)} collective-permute-done((bf16[112,512]{1,0:T(8,128)(2,1)S(1)}, bf16[112,512]{1,0:T(8,128)(2,1)S(1)}, u32[]{:S(2)}, u32[]{:S(2)}) %collective-permute-start.2) | collective-permute-done | bytes 114720 | tf_op jit(solution)/shard_map/ppermute | solution.py:222
  17.5 0.2 fusion.14
  17.8 0.2 fusion.18
  18.0 2.1 %collective-permute-start.7 = (f32[32,384]{1,0:T(8,128)S(1)}, f32[32,384]{1,0:T(8,128)S(1)}, u32[]{:S(2)}, u32[]{:S(2)}) collective-permute-start(f32[32,384]{1,0:T(8,128)S(1)} %get-tuple-element.14), channel_id=1, source_target_pairs={{0,192},{64,128},{128,64},{192,0},{1,193},{65,129},{129,65},{193,1... | collective-permute-start | bytes 147464 | tf_op jit(solution)/shard_map/ppermute | solution.py:222
  20.1 0.5 collective-permute-start.6
  20.6 0.7 collective-permute-start.5
  21.4 3.3 %collective-permute-start.18 = (bf16[224,256]{1,0:T(8,128)(2,1)S(1)}, bf16[224,256]{1,0:T(8,128)(2,1)S(1)}, u32[]{:S(2)}, u32[]{:S(2)}) collective-permute-start(bf16[224,256]{1,0:T(8,128)(2,1)S(1)} %get-tuple-element.7), channel_id=1, source_target_pairs={{0,1},{1,0},{2,3},{3,2},{4,5},{5,4},{6,7},{7,6},{8,9},{9,8},{10,11... | collective-permute-start | bytes 344072 | tf_op jit(solution)/shard_map/ppermute | solution.py:222
  24.7 7.0 %collective-permute-start.8 = (f32[32,384]{1,0:T(8,128)S(1)}, f32[32,384]{1,0:T(8,128)S(1)}, u32[]{:S(2)}, u32[]{:S(2)}) collective-permute-start(f32[32,384]{1,0:T(8,128)S(1)} %fusion.20), channel_id=1, source_target_pairs={{0,32},{8,40},{16,48},{24,56},{32,0},{40,8},{48,16},{56,24},{1,33}... | collective-permute-start | bytes 147464 | tf_op jit(solution)/shard_map/ppermute | solution.py:222
  31.6 1.5 %collective-permute-done.8 = f32[32,384]{1,0:T(8,128)S(1)} collective-permute-done((f32[32,384]{1,0:T(8,128)S(1)}, f32[32,384]{1,0:T(8,128)S(1)}, u32[]{:S(2)}, u32[]{:S(2)}) %collective-permute-start.8) | collective-permute-done | bytes 49184 | tf_op jit(solution)/shard_map/ppermute | solution.py:222
  33.1 2.9 %collective-permute-start.11 = (f32[32,384]{1,0:T(8,128)S(1)}, f32[32,384]{1,0:T(8,128)S(1)}, u32[]{:S(2)}, u32[]{:S(2)}) collective-permute-start(f32[32,384]{1,0:T(8,128)S(1)} %add.63), channel_id=1, source_target_pairs={{0,24},{8,16},{16,8},{24,0},{32,56},{40,48},{48,40},{56,32},{1,25}... | collective-permute-start | bytes 147464 | tf_op jit(solution)/shard_map/ppermute | solution.py:222
  36.0 0.7 collective-permute-start.9
  36.8 1.1 %convolution_convert_fusion = bf16[2,256,512]{2,1,0:T(8,128)(2,1)} fusion(bf16[1,224,256]{2,1,0:T(8,128)(2,1)S(1)} %bitcast.63, bf16[1,224,256]{2,1,0:T(8,128)(2,1)S(1)} %get-tuple-element.6, bf16[112,512]{1,0:T(8,128)(2,1)S(1)} %add.59, bf16[112,512]{1,0:T(8,128)(2,1)S(1)} %add.57), kind=kOutput, calls=%fused_computation | convolution fusion | flops 118276096 | bytes 983040 | tf_op jit(solution)/shard_map/hrc,rk->hck/dot_general | solution.py:285
  37.9 9.5 %all-to-all-start = ((bf16[32,16,512]{2,1,0:T(8,128)(2,1)}), bf16[32,16,512]{2,1,0:T(8,128)(2,1)S(1)}, u32[]{:S(2)}, u32[]{:S(2)}) async-start(bf16[32,16,512]{2,1,0:T(8,128)(2,1)} %bitcast.16), calls=%async_computation | async-start | bytes 1048576 | tf_op jit(solution)/shard_map/all_to_all | solution.py:218
  47.4 1.3 %collective-permute-start.12 = (f32[32,384]{1,0:T(8,128)S(1)}, f32[32,384]{1,0:T(8,128)S(1)}, u32[]{:S(2)}, u32[]{:S(2)}) collective-permute-start(f32[32,384]{1,0:T(8,128)S(1)} %add_add_fusion), channel_id=1, source_target_pairs={{0,64},{64,0},{128,192},{192,128},{1,65},{65,1},{129,193},{193,129... | collective-permute-start | bytes 147464 | tf_op jit(solution)/shard_map/ppermute | solution.py:222
  48.8 2.4 %collective-permute-start.13 = (f32[32,384]{1,0:T(8,128)S(1)}, f32[32,384]{1,0:T(8,128)S(1)}, u32[]{:S(2)}, u32[]{:S(2)}) collective-permute-start(f32[32,384]{1,0:T(8,128)S(1)} %add_add_fusion), channel_id=1, source_target_pairs={{0,128},{64,192},{128,0},{192,64},{1,129},{65,193},{129,1},{193,65... | collective-permute-start | bytes 147464 | tf_op jit(solution)/shard_map/ppermute | solution.py:222
  51.2 0.2 collective-permute-start.14
  51.4 2.0 %collective-permute-done.13 = f32[32,384]{1,0:T(8,128)S(1)} collective-permute-done((f32[32,384]{1,0:T(8,128)S(1)}, f32[32,384]{1,0:T(8,128)S(1)}, u32[]{:S(2)}, u32[]{:S(2)}) %collective-permute-start.13) | collective-permute-done | bytes 49184 | tf_op jit(solution)/shard_map/ppermute | solution.py:222
  53.4 2.3 %collective-permute-done.14 = f32[32,384]{1,0:T(8,128)S(1)} collective-permute-done((f32[32,384]{1,0:T(8,128)S(1)}, f32[32,384]{1,0:T(8,128)S(1)}, u32[]{:S(2)}, u32[]{:S(2)}) %collective-permute-start.14) | collective-permute-done | bytes 49184 | tf_op jit(solution)/shard_map/ppermute | solution.py:222
  55.7 1.1 %collective-permute-start.17 = (f32[128,384]{1,0:T(8,128)S(1)}, f32[128,384]{1,0:T(8,128)S(1)}, u32[]{:S(2)}, u32[]{:S(2)}) collective-permute-start(f32[128,384]{1,0:T(8,128)S(1)} %bitcast.51), channel_id=1, source_target_pairs={{0,6},{2,0},{4,2},{6,4},{1,7},{3,1},{5,3},{7,5},{8,14},{10,8},{12,... | collective-permute-start | bytes 589832 | tf_op jit(solution)/shard_map/ppermute | solution.py:282
  56.8 1.0 collective-permute-start.16
  57.9 0.0 collective-permute-start.15
  57.9 1.0 all-to-all-done
  58.8 0.1 reduce_sum.21
  58.9 0.9 broadcast_in_dim.4
  59.7 6.6 %all-to-all-start.1 = ((bf16[32,16,512]{2,1,0:T(8,128)(2,1)}), bf16[32,16,512]{2,1,0:T(8,128)(2,1)S(1)}, u32[]{:S(2)}, u32[]{:S(2)}) async-start(bf16[32,16,512]{2,1,0:T(8,128)(2,1)} %broadcast_in_dim.4), calls=%async_computation.1 | async-start | bytes 1048576 | tf_op jit(solution)/shard_map/all_to_all | solution.py:218
  66.4 18.4 %shard_map.50 = bf16[512,512]{1,0:T(8,128)(2,1)S(1)} custom-call(s32[1]{0:T(128)} %bitcast.2.where_ref, f32[128,384]{1,0:T(8,128)S(1)} %bitcast.54, f32[128,384]{1,0:T(8,128)S(1)} %collective-permute-done.15.one_ref, f32[128,384]{1,0:T(8,128)S(1)} %collective-permute-done.16.two_ref, f32[128,384]{1,0:T(8,128)S(1)} %collective-permute-done.17.three_ref), custom_call_target="tpu_custom_call" | custom-call | flops 20000000000 | tf_op jit(solution)/shard_map/pallas_call | solution.py:200
  84.8 0.3 convolution_convert_fusion.2
  85.1 0.5 multiply_reduce_fusion
  85.6 2.8 %collective-permute-start.22 = (f32[1,512]{1,0:T(1,128)S(1)}, f32[1,512]{1,0:T(1,128)S(1)}, u32[]{:S(2)}, u32[]{:S(2)}) collective-permute-start(f32[1,512]{1,0:T(1,128)S(1)} %bitcast.58), channel_id=1, source_target_pairs={{0,6},{2,4},{4,2},{6,0},{1,7},{3,5},{5,3},{7,1},{8,14},{10,12},{12... | collective-permute-start | bytes 6152 | tf_op jit(solution)/shard_map/ppermute | solution.py:222
  88.4 0.8 collective-permute-start.21
  89.2 0.3 fusion.2
  89.5 8.6 %collective-permute-start.19 = (bf16[224,256]{1,0:T(8,128)(2,1)S(1)}, bf16[224,256]{1,0:T(8,128)(2,1)S(1)}, u32[]{:S(2)}, u32[]{:S(2)}) collective-permute-start(bf16[224,256]{1,0:T(8,128)(2,1)S(1)} %fusion.8), channel_id=1, source_target_pairs={{0,1},{1,0},{2,3},{3,2},{4,5},{5,4},{6,7},{7,6},{8,9},{9,8},{10,11... | collective-permute-start | bytes 344072 | tf_op jit(solution)/shard_map/ppermute | solution.py:222
  98.2 0.3 fusion
  98.6 3.6 %collective-permute-start.23 = (bf16[224,256]{1,0:T(8,128)(2,1)S(1)}, bf16[224,256]{1,0:T(8,128)(2,1)S(1)}, u32[]{:S(2)}, u32[]{:S(2)}) collective-permute-start(bf16[224,256]{1,0:T(8,128)(2,1)S(1)} %fusion.6), channel_id=1, source_target_pairs={{0,1},{1,0},{2,3},{3,2},{4,5},{5,4},{6,7},{7,6},{8,9},{9,8},{10,11... | collective-permute-start | bytes 344072 | tf_op jit(solution)/shard_map/ppermute | solution.py:222
  102.2 0.8 maximum_subtract_fusion
  103.0 0.1 collective-permute-done.23
  103.1 0.7 pad_maximum_fusion.1
  (42 shorter events, 0.5 us)
Async XLA Ops:
  0.6 1.3 %copy-start = (bf16[2,256,512]{2,1,0:T(8,128)(2,1)S(1)}, bf16[2,256,512]{2,1,0:T(8,128)(2,1)}, u32[]{:S(2)}) copy-start(bf16[2,256,512]{2,1,0:T(8,128)(2,1)} %param.5) | copy-start | bytes 1572868
  2.2 4.4 %collective-permute-start = (bf16[224,512]{1,0:T(8,128)(2,1)S(1)}, bf16[224,512]{1,0:T(8,128)(2,1)S(1)}, u32[]{:S(2)}, u32[]{:S(2)}) collective-permute-start(bf16[224,512]{1,0:T(8,128)(2,1)S(1)} %dynamic-slice_bitcast_fusion), channel_id=1, source_target_pairs={{0,1},{1,0},{2,3},{3,2},{4,5},{5,4},{6,7},{7,6},{8,9},{9,8},{10,11... | collective-permute-start | bytes 688136 | tf_op jit(solution)/shard_map/ppermute | solution.py:222
  6.7 5.7 %collective-permute-start.3 = (bf16[112,512]{1,0:T(8,128)(2,1)S(1)}, bf16[112,512]{1,0:T(8,128)(2,1)S(1)}, u32[]{:S(2)}, u32[]{:S(2)}) collective-permute-start(bf16[112,512]{1,0:T(8,128)(2,1)S(1)} %get-tuple-element.10), channel_id=1, source_target_pairs={{0,6},{2,4},{4,2},{6,0},{1,7},{3,5},{5,3},{7,1},{8,14},{10,12},{12... | collective-permute-start | bytes 344072 | tf_op jit(solution)/shard_map/ppermute | solution.py:222
  7.8 4.6 %collective-permute-start.1 = (bf16[112,512]{1,0:T(8,128)(2,1)S(1)}, bf16[112,512]{1,0:T(8,128)(2,1)S(1)}, u32[]{:S(2)}, u32[]{:S(2)}) collective-permute-start(bf16[112,512]{1,0:T(8,128)(2,1)S(1)} %get-tuple-element.11), channel_id=1, source_target_pairs={{0,2},{2,0},{4,6},{6,4},{1,3},{3,1},{5,7},{7,5},{8,10},{10,8},{12,... | collective-permute-start | bytes 344072 | tf_op jit(solution)/shard_map/ppermute | solution.py:222
  12.4 3.7 %collective-permute-start.4 = (bf16[112,512]{1,0:T(8,128)(2,1)S(1)}, bf16[112,512]{1,0:T(8,128)(2,1)S(1)}, u32[]{:S(2)}, u32[]{:S(2)}) collective-permute-start(bf16[112,512]{1,0:T(8,128)(2,1)S(1)} %get-tuple-element.8), channel_id=1, source_target_pairs={{0,2},{2,0},{4,6},{6,4},{1,3},{3,1},{5,7},{7,5},{8,10},{10,8},{12,... | collective-permute-start | bytes 344072 | tf_op jit(solution)/shard_map/ppermute | solution.py:222
  12.5 4.9 %collective-permute-start.2 = (bf16[112,512]{1,0:T(8,128)(2,1)S(1)}, bf16[112,512]{1,0:T(8,128)(2,1)S(1)}, u32[]{:S(2)}, u32[]{:S(2)}) collective-permute-start(bf16[112,512]{1,0:T(8,128)(2,1)S(1)} %get-tuple-element.9), channel_id=1, source_target_pairs={{0,6},{2,4},{4,2},{6,0},{1,7},{3,5},{5,3},{7,1},{8,14},{10,12},{12... | collective-permute-start | bytes 344072 | tf_op jit(solution)/shard_map/ppermute | solution.py:222
  18.0 6.6 %collective-permute-start.7 = (f32[32,384]{1,0:T(8,128)S(1)}, f32[32,384]{1,0:T(8,128)S(1)}, u32[]{:S(2)}, u32[]{:S(2)}) collective-permute-start(f32[32,384]{1,0:T(8,128)S(1)} %get-tuple-element.14), channel_id=1, source_target_pairs={{0,192},{64,128},{128,64},{192,0},{1,193},{65,129},{129,65},{193,1... | collective-permute-start | bytes 147464 | tf_op jit(solution)/shard_map/ppermute | solution.py:222
  20.1 4.6 %collective-permute-start.6 = (f32[32,384]{1,0:T(8,128)S(1)}, f32[32,384]{1,0:T(8,128)S(1)}, u32[]{:S(2)}, u32[]{:S(2)}) collective-permute-start(f32[32,384]{1,0:T(8,128)S(1)} %get-tuple-element.15), channel_id=1, source_target_pairs={{0,128},{64,192},{128,0},{192,64},{1,129},{65,193},{129,1},{193,65... | collective-permute-start | bytes 147464 | tf_op jit(solution)/shard_map/ppermute | solution.py:222
  20.6 4.0 %collective-permute-start.5 = (f32[32,384]{1,0:T(8,128)S(1)}, f32[32,384]{1,0:T(8,128)S(1)}, u32[]{:S(2)}, u32[]{:S(2)}) collective-permute-start(f32[32,384]{1,0:T(8,128)S(1)} %get-tuple-element.16), channel_id=1, source_target_pairs={{0,64},{64,0},{128,192},{192,128},{1,65},{65,1},{129,193},{193,129... | collective-permute-start | bytes 147464 | tf_op jit(solution)/shard_map/ppermute | solution.py:222
  21.4 15.4 %collective-permute-start.18 = (bf16[224,256]{1,0:T(8,128)(2,1)S(1)}, bf16[224,256]{1,0:T(8,128)(2,1)S(1)}, u32[]{:S(2)}, u32[]{:S(2)}) collective-permute-start(bf16[224,256]{1,0:T(8,128)(2,1)S(1)} %get-tuple-element.7), channel_id=1, source_target_pairs={{0,1},{1,0},{2,3},{3,2},{4,5},{5,4},{6,7},{7,6},{8,9},{9,8},{10,11... | collective-permute-start | bytes 344072 | tf_op jit(solution)/shard_map/ppermute | solution.py:222
  24.7 8.4 %collective-permute-start.8 = (f32[32,384]{1,0:T(8,128)S(1)}, f32[32,384]{1,0:T(8,128)S(1)}, u32[]{:S(2)}, u32[]{:S(2)}) collective-permute-start(f32[32,384]{1,0:T(8,128)S(1)} %fusion.20), channel_id=1, source_target_pairs={{0,32},{8,40},{16,48},{24,56},{32,0},{40,8},{48,16},{56,24},{1,33}... | collective-permute-start | bytes 147464 | tf_op jit(solution)/shard_map/ppermute | solution.py:222
  33.1 14.3 %collective-permute-start.11 = (f32[32,384]{1,0:T(8,128)S(1)}, f32[32,384]{1,0:T(8,128)S(1)}, u32[]{:S(2)}, u32[]{:S(2)}) collective-permute-start(f32[32,384]{1,0:T(8,128)S(1)} %add.63), channel_id=1, source_target_pairs={{0,24},{8,16},{16,8},{24,0},{32,56},{40,48},{48,40},{56,32},{1,25}... | collective-permute-start | bytes 147464 | tf_op jit(solution)/shard_map/ppermute | solution.py:222
  36.0 11.4 %collective-permute-start.10 = (f32[32,384]{1,0:T(8,128)S(1)}, f32[32,384]{1,0:T(8,128)S(1)}, u32[]{:S(2)}, u32[]{:S(2)}) collective-permute-start(f32[32,384]{1,0:T(8,128)S(1)} %add.63), channel_id=1, source_target_pairs={{0,16},{8,24},{16,0},{24,8},{32,48},{40,56},{48,32},{56,40},{1,17}... | collective-permute-start | bytes 147464 | tf_op jit(solution)/shard_map/ppermute | solution.py:222
  36.0 11.4 %collective-permute-start.9 = (f32[32,384]{1,0:T(8,128)S(1)}, f32[32,384]{1,0:T(8,128)S(1)}, u32[]{:S(2)}, u32[]{:S(2)}) collective-permute-start(f32[32,384]{1,0:T(8,128)S(1)} %add.63), channel_id=1, source_target_pairs={{0,8},{8,0},{16,24},{24,16},{32,40},{40,32},{48,56},{56,48},{1,9},... | collective-permute-start | bytes 147464 | tf_op jit(solution)/shard_map/ppermute | solution.py:222
  37.9 20.9 %all-to-all-start = ((bf16[32,16,512]{2,1,0:T(8,128)(2,1)}), bf16[32,16,512]{2,1,0:T(8,128)(2,1)S(1)}, u32[]{:S(2)}, u32[]{:S(2)}) async-start(bf16[32,16,512]{2,1,0:T(8,128)(2,1)} %bitcast.16), calls=%async_computation | async-start | bytes 1048576 | tf_op jit(solution)/shard_map/all_to_all | solution.py:218
  47.4 3.9 %collective-permute-start.12 = (f32[32,384]{1,0:T(8,128)S(1)}, f32[32,384]{1,0:T(8,128)S(1)}, u32[]{:S(2)}, u32[]{:S(2)}) collective-permute-start(f32[32,384]{1,0:T(8,128)S(1)} %add_add_fusion), channel_id=1, source_target_pairs={{0,64},{64,0},{128,192},{192,128},{1,65},{65,1},{129,193},{193,129... | collective-permute-start | bytes 147464 | tf_op jit(solution)/shard_map/ppermute | solution.py:222
  48.8 4.6 %collective-permute-start.13 = (f32[32,384]{1,0:T(8,128)S(1)}, f32[32,384]{1,0:T(8,128)S(1)}, u32[]{:S(2)}, u32[]{:S(2)}) collective-permute-start(f32[32,384]{1,0:T(8,128)S(1)} %add_add_fusion), channel_id=1, source_target_pairs={{0,128},{64,192},{128,0},{192,64},{1,129},{65,193},{129,1},{193,65... | collective-permute-start | bytes 147464 | tf_op jit(solution)/shard_map/ppermute | solution.py:222
  51.2 4.5 %collective-permute-start.14 = (f32[32,384]{1,0:T(8,128)S(1)}, f32[32,384]{1,0:T(8,128)S(1)}, u32[]{:S(2)}, u32[]{:S(2)}) collective-permute-start(f32[32,384]{1,0:T(8,128)S(1)} %add_add_fusion), channel_id=1, source_target_pairs={{0,192},{64,128},{128,64},{192,0},{1,193},{65,129},{129,65},{193,1... | collective-permute-start | bytes 147464 | tf_op jit(solution)/shard_map/ppermute | solution.py:222
  55.7 10.6 %collective-permute-start.17 = (f32[128,384]{1,0:T(8,128)S(1)}, f32[128,384]{1,0:T(8,128)S(1)}, u32[]{:S(2)}, u32[]{:S(2)}) collective-permute-start(f32[128,384]{1,0:T(8,128)S(1)} %bitcast.51), channel_id=1, source_target_pairs={{0,6},{2,0},{4,2},{6,4},{1,7},{3,1},{5,3},{7,5},{8,14},{10,8},{12,... | collective-permute-start | bytes 589832 | tf_op jit(solution)/shard_map/ppermute | solution.py:282
  56.8 9.5 %collective-permute-start.16 = (f32[128,384]{1,0:T(8,128)S(1)}, f32[128,384]{1,0:T(8,128)S(1)}, u32[]{:S(2)}, u32[]{:S(2)}) collective-permute-start(f32[128,384]{1,0:T(8,128)S(1)} %bitcast.52), channel_id=1, source_target_pairs={{0,4},{2,6},{4,0},{6,2},{1,5},{3,7},{5,1},{7,3},{8,12},{10,14},{12... | collective-permute-start | bytes 589832 | tf_op jit(solution)/shard_map/ppermute | solution.py:282
  57.9 8.5 %collective-permute-start.15 = (f32[128,384]{1,0:T(8,128)S(1)}, f32[128,384]{1,0:T(8,128)S(1)}, u32[]{:S(2)}, u32[]{:S(2)}) collective-permute-start(f32[128,384]{1,0:T(8,128)S(1)} %bitcast.53), channel_id=1, source_target_pairs={{0,2},{2,4},{4,6},{6,0},{1,3},{3,5},{5,7},{7,1},{8,10},{10,12},{12... | collective-permute-start | bytes 589832 | tf_op jit(solution)/shard_map/ppermute | solution.py:282
  59.7 25.4 %all-to-all-start.1 = ((bf16[32,16,512]{2,1,0:T(8,128)(2,1)}), bf16[32,16,512]{2,1,0:T(8,128)(2,1)S(1)}, u32[]{:S(2)}, u32[]{:S(2)}) async-start(bf16[32,16,512]{2,1,0:T(8,128)(2,1)} %broadcast_in_dim.4), calls=%async_computation.1 | async-start | bytes 1048576 | tf_op jit(solution)/shard_map/all_to_all | solution.py:218
  85.6 12.5 %collective-permute-start.22 = (f32[1,512]{1,0:T(1,128)S(1)}, f32[1,512]{1,0:T(1,128)S(1)}, u32[]{:S(2)}, u32[]{:S(2)}) collective-permute-start(f32[1,512]{1,0:T(1,128)S(1)} %bitcast.58), channel_id=1, source_target_pairs={{0,6},{2,4},{4,2},{6,0},{1,7},{3,5},{5,3},{7,1},{8,14},{10,12},{12... | collective-permute-start | bytes 6152 | tf_op jit(solution)/shard_map/ppermute | solution.py:222
  88.4 9.8 %collective-permute-start.21 = (f32[1,512]{1,0:T(1,128)S(1)}, f32[1,512]{1,0:T(1,128)S(1)}, u32[]{:S(2)}, u32[]{:S(2)}) collective-permute-start(f32[1,512]{1,0:T(1,128)S(1)} %bitcast.59), channel_id=1, source_target_pairs={{0,4},{2,6},{4,0},{6,2},{1,5},{3,7},{5,1},{7,3},{8,12},{10,14},{12... | collective-permute-start | bytes 6152 | tf_op jit(solution)/shard_map/ppermute | solution.py:222
  89.2 9.0 %collective-permute-start.20 = (f32[1,512]{1,0:T(1,128)S(1)}, f32[1,512]{1,0:T(1,128)S(1)}, u32[]{:S(2)}, u32[]{:S(2)}) collective-permute-start(f32[1,512]{1,0:T(1,128)S(1)} %bitcast.60), channel_id=1, source_target_pairs={{0,2},{2,0},{4,6},{6,4},{1,3},{3,1},{5,7},{7,5},{8,10},{10,8},{12,... | collective-permute-start | bytes 6152 | tf_op jit(solution)/shard_map/ppermute | solution.py:222
  89.5 12.6 %collective-permute-start.19 = (bf16[224,256]{1,0:T(8,128)(2,1)S(1)}, bf16[224,256]{1,0:T(8,128)(2,1)S(1)}, u32[]{:S(2)}, u32[]{:S(2)}) collective-permute-start(bf16[224,256]{1,0:T(8,128)(2,1)S(1)} %fusion.8), channel_id=1, source_target_pairs={{0,1},{1,0},{2,3},{3,2},{4,5},{5,4},{6,7},{7,6},{8,9},{9,8},{10,11... | collective-permute-start | bytes 344072 | tf_op jit(solution)/shard_map/ppermute | solution.py:222
  98.6 4.5 %collective-permute-start.23 = (bf16[224,256]{1,0:T(8,128)(2,1)S(1)}, bf16[224,256]{1,0:T(8,128)(2,1)S(1)}, u32[]{:S(2)}, u32[]{:S(2)}) collective-permute-start(bf16[224,256]{1,0:T(8,128)(2,1)S(1)} %fusion.6), channel_id=1, source_target_pairs={{0,1},{1,0},{2,3},{3,2},{4,5},{5,4},{6,7},{7,6},{8,9},{9,8},{10,11... | collective-permute-start | bytes 344072 | tf_op jit(solution)/shard_map/ppermute | solution.py:222

commit v7 on v6

--- a/solution.py
+++ b/solution.py
@@ -18,7 +18,7 @@
 BLOCKS = RANK // BLOCK
 PANELS = BLOCK // PANEL
 KEPT = 3
-AHEAD = 4
+AHEAD = 8
 X_SIZE = 4
 Z_SIZE = 8
 
@@ -44,7 +44,8 @@
         first, second = row == j, row == j + 1
         both = first | second
         left, right = cols[j], cols[j + 1]
-        a, b, c = row_of(left, j), row_of(right, j), row_of(right, j + 1)
+        if j == 0:
+            a, b, c = row_of(left, 0), row_of(right, 0), row_of(right, 1)
         root = lax.rsqrt(a * c - b * b)
         inv = root * root
         root_a = lax.rsqrt(a)
@@ -53,6 +54,13 @@
         left = jnp.where(first, -1.0, jnp.where(second, 0.0, left))
         right = jnp.where(first, 0.0, jnp.where(second, -1.0, right))
         alpha, beta = left * c - right * b, right * a - left * b
+
+        def entry(i, k):
+            change = row_of(alpha, i) * row_of(cols[k], j) + row_of(beta, i) * row_of(cols[k], j + 1)
+            return row_of(cols[k], i) - inv * change
+
+        if j + 2 < PANEL:
+            a, b, c = entry(j + 2, j + 2), entry(j + 2, j + 3), entry(j + 3, j + 3)
         for k in range(PANEL):
             if k in (j, j + 1):
                 continue

time: 104 us -> 104 us (level)
  transfers between devices with their start and end apart: 26 -> 26, of which waited for: 9 -> 9; matrix products, arithmetic and copies ran while one was open for 4% -> 4% of each run, Pallas kernels for 18% -> 17%
where the time goes in v7:
time: 104 us; the launch traced here: 103 us
  starting transfers between devices  61.1 us (59%)
  Pallas kernels  17.8 us (17%)
  waiting for transfers between devices  16 us (15%)
  other arithmetic  3.39 us (3%)
  matrix products  3.09 us (3%)
    ppermute x21, starting transfers between devices, swap(): lax.ppermute(value, axis, [(i, i ^ mask) for i in range(SIZES[axis])])  42.8 us
    pallas_call x1, Pallas kernels, inverse_factor(): pl.pallas_call(factor_kernel, out_shape=jax.ShapeDtypeStruct((RANK, RANK)...  17.8 us
    all_to_all x2, starting transfers between devices, spread(): return lax.all_to_all(chunks, axis, split_axis=0, concat_axis=0, tiled=True)  16.1 us
    ppermute x21, waiting for transfers between devices, swap(): lax.ppermute(value, axis, [(i, i ^ mask) for i in range(SIZES[axis])])  15 us
    ppermute x3, starting transfers between devices, local(): lax.ppermute(slab, 'y', [(i, (i + step) % BLOCKS) for i in range(BLOCKS)])  2.12 us
  transfers between devices with their start and end apart: 26, of which 9 were waited for; matrix products, arithmetic and copies ran while one was open for 4% of the time, Pallas kernels for 17%

profile of v7, /device:TPU:1, one launch (start us, length us, event | category | flops | bytes accessed | tf_op | source)
XLA Modules:
  0.0 103.3 jit_solution(729905266488613650)
XLA Ops:
  0.6 0.0 copy-start
  0.7 1.2 %convert_add_fusion = f32[2,224,256]{2,1,0:T(8,128)S(1)} fusion(f32[2,224,256]{2,1,0:T(8,128)} %param.3, bf16[2,224,256]{2,1,0:T(8,128)(2,1)} %param.4), kind=kLoop, calls=%fused_computation.10 | loop fusion | flops 229376 | bytes 1146880 | tf_op jit(solution)/shard_map/add | solution.py:261
  1.9 0.1 copy-done
  1.9 0.3 convolution_convert_fusion.1
  2.2 3.3 %collective-permute-start = (bf16[224,512]{1,0:T(8,128)(2,1)S(1)}, bf16[224,512]{1,0:T(8,128)(2,1)S(1)}, u32[]{:S(2)}, u32[]{:S(2)}) collective-permute-start(bf16[224,512]{1,0:T(8,128)(2,1)S(1)} %dynamic-slice_bitcast_fusion), channel_id=1, source_target_pairs={{0,1},{1,0},{2,3},{3,2},{4,5},{5,4},{6,7},{7,6},{8,9},{9,8},{10,11... | collective-permute-start | bytes 688136 | tf_op jit(solution)/shard_map/ppermute | solution.py:230
  5.6 1.1 %collective-permute-done = bf16[224,512]{1,0:T(8,128)(2,1)S(1)} collective-permute-done((bf16[224,512]{1,0:T(8,128)(2,1)S(1)}, bf16[224,512]{1,0:T(8,128)(2,1)S(1)}, u32[]{:S(2)}, u32[]{:S(2)}) %collective-permute-start) | collective-permute-done | bytes 229408 | tf_op jit(solution)/shard_map/ppermute | solution.py:230
  6.7 1.1 %collective-permute-start.3 = (bf16[112,512]{1,0:T(8,128)(2,1)S(1)}, bf16[112,512]{1,0:T(8,128)(2,1)S(1)}, u32[]{:S(2)}, u32[]{:S(2)}) collective-permute-start(bf16[112,512]{1,0:T(8,128)(2,1)S(1)} %get-tuple-element.10), channel_id=1, source_target_pairs={{0,6},{2,4},{4,2},{6,0},{1,7},{3,5},{5,3},{7,1},{8,14},{10,12},{12... | collective-permute-start | bytes 344072 | tf_op jit(solution)/shard_map/ppermute | solution.py:230
  7.8 4.6 %collective-permute-done.3 = bf16[112,512]{1,0:T(8,128)(2,1)S(1)} collective-permute-done((bf16[112,512]{1,0:T(8,128)(2,1)S(1)}, bf16[112,512]{1,0:T(8,128)(2,1)S(1)}, u32[]{:S(2)}, u32[]{:S(2)}) %collective-permute-start.3) | collective-permute-done | bytes 114720 | tf_op jit(solution)/shard_map/ppermute | solution.py:230
  12.4 0.1 collective-permute-start.4
  12.5 1.5 %collective-permute-start.2 = (bf16[112,512]{1,0:T(8,128)(2,1)S(1)}, bf16[112,512]{1,0:T(8,128)(2,1)S(1)}, u32[]{:S(2)}, u32[]{:S(2)}) collective-permute-start(bf16[112,512]{1,0:T(8,128)(2,1)S(1)} %get-tuple-element.9), channel_id=1, source_target_pairs={{0,6},{2,4},{4,2},{6,0},{1,7},{3,5},{5,3},{7,1},{8,14},{10,12},{12... | collective-permute-start | bytes 344072 | tf_op jit(solution)/shard_map/ppermute | solution.py:230
  14.0 2.2 %collective-permute-done.4 = bf16[112,512]{1,0:T(8,128)(2,1)S(1)} collective-permute-done((bf16[112,512]{1,0:T(8,128)(2,1)S(1)}, bf16[112,512]{1,0:T(8,128)(2,1)S(1)}, u32[]{:S(2)}, u32[]{:S(2)}) %collective-permute-start.4) | collective-permute-done | bytes 114720 | tf_op jit(solution)/shard_map/ppermute | solution.py:230
  16.2 1.3 %collective-permute-done.2 = bf16[112,512]{1,0:T(8,128)(2,1)S(1)} collective-permute-done((bf16[112,512]{1,0:T(8,128)(2,1)S(1)}, bf16[112,512]{1,0:T(8,128)(2,1)S(1)}, u32[]{:S(2)}, u32[]{:S(2)}) %collective-permute-start.2) | collective-permute-done | bytes 114720 | tf_op jit(solution)/shard_map/ppermute | solution.py:230
  17.5 0.2 fusion.14
  17.8 0.2 fusion.18
  18.0 2.1 %collective-permute-start.7 = (f32[32,384]{1,0:T(8,128)S(1)}, f32[32,384]{1,0:T(8,128)S(1)}, u32[]{:S(2)}, u32[]{:S(2)}) collective-permute-start(f32[32,384]{1,0:T(8,128)S(1)} %get-tuple-element.14), channel_id=1, source_target_pairs={{0,192},{64,128},{128,64},{192,0},{1,193},{65,129},{129,65},{193,1... | collective-permute-start | bytes 147464 | tf_op jit(solution)/shard_map/ppermute | solution.py:230
  20.1 0.5 collective-permute-start.6
  20.6 0.7 collective-permute-start.5
  21.4 3.3 %collective-permute-start.18 = (bf16[224,256]{1,0:T(8,128)(2,1)S(1)}, bf16[224,256]{1,0:T(8,128)(2,1)S(1)}, u32[]{:S(2)}, u32[]{:S(2)}) collective-permute-start(bf16[224,256]{1,0:T(8,128)(2,1)S(1)} %get-tuple-element.7), channel_id=1, source_target_pairs={{0,1},{1,0},{2,3},{3,2},{4,5},{5,4},{6,7},{7,6},{8,9},{9,8},{10,11... | collective-permute-start | bytes 344072 | tf_op jit(solution)/shard_map/ppermute | solution.py:230
  24.7 7.0 %collective-permute-start.8 = (f32[32,384]{1,0:T(8,128)S(1)}, f32[32,384]{1,0:T(8,128)S(1)}, u32[]{:S(2)}, u32[]{:S(2)}) collective-permute-start(f32[32,384]{1,0:T(8,128)S(1)} %fusion.20), channel_id=1, source_target_pairs={{0,32},{8,40},{16,48},{24,56},{32,0},{40,8},{48,16},{56,24},{1,33}... | collective-permute-start | bytes 147464 | tf_op jit(solution)/shard_map/ppermute | solution.py:230
  31.6 1.5 %collective-permute-done.8 = f32[32,384]{1,0:T(8,128)S(1)} collective-permute-done((f32[32,384]{1,0:T(8,128)S(1)}, f32[32,384]{1,0:T(8,128)S(1)}, u32[]{:S(2)}, u32[]{:S(2)}) %collective-permute-start.8) | collective-permute-done | bytes 49184 | tf_op jit(solution)/shard_map/ppermute | solution.py:230
  33.1 2.9 %collective-permute-start.11 = (f32[32,384]{1,0:T(8,128)S(1)}, f32[32,384]{1,0:T(8,128)S(1)}, u32[]{:S(2)}, u32[]{:S(2)}) collective-permute-start(f32[32,384]{1,0:T(8,128)S(1)} %add.63), channel_id=1, source_target_pairs={{0,24},{8,16},{16,8},{24,0},{32,56},{40,48},{48,40},{56,32},{1,25}... | collective-permute-start | bytes 147464 | tf_op jit(solution)/shard_map/ppermute | solution.py:230
  36.0 0.7 collective-permute-start.9
  36.8 1.1 %convolution_convert_fusion = bf16[2,256,512]{2,1,0:T(8,128)(2,1)} fusion(bf16[1,224,256]{2,1,0:T(8,128)(2,1)S(1)} %bitcast.63, bf16[1,224,256]{2,1,0:T(8,128)(2,1)S(1)} %get-tuple-element.6, bf16[112,512]{1,0:T(8,128)(2,1)S(1)} %add.59, bf16[112,512]{1,0:T(8,128)(2,1)S(1)} %add.57), kind=kOutput, calls=%fused_computation | convolution fusion | flops 118276096 | bytes 983040 | tf_op jit(solution)/shard_map/hrc,rk->hck/dot_general | solution.py:293
  37.9 9.5 %all-to-all-start = ((bf16[32,16,512]{2,1,0:T(8,128)(2,1)}), bf16[32,16,512]{2,1,0:T(8,128)(2,1)S(1)}, u32[]{:S(2)}, u32[]{:S(2)}) async-start(bf16[32,16,512]{2,1,0:T(8,128)(2,1)} %bitcast.16), calls=%async_computation | async-start | bytes 1048576 | tf_op jit(solution)/shard_map/all_to_all | solution.py:226
  47.4 1.3 %collective-permute-start.12 = (f32[32,384]{1,0:T(8,128)S(1)}, f32[32,384]{1,0:T(8,128)S(1)}, u32[]{:S(2)}, u32[]{:S(2)}) collective-permute-start(f32[32,384]{1,0:T(8,128)S(1)} %add_add_fusion), channel_id=1, source_target_pairs={{0,64},{64,0},{128,192},{192,128},{1,65},{65,1},{129,193},{193,129... | collective-permute-start | bytes 147464 | tf_op jit(solution)/shard_map/ppermute | solution.py:230
  48.8 2.4 %collective-permute-start.13 = (f32[32,384]{1,0:T(8,128)S(1)}, f32[32,384]{1,0:T(8,128)S(1)}, u32[]{:S(2)}, u32[]{:S(2)}) collective-permute-start(f32[32,384]{1,0:T(8,128)S(1)} %add_add_fusion), channel_id=1, source_target_pairs={{0,128},{64,192},{128,0},{192,64},{1,129},{65,193},{129,1},{193,65... | collective-permute-start | bytes 147464 | tf_op jit(solution)/shard_map/ppermute | solution.py:230
  51.2 0.2 collective-permute-start.14
  51.4 2.0 %collective-permute-done.13 = f32[32,384]{1,0:T(8,128)S(1)} collective-permute-done((f32[32,384]{1,0:T(8,128)S(1)}, f32[32,384]{1,0:T(8,128)S(1)}, u32[]{:S(2)}, u32[]{:S(2)}) %collective-permute-start.13) | collective-permute-done | bytes 49184 | tf_op jit(solution)/shard_map/ppermute | solution.py:230
  53.4 2.3 %collective-permute-done.14 = f32[32,384]{1,0:T(8,128)S(1)} collective-permute-done((f32[32,384]{1,0:T(8,128)S(1)}, f32[32,384]{1,0:T(8,128)S(1)}, u32[]{:S(2)}, u32[]{:S(2)}) %collective-permute-start.14) | collective-permute-done | bytes 49184 | tf_op jit(solution)/shard_map/ppermute | solution.py:230
  55.7 1.1 %collective-permute-start.17 = (f32[128,384]{1,0:T(8,128)S(1)}, f32[128,384]{1,0:T(8,128)S(1)}, u32[]{:S(2)}, u32[]{:S(2)}) collective-permute-start(f32[128,384]{1,0:T(8,128)S(1)} %bitcast.51), channel_id=1, source_target_pairs={{0,6},{2,0},{4,2},{6,4},{1,7},{3,1},{5,3},{7,5},{8,14},{10,8},{12,... | collective-permute-start | bytes 589832 | tf_op jit(solution)/shard_map/ppermute | solution.py:290
  56.8 1.0 collective-permute-start.16
  57.9 0.0 collective-permute-start.15
  57.9 1.0 all-to-all-done
  58.8 0.1 reduce_sum.21
  58.9 0.9 broadcast_in_dim.4
  59.7 6.6 %all-to-all-start.1 = ((bf16[32,16,512]{2,1,0:T(8,128)(2,1)}), bf16[32,16,512]{2,1,0:T(8,128)(2,1)S(1)}, u32[]{:S(2)}, u32[]{:S(2)}) async-start(bf16[32,16,512]{2,1,0:T(8,128)(2,1)} %broadcast_in_dim.4), calls=%async_computation.1 | async-start | bytes 1048576 | tf_op jit(solution)/shard_map/all_to_all | solution.py:226
  66.4 17.8 %shard_map.50 = bf16[512,512]{1,0:T(8,128)(2,1)S(1)} custom-call(s32[1]{0:T(128)} %bitcast.2.where_ref, f32[128,384]{1,0:T(8,128)S(1)} %bitcast.54, f32[128,384]{1,0:T(8,128)S(1)} %collective-permute-done.15.one_ref, f32[128,384]{1,0:T(8,128)S(1)} %collective-permute-done.16.two_ref, f32[128,384]{1,0:T(8,128)S(1)} %collective-permute-done.17.three_ref), custom_call_target="tpu_custom_call" | custom-call | flops 20000000000 | tf_op jit(solution)/shard_map/pallas_call | solution.py:208
  84.2 0.3 convolution_convert_fusion.2
  84.6 0.5 multiply_reduce_fusion
  85.0 2.8 %collective-permute-start.22 = (f32[1,512]{1,0:T(1,128)S(1)}, f32[1,512]{1,0:T(1,128)S(1)}, u32[]{:S(2)}, u32[]{:S(2)}) collective-permute-start(f32[1,512]{1,0:T(1,128)S(1)} %bitcast.58), channel_id=1, source_target_pairs={{0,6},{2,4},{4,2},{6,0},{1,7},{3,5},{5,3},{7,1},{8,14},{10,12},{12... | collective-permute-start | bytes 6152 | tf_op jit(solution)/shard_map/ppermute | solution.py:230
  87.8 0.7 collective-permute-start.21
  88.6 0.3 fusion.2
  88.9 8.6 %collective-permute-start.19 = (bf16[224,256]{1,0:T(8,128)(2,1)S(1)}, bf16[224,256]{1,0:T(8,128)(2,1)S(1)}, u32[]{:S(2)}, u32[]{:S(2)}) collective-permute-start(bf16[224,256]{1,0:T(8,128)(2,1)S(1)} %fusion.8), channel_id=1, source_target_pairs={{0,1},{1,0},{2,3},{3,2},{4,5},{5,4},{6,7},{7,6},{8,9},{9,8},{10,11... | collective-permute-start | bytes 344072 | tf_op jit(solution)/shard_map/ppermute | solution.py:230
  97.6 0.3 fusion
  98.0 3.6 %collective-permute-start.23 = (bf16[224,256]{1,0:T(8,128)(2,1)S(1)}, bf16[224,256]{1,0:T(8,128)(2,1)S(1)}, u32[]{:S(2)}, u32[]{:S(2)}) collective-permute-start(bf16[224,256]{1,0:T(8,128)(2,1)S(1)} %fusion.6), channel_id=1, source_target_pairs={{0,1},{1,0},{2,3},{3,2},{4,5},{5,4},{6,7},{7,6},{8,9},{9,8},{10,11... | collective-permute-start | bytes 344072 | tf_op jit(solution)/shard_map/ppermute | solution.py:230
  101.6 0.8 maximum_subtract_fusion
  102.4 0.1 collective-permute-done.23
  102.5 0.7 pad_maximum_fusion.1
  (42 shorter events, 0.5 us)
Async XLA Ops:
  0.6 1.3 %copy-start = (bf16[2,256,512]{2,1,0:T(8,128)(2,1)S(1)}, bf16[2,256,512]{2,1,0:T(8,128)(2,1)}, u32[]{:S(2)}) copy-start(bf16[2,256,512]{2,1,0:T(8,128)(2,1)} %param.5) | copy-start | bytes 1572868
  2.2 4.4 %collective-permute-start = (bf16[224,512]{1,0:T(8,128)(2,1)S(1)}, bf16[224,512]{1,0:T(8,128)(2,1)S(1)}, u32[]{:S(2)}, u32[]{:S(2)}) collective-permute-start(bf16[224,512]{1,0:T(8,128)(2,1)S(1)} %dynamic-slice_bitcast_fusion), channel_id=1, source_target_pairs={{0,1},{1,0},{2,3},{3,2},{4,5},{5,4},{6,7},{7,6},{8,9},{9,8},{10,11... | collective-permute-start | bytes 688136 | tf_op jit(solution)/shard_map/ppermute | solution.py:230
  6.7 5.7 %collective-permute-start.3 = (bf16[112,512]{1,0:T(8,128)(2,1)S(1)}, bf16[112,512]{1,0:T(8,128)(2,1)S(1)}, u32[]{:S(2)}, u32[]{:S(2)}) collective-permute-start(bf16[112,512]{1,0:T(8,128)(2,1)S(1)} %get-tuple-element.10), channel_id=1, source_target_pairs={{0,6},{2,4},{4,2},{6,0},{1,7},{3,5},{5,3},{7,1},{8,14},{10,12},{12... | collective-permute-start | bytes 344072 | tf_op jit(solution)/shard_map/ppermute | solution.py:230
  7.8 4.6 %collective-permute-start.1 = (bf16[112,512]{1,0:T(8,128)(2,1)S(1)}, bf16[112,512]{1,0:T(8,128)(2,1)S(1)}, u32[]{:S(2)}, u32[]{:S(2)}) collective-permute-start(bf16[112,512]{1,0:T(8,128)(2,1)S(1)} %get-tuple-element.11), channel_id=1, source_target_pairs={{0,2},{2,0},{4,6},{6,4},{1,3},{3,1},{5,7},{7,5},{8,10},{10,8},{12,... | collective-permute-start | bytes 344072 | tf_op jit(solution)/shard_map/ppermute | solution.py:230
  12.4 3.7 %collective-permute-start.4 = (bf16[112,512]{1,0:T(8,128)(2,1)S(1)}, bf16[112,512]{1,0:T(8,128)(2,1)S(1)}, u32[]{:S(2)}, u32[]{:S(2)}) collective-permute-start(bf16[112,512]{1,0:T(8,128)(2,1)S(1)} %get-tuple-element.8), channel_id=1, source_target_pairs={{0,2},{2,0},{4,6},{6,4},{1,3},{3,1},{5,7},{7,5},{8,10},{10,8},{12,... | collective-permute-start | bytes 344072 | tf_op jit(solution)/shard_map/ppermute | solution.py:230
  12.5 4.9 %collective-permute-start.2 = (bf16[112,512]{1,0:T(8,128)(2,1)S(1)}, bf16[112,512]{1,0:T(8,128)(2,1)S(1)}, u32[]{:S(2)}, u32[]{:S(2)}) collective-permute-start(bf16[112,512]{1,0:T(8,128)(2,1)S(1)} %get-tuple-element.9), channel_id=1, source_target_pairs={{0,6},{2,4},{4,2},{6,0},{1,7},{3,5},{5,3},{7,1},{8,14},{10,12},{12... | collective-permute-start | bytes 344072 | tf_op jit(solution)/shard_map/ppermute | solution.py:230
  18.0 6.6 %collective-permute-start.7 = (f32[32,384]{1,0:T(8,128)S(1)}, f32[32,384]{1,0:T(8,128)S(1)}, u32[]{:S(2)}, u32[]{:S(2)}) collective-permute-start(f32[32,384]{1,0:T(8,128)S(1)} %get-tuple-element.14), channel_id=1, source_target_pairs={{0,192},{64,128},{128,64},{192,0},{1,193},{65,129},{129,65},{193,1... | collective-permute-start | bytes 147464 | tf_op jit(solution)/shard_map/ppermute | solution.py:230
  20.1 4.6 %collective-permute-start.6 = (f32[32,384]{1,0:T(8,128)S(1)}, f32[32,384]{1,0:T(8,128)S(1)}, u32[]{:S(2)}, u32[]{:S(2)}) collective-permute-start(f32[32,384]{1,0:T(8,128)S(1)} %get-tuple-element.15), channel_id=1, source_target_pairs={{0,128},{64,192},{128,0},{192,64},{1,129},{65,193},{129,1},{193,65... | collective-permute-start | bytes 147464 | tf_op jit(solution)/shard_map/ppermute | solution.py:230
  20.6 4.0 %collective-permute-start.5 = (f32[32,384]{1,0:T(8,128)S(1)}, f32[32,384]{1,0:T(8,128)S(1)}, u32[]{:S(2)}, u32[]{:S(2)}) collective-permute-start(f32[32,384]{1,0:T(8,128)S(1)} %get-tuple-element.16), channel_id=1, source_target_pairs={{0,64},{64,0},{128,192},{192,128},{1,65},{65,1},{129,193},{193,129... | collective-permute-start | bytes 147464 | tf_op jit(solution)/shard_map/ppermute | solution.py:230
  21.4 15.4 %collective-permute-start.18 = (bf16[224,256]{1,0:T(8,128)(2,1)S(1)}, bf16[224,256]{1,0:T(8,128)(2,1)S(1)}, u32[]{:S(2)}, u32[]{:S(2)}) collective-permute-start(bf16[224,256]{1,0:T(8,128)(2,1)S(1)} %get-tuple-element.7), channel_id=1, source_target_pairs={{0,1},{1,0},{2,3},{3,2},{4,5},{5,4},{6,7},{7,6},{8,9},{9,8},{10,11... | collective-permute-start | bytes 344072 | tf_op jit(solution)/shard_map/ppermute | solution.py:230
  24.7 8.4 %collective-permute-start.8 = (f32[32,384]{1,0:T(8,128)S(1)}, f32[32,384]{1,0:T(8,128)S(1)}, u32[]{:S(2)}, u32[]{:S(2)}) collective-permute-start(f32[32,384]{1,0:T(8,128)S(1)} %fusion.20), channel_id=1, source_target_pairs={{0,32},{8,40},{16,48},{24,56},{32,0},{40,8},{48,16},{56,24},{1,33}... | collective-permute-start | bytes 147464 | tf_op jit(solution)/shard_map/ppermute | solution.py:230
  33.1 14.3 %collective-permute-start.11 = (f32[32,384]{1,0:T(8,128)S(1)}, f32[32,384]{1,0:T(8,128)S(1)}, u32[]{:S(2)}, u32[]{:S(2)}) collective-permute-start(f32[32,384]{1,0:T(8,128)S(1)} %add.63), channel_id=1, source_target_pairs={{0,24},{8,16},{16,8},{24,0},{32,56},{40,48},{48,40},{56,32},{1,25}... | collective-permute-start | bytes 147464 | tf_op jit(solution)/shard_map/ppermute | solution.py:230
  36.0 11.4 %collective-permute-start.10 = (f32[32,384]{1,0:T(8,128)S(1)}, f32[32,384]{1,0:T(8,128)S(1)}, u32[]{:S(2)}, u32[]{:S(2)}) collective-permute-start(f32[32,384]{1,0:T(8,128)S(1)} %add.63), channel_id=1, source_target_pairs={{0,16},{8,24},{16,0},{24,8},{32,48},{40,56},{48,32},{56,40},{1,17}... | collective-permute-start | bytes 147464 | tf_op jit(solution)/shard_map/ppermute | solution.py:230
  36.0 11.4 %collective-permute-start.9 = (f32[32,384]{1,0:T(8,128)S(1)}, f32[32,384]{1,0:T(8,128)S(1)}, u32[]{:S(2)}, u32[]{:S(2)}) collective-permute-start(f32[32,384]{1,0:T(8,128)S(1)} %add.63), channel_id=1, source_target_pairs={{0,8},{8,0},{16,24},{24,16},{32,40},{40,32},{48,56},{56,48},{1,9},... | collective-permute-start | bytes 147464 | tf_op jit(solution)/shard_map/ppermute | solution.py:230
  37.9 20.9 %all-to-all-start = ((bf16[32,16,512]{2,1,0:T(8,128)(2,1)}), bf16[32,16,512]{2,1,0:T(8,128)(2,1)S(1)}, u32[]{:S(2)}, u32[]{:S(2)}) async-start(bf16[32,16,512]{2,1,0:T(8,128)(2,1)} %bitcast.16), calls=%async_computation | async-start | bytes 1048576 | tf_op jit(solution)/shard_map/all_to_all | solution.py:226
  47.4 3.9 %collective-permute-start.12 = (f32[32,384]{1,0:T(8,128)S(1)}, f32[32,384]{1,0:T(8,128)S(1)}, u32[]{:S(2)}, u32[]{:S(2)}) collective-permute-start(f32[32,384]{1,0:T(8,128)S(1)} %add_add_fusion), channel_id=1, source_target_pairs={{0,64},{64,0},{128,192},{192,128},{1,65},{65,1},{129,193},{193,129... | collective-permute-start | bytes 147464 | tf_op jit(solution)/shard_map/ppermute | solution.py:230
  48.8 4.6 %collective-permute-start.13 = (f32[32,384]{1,0:T(8,128)S(1)}, f32[32,384]{1,0:T(8,128)S(1)}, u32[]{:S(2)}, u32[]{:S(2)}) collective-permute-start(f32[32,384]{1,0:T(8,128)S(1)} %add_add_fusion), channel_id=1, source_target_pairs={{0,128},{64,192},{128,0},{192,64},{1,129},{65,193},{129,1},{193,65... | collective-permute-start | bytes 147464 | tf_op jit(solution)/shard_map/ppermute | solution.py:230
  51.2 4.5 %collective-permute-start.14 = (f32[32,384]{1,0:T(8,128)S(1)}, f32[32,384]{1,0:T(8,128)S(1)}, u32[]{:S(2)}, u32[]{:S(2)}) collective-permute-start(f32[32,384]{1,0:T(8,128)S(1)} %add_add_fusion), channel_id=1, source_target_pairs={{0,192},{64,128},{128,64},{192,0},{1,193},{65,129},{129,65},{193,1... | collective-permute-start | bytes 147464 | tf_op jit(solution)/shard_map/ppermute | solution.py:230
  55.7 10.6 %collective-permute-start.17 = (f32[128,384]{1,0:T(8,128)S(1)}, f32[128,384]{1,0:T(8,128)S(1)}, u32[]{:S(2)}, u32[]{:S(2)}) collective-permute-start(f32[128,384]{1,0:T(8,128)S(1)} %bitcast.51), channel_id=1, source_target_pairs={{0,6},{2,0},{4,2},{6,4},{1,7},{3,1},{5,3},{7,5},{8,14},{10,8},{12,... | collective-permute-start | bytes 589832 | tf_op jit(solution)/shard_map/ppermute | solution.py:290
  56.8 9.5 %collective-permute-start.16 = (f32[128,384]{1,0:T(8,128)S(1)}, f32[128,384]{1,0:T(8,128)S(1)}, u32[]{:S(2)}, u32[]{:S(2)}) collective-permute-start(f32[128,384]{1,0:T(8,128)S(1)} %bitcast.52), channel_id=1, source_target_pairs={{0,4},{2,6},{4,0},{6,2},{1,5},{3,7},{5,1},{7,3},{8,12},{10,14},{12... | collective-permute-start | bytes 589832 | tf_op jit(solution)/shard_map/ppermute | solution.py:290
  57.9 8.5 %collective-permute-start.15 = (f32[128,384]{1,0:T(8,128)S(1)}, f32[128,384]{1,0:T(8,128)S(1)}, u32[]{:S(2)}, u32[]{:S(2)}) collective-permute-start(f32[128,384]{1,0:T(8,128)S(1)} %bitcast.53), channel_id=1, source_target_pairs={{0,2},{2,4},{4,6},{6,0},{1,3},{3,5},{5,7},{7,1},{8,10},{10,12},{12... | collective-permute-start | bytes 589832 | tf_op jit(solution)/shard_map/ppermute | solution.py:290
  59.7 24.8 %all-to-all-start.1 = ((bf16[32,16,512]{2,1,0:T(8,128)(2,1)}), bf16[32,16,512]{2,1,0:T(8,128)(2,1)S(1)}, u32[]{:S(2)}, u32[]{:S(2)}) async-start(bf16[32,16,512]{2,1,0:T(8,128)(2,1)} %broadcast_in_dim.4), calls=%async_computation.1 | async-start | bytes 1048576 | tf_op jit(solution)/shard_map/all_to_all | solution.py:226
  85.0 12.5 %collective-permute-start.22 = (f32[1,512]{1,0:T(1,128)S(1)}, f32[1,512]{1,0:T(1,128)S(1)}, u32[]{:S(2)}, u32[]{:S(2)}) collective-permute-start(f32[1,512]{1,0:T(1,128)S(1)} %bitcast.58), channel_id=1, source_target_pairs={{0,6},{2,4},{4,2},{6,0},{1,7},{3,5},{5,3},{7,1},{8,14},{10,12},{12... | collective-permute-start | bytes 6152 | tf_op jit(solution)/shard_map/ppermute | solution.py:230
  87.8 9.8 %collective-permute-start.21 = (f32[1,512]{1,0:T(1,128)S(1)}, f32[1,512]{1,0:T(1,128)S(1)}, u32[]{:S(2)}, u32[]{:S(2)}) collective-permute-start(f32[1,512]{1,0:T(1,128)S(1)} %bitcast.59), channel_id=1, source_target_pairs={{0,4},{2,6},{4,0},{6,2},{1,5},{3,7},{5,1},{7,3},{8,12},{10,14},{12... | collective-permute-start | bytes 6152 | tf_op jit(solution)/shard_map/ppermute | solution.py:230
  88.6 9.0 %collective-permute-start.20 = (f32[1,512]{1,0:T(1,128)S(1)}, f32[1,512]{1,0:T(1,128)S(1)}, u32[]{:S(2)}, u32[]{:S(2)}) collective-permute-start(f32[1,512]{1,0:T(1,128)S(1)} %bitcast.60), channel_id=1, source_target_pairs={{0,2},{2,0},{4,6},{6,4},{1,3},{3,1},{5,7},{7,5},{8,10},{10,8},{12,... | collective-permute-start | bytes 6152 | tf_op jit(solution)/shard_map/ppermute | solution.py:230
  88.9 12.6 %collective-permute-start.19 = (bf16[224,256]{1,0:T(8,128)(2,1)S(1)}, bf16[224,256]{1,0:T(8,128)(2,1)S(1)}, u32[]{:S(2)}, u32[]{:S(2)}) collective-permute-start(bf16[224,256]{1,0:T(8,128)(2,1)S(1)} %fusion.8), channel_id=1, source_target_pairs={{0,1},{1,0},{2,3},{3,2},{4,5},{5,4},{6,7},{7,6},{8,9},{9,8},{10,11... | collective-permute-start | bytes 344072 | tf_op jit(solution)/shard_map/ppermute | solution.py:230
  98.0 4.5 %collective-permute-start.23 = (bf16[224,256]{1,0:T(8,128)(2,1)S(1)}, bf16[224,256]{1,0:T(8,128)(2,1)S(1)}, u32[]{:S(2)}, u32[]{:S(2)}) collective-permute-start(bf16[224,256]{1,0:T(8,128)(2,1)S(1)} %fusion.6), channel_id=1, source_target_pairs={{0,1},{1,0},{2,3},{3,2},{4,5},{5,4},{6,7},{7,6},{8,9},{9,8},{10,11... | collective-permute-start | bytes 344072 | tf_op jit(solution)/shard_map/ppermute | solution.py:230

commit v8 on v7

--- a/solution.py
+++ b/solution.py
@@ -37,7 +37,7 @@
     return terms[0]
 
 
-def small_inverse(cols, row):
+def small_inverse(cols, pivots, row):
     cols = list(cols)
     factor = [jnp.zeros((PANEL, BLOCK), jnp.float32) for _ in range(PANEL)]
     for j in range(0, PANEL, 2):
@@ -45,7 +45,7 @@
         both = first | second
         left, right = cols[j], cols[j + 1]
         if j == 0:
-            a, b, c = row_of(left, 0), row_of(right, 0), row_of(right, 1)
+            a, b, c = pivots
         root = lax.rsqrt(a * c - b * b)
         inv = root * root
         root_a = lax.rsqrt(a)
@@ -85,17 +85,26 @@
     row = lax.broadcasted_iota(jnp.int32, (PANEL, BLOCK), 0)
     lane = lax.broadcasted_iota(jnp.int32, (PANEL, BLOCK), 1)
     block = [lanes_of(groups[0], j) for j in range(PANEL)]
+    pivots = row_of(block[0], 0), row_of(block[1], 0), row_of(block[1], 1)
     for k in range(PANELS):
         base = k * PANEL
         inside = (lane >= base) & (lane < base + PANEL)
-        full, factor = small_inverse(block, row)
+        full, factor = small_inverse(block, pivots, row)
         panel = jnp.where(inside, (lane == row + base).astype(jnp.float32), groups[k])
         if k + 1 < PANELS:
             down = [lanes_of(groups[k + 1], base + j) for j in range(PANEL)]
             block = []
+            solved_cols = []
             for m in range(base + PANEL, base + PANEL + AHEAD):
                 column = combine(full, lanes_of(groups[k], m))
+                solved_cols.append(column)
                 block.append(lanes_of(groups[k + 1], m) - combine(down, column))
+
+            def entry(i, m):
+                change = combine([row_of(part, i) for part in down], solved_cols[m])
+                return row_of(lanes_of(groups[k + 1], base + PANEL + m), i) - change
+
+            pivots = entry(0, 0), entry(0, 1), entry(1, 1)
             solved = combine(full, panel)
             rows = [row_of(solved, j) for j in range(PANEL)]
             for i in range(k + 1, PANELS):

time: 104 us -> 105 us (level)
  Pallas kernels: 17.8 us -> 19.1 us
    pallas_call x1, Pallas kernels: 17.8 us -> 19.1 us  [inverse_factor(): pl.pallas_call(factor_kernel, out_shape=jax.ShapeDtypeStruct((RANK, RANK)...]
  transfers between devices with their start and end apart: 26 -> 26, of which waited for: 9 -> 9; matrix products, arithmetic and copies ran while one was open for 4% -> 4% of each run, Pallas kernels for 17% -> 18%
where the time goes in v8:
time: 105 us
  starting transfers between devices  61.1 us (58%)
  Pallas kernels  19.1 us (18%)
  waiting for transfers between devices  16 us (15%)
  other arithmetic  3.39 us (3%)
  matrix products  3.09 us (3%)
    ppermute x21, starting transfers between devices, swap(): lax.ppermute(value, axis, [(i, i ^ mask) for i in range(SIZES[axis])])  42.8 us
    pallas_call x1, Pallas kernels, inverse_factor(): pl.pallas_call(factor_kernel, out_shape=jax.ShapeDtypeStruct((RANK, RANK)...  19.1 us
    all_to_all x2, starting transfers between devices, spread(): return lax.all_to_all(chunks, axis, split_axis=0, concat_axis=0, tiled=True)  16.1 us
    ppermute x21, waiting for transfers between devices, swap(): lax.ppermute(value, axis, [(i, i ^ mask) for i in range(SIZES[axis])])  15 us
    ppermute x3, starting transfers between devices, local(): lax.ppermute(slab, 'y', [(i, (i + step) % BLOCKS) for i in range(BLOCKS)])  2.12 us
  transfers between devices with their start and end apart: 26, of which 9 were waited for; matrix products, arithmetic and copies ran while one was open for 4% of the time, Pallas kernels for 18%

profile of v8, /device:TPU:1, one launch (start us, length us, event | category | flops | bytes accessed | tf_op | source)
XLA Modules:
  0.0 104.6 jit_solution(13813288698304200669)
XLA Ops:
  0.6 0.0 copy-start
  0.7 1.2 %convert_add_fusion = f32[2,224,256]{2,1,0:T(8,128)S(1)} fusion(f32[2,224,256]{2,1,0:T(8,128)} %param.3, bf16[2,224,256]{2,1,0:T(8,128)(2,1)} %param.4), kind=kLoop, calls=%fused_computation.10 | loop fusion | flops 229376 | bytes 1146880 | tf_op jit(solution)/shard_map/add | solution.py:270
  1.9 0.1 copy-done
  1.9 0.3 convolution_convert_fusion.1
  2.2 3.3 %collective-permute-start = (bf16[224,512]{1,0:T(8,128)(2,1)S(1)}, bf16[224,512]{1,0:T(8,128)(2,1)S(1)}, u32[]{:S(2)}, u32[]{:S(2)}) collective-permute-start(bf16[224,512]{1,0:T(8,128)(2,1)S(1)} %dynamic-slice_bitcast_fusion), channel_id=1, source_target_pairs={{0,1},{1,0},{2,3},{3,2},{4,5},{5,4},{6,7},{7,6},{8,9},{9,8},{10,11... | collective-permute-start | bytes 688136 | tf_op jit(solution)/shard_map/ppermute | solution.py:239
  5.6 1.1 %collective-permute-done = bf16[224,512]{1,0:T(8,128)(2,1)S(1)} collective-permute-done((bf16[224,512]{1,0:T(8,128)(2,1)S(1)}, bf16[224,512]{1,0:T(8,128)(2,1)S(1)}, u32[]{:S(2)}, u32[]{:S(2)}) %collective-permute-start) | collective-permute-done | bytes 229408 | tf_op jit(solution)/shard_map/ppermute | solution.py:239
  6.7 1.1 %collective-permute-start.3 = (bf16[112,512]{1,0:T(8,128)(2,1)S(1)}, bf16[112,512]{1,0:T(8,128)(2,1)S(1)}, u32[]{:S(2)}, u32[]{:S(2)}) collective-permute-start(bf16[112,512]{1,0:T(8,128)(2,1)S(1)} %get-tuple-element.10), channel_id=1, source_target_pairs={{0,6},{2,4},{4,2},{6,0},{1,7},{3,5},{5,3},{7,1},{8,14},{10,12},{12... | collective-permute-start | bytes 344072 | tf_op jit(solution)/shard_map/ppermute | solution.py:239
  7.8 4.6 %collective-permute-done.3 = bf16[112,512]{1,0:T(8,128)(2,1)S(1)} collective-permute-done((bf16[112,512]{1,0:T(8,128)(2,1)S(1)}, bf16[112,512]{1,0:T(8,128)(2,1)S(1)}, u32[]{:S(2)}, u32[]{:S(2)}) %collective-permute-start.3) | collective-permute-done | bytes 114720 | tf_op jit(solution)/shard_map/ppermute | solution.py:239
  12.4 0.1 collective-permute-start.4
  12.5 1.5 %collective-permute-start.2 = (bf16[112,512]{1,0:T(8,128)(2,1)S(1)}, bf16[112,512]{1,0:T(8,128)(2,1)S(1)}, u32[]{:S(2)}, u32[]{:S(2)}) collective-permute-start(bf16[112,512]{1,0:T(8,128)(2,1)S(1)} %get-tuple-element.9), channel_id=1, source_target_pairs={{0,6},{2,4},{4,2},{6,0},{1,7},{3,5},{5,3},{7,1},{8,14},{10,12},{12... | collective-permute-start | bytes 344072 | tf_op jit(solution)/shard_map/ppermute | solution.py:239
  14.0 2.2 %collective-permute-done.4 = bf16[112,512]{1,0:T(8,128)(2,1)S(1)} collective-permute-done((bf16[112,512]{1,0:T(8,128)(2,1)S(1)}, bf16[112,512]{1,0:T(8,128)(2,1)S(1)}, u32[]{:S(2)}, u32[]{:S(2)}) %collective-permute-start.4) | collective-permute-done | bytes 114720 | tf_op jit(solution)/shard_map/ppermute | solution.py:239
  16.2 1.3 %collective-permute-done.2 = bf16[112,512]{1,0:T(8,128)(2,1)S(1)} collective-permute-done((bf16[112,512]{1,0:T(8,128)(2,1)S(1)}, bf16[112,512]{1,0:T(8,128)(2,1)S(1)}, u32[]{:S(2)}, u32[]{:S(2)}) %collective-permute-start.2) | collective-permute-done | bytes 114720 | tf_op jit(solution)/shard_map/ppermute | solution.py:239
  17.5 0.2 fusion.14
  17.8 0.2 fusion.18
  18.0 2.1 %collective-permute-start.7 = (f32[32,384]{1,0:T(8,128)S(1)}, f32[32,384]{1,0:T(8,128)S(1)}, u32[]{:S(2)}, u32[]{:S(2)}) collective-permute-start(f32[32,384]{1,0:T(8,128)S(1)} %get-tuple-element.14), channel_id=1, source_target_pairs={{0,192},{64,128},{128,64},{192,0},{1,193},{65,129},{129,65},{193,1... | collective-permute-start | bytes 147464 | tf_op jit(solution)/shard_map/ppermute | solution.py:239
  20.1 0.5 collective-permute-start.6
  20.6 0.7 collective-permute-start.5
  21.4 3.3 %collective-permute-start.18 = (bf16[224,256]{1,0:T(8,128)(2,1)S(1)}, bf16[224,256]{1,0:T(8,128)(2,1)S(1)}, u32[]{:S(2)}, u32[]{:S(2)}) collective-permute-start(bf16[224,256]{1,0:T(8,128)(2,1)S(1)} %get-tuple-element.7), channel_id=1, source_target_pairs={{0,1},{1,0},{2,3},{3,2},{4,5},{5,4},{6,7},{7,6},{8,9},{9,8},{10,11... | collective-permute-start | bytes 344072 | tf_op jit(solution)/shard_map/ppermute | solution.py:239
  24.7 7.0 %collective-permute-start.8 = (f32[32,384]{1,0:T(8,128)S(1)}, f32[32,384]{1,0:T(8,128)S(1)}, u32[]{:S(2)}, u32[]{:S(2)}) collective-permute-start(f32[32,384]{1,0:T(8,128)S(1)} %fusion.20), channel_id=1, source_target_pairs={{0,32},{8,40},{16,48},{24,56},{32,0},{40,8},{48,16},{56,24},{1,33}... | collective-permute-start | bytes 147464 | tf_op jit(solution)/shard_map/ppermute | solution.py:239
  31.6 1.5 %collective-permute-done.8 = f32[32,384]{1,0:T(8,128)S(1)} collective-permute-done((f32[32,384]{1,0:T(8,128)S(1)}, f32[32,384]{1,0:T(8,128)S(1)}, u32[]{:S(2)}, u32[]{:S(2)}) %collective-permute-start.8) | collective-permute-done | bytes 49184 | tf_op jit(solution)/shard_map/ppermute | solution.py:239
  33.1 2.9 %collective-permute-start.11 = (f32[32,384]{1,0:T(8,128)S(1)}, f32[32,384]{1,0:T(8,128)S(1)}, u32[]{:S(2)}, u32[]{:S(2)}) collective-permute-start(f32[32,384]{1,0:T(8,128)S(1)} %add.63), channel_id=1, source_target_pairs={{0,24},{8,16},{16,8},{24,0},{32,56},{40,48},{48,40},{56,32},{1,25}... | collective-permute-start | bytes 147464 | tf_op jit(solution)/shard_map/ppermute | solution.py:239
  36.0 0.7 collective-permute-start.9
  36.8 1.1 %convolution_convert_fusion = bf16[2,256,512]{2,1,0:T(8,128)(2,1)} fusion(bf16[1,224,256]{2,1,0:T(8,128)(2,1)S(1)} %bitcast.63, bf16[1,224,256]{2,1,0:T(8,128)(2,1)S(1)} %get-tuple-element.6, bf16[112,512]{1,0:T(8,128)(2,1)S(1)} %add.59, bf16[112,512]{1,0:T(8,128)(2,1)S(1)} %add.57), kind=kOutput, calls=%fused_computation | convolution fusion | flops 118276096 | bytes 983040 | tf_op jit(solution)/shard_map/hrc,rk->hck/dot_general | solution.py:302
  37.9 9.5 %all-to-all-start = ((bf16[32,16,512]{2,1,0:T(8,128)(2,1)}), bf16[32,16,512]{2,1,0:T(8,128)(2,1)S(1)}, u32[]{:S(2)}, u32[]{:S(2)}) async-start(bf16[32,16,512]{2,1,0:T(8,128)(2,1)} %bitcast.16), calls=%async_computation | async-start | bytes 1048576 | tf_op jit(solution)/shard_map/all_to_all | solution.py:235
  47.4 1.3 %collective-permute-start.12 = (f32[32,384]{1,0:T(8,128)S(1)}, f32[32,384]{1,0:T(8,128)S(1)}, u32[]{:S(2)}, u32[]{:S(2)}) collective-permute-start(f32[32,384]{1,0:T(8,128)S(1)} %add_add_fusion), channel_id=1, source_target_pairs={{0,64},{64,0},{128,192},{192,128},{1,65},{65,1},{129,193},{193,129... | collective-permute-start | bytes 147464 | tf_op jit(solution)/shard_map/ppermute | solution.py:239
  48.8 2.4 %collective-permute-start.13 = (f32[32,384]{1,0:T(8,128)S(1)}, f32[32,384]{1,0:T(8,128)S(1)}, u32[]{:S(2)}, u32[]{:S(2)}) collective-permute-start(f32[32,384]{1,0:T(8,128)S(1)} %add_add_fusion), channel_id=1, source_target_pairs={{0,128},{64,192},{128,0},{192,64},{1,129},{65,193},{129,1},{193,65... | collective-permute-start | bytes 147464 | tf_op jit(solution)/shard_map/ppermute | solution.py:239
  51.2 0.2 collective-permute-start.14
  51.4 2.0 %collective-permute-done.13 = f32[32,384]{1,0:T(8,128)S(1)} collective-permute-done((f32[32,384]{1,0:T(8,128)S(1)}, f32[32,384]{1,0:T(8,128)S(1)}, u32[]{:S(2)}, u32[]{:S(2)}) %collective-permute-start.13) | collective-permute-done | bytes 49184 | tf_op jit(solution)/shard_map/ppermute | solution.py:239
  53.4 2.3 %collective-permute-done.14 = f32[32,384]{1,0:T(8,128)S(1)} collective-permute-done((f32[32,384]{1,0:T(8,128)S(1)}, f32[32,384]{1,0:T(8,128)S(1)}, u32[]{:S(2)}, u32[]{:S(2)}) %collective-permute-start.14) | collective-permute-done | bytes 49184 | tf_op jit(solution)/shard_map/ppermute | solution.py:239
  55.7 1.1 %collective-permute-start.17 = (f32[128,384]{1,0:T(8,128)S(1)}, f32[128,384]{1,0:T(8,128)S(1)}, u32[]{:S(2)}, u32[]{:S(2)}) collective-permute-start(f32[128,384]{1,0:T(8,128)S(1)} %bitcast.51), channel_id=1, source_target_pairs={{0,6},{2,0},{4,2},{6,4},{1,7},{3,1},{5,3},{7,5},{8,14},{10,8},{12,... | collective-permute-start | bytes 589832 | tf_op jit(solution)/shard_map/ppermute | solution.py:299
  56.8 1.0 collective-permute-start.16
  57.9 0.0 collective-permute-start.15
  57.9 1.0 all-to-all-done
  58.8 0.1 reduce_sum.21
  58.9 0.9 broadcast_in_dim.4
  59.7 6.6 %all-to-all-start.1 = ((bf16[32,16,512]{2,1,0:T(8,128)(2,1)}), bf16[32,16,512]{2,1,0:T(8,128)(2,1)S(1)}, u32[]{:S(2)}, u32[]{:S(2)}) async-start(bf16[32,16,512]{2,1,0:T(8,128)(2,1)} %broadcast_in_dim.4), calls=%async_computation.1 | async-start | bytes 1048576 | tf_op jit(solution)/shard_map/all_to_all | solution.py:235
  66.4 19.1 %shard_map.50 = bf16[512,512]{1,0:T(8,128)(2,1)S(1)} custom-call(s32[1]{0:T(128)} %bitcast.2.where_ref, f32[128,384]{1,0:T(8,128)S(1)} %bitcast.54, f32[128,384]{1,0:T(8,128)S(1)} %collective-permute-done.15.one_ref, f32[128,384]{1,0:T(8,128)S(1)} %collective-permute-done.16.two_ref, f32[128,384]{1,0:T(8,128)S(1)} %collective-permute-done.17.three_ref), custom_call_target="tpu_custom_call" | custom-call | flops 20000000000 | tf_op jit(solution)/shard_map/pallas_call | solution.py:217
  85.5 0.3 convolution_convert_fusion.2
  85.9 0.5 multiply_reduce_fusion
  86.3 2.8 %collective-permute-start.22 = (f32[1,512]{1,0:T(1,128)S(1)}, f32[1,512]{1,0:T(1,128)S(1)}, u32[]{:S(2)}, u32[]{:S(2)}) collective-permute-start(f32[1,512]{1,0:T(1,128)S(1)} %bitcast.58), channel_id=1, source_target_pairs={{0,6},{2,4},{4,2},{6,0},{1,7},{3,5},{5,3},{7,1},{8,14},{10,12},{12... | collective-permute-start | bytes 6152 | tf_op jit(solution)/shard_map/ppermute | solution.py:239
  89.1 0.8 collective-permute-start.21
  89.9 0.3 fusion.2
  90.2 8.6 %collective-permute-start.19 = (bf16[224,256]{1,0:T(8,128)(2,1)S(1)}, bf16[224,256]{1,0:T(8,128)(2,1)S(1)}, u32[]{:S(2)}, u32[]{:S(2)}) collective-permute-start(bf16[224,256]{1,0:T(8,128)(2,1)S(1)} %fusion.8), channel_id=1, source_target_pairs={{0,1},{1,0},{2,3},{3,2},{4,5},{5,4},{6,7},{7,6},{8,9},{9,8},{10,11... | collective-permute-start | bytes 344072 | tf_op jit(solution)/shard_map/ppermute | solution.py:239
  98.9 0.3 fusion
  99.3 3.6 %collective-permute-start.23 = (bf16[224,256]{1,0:T(8,128)(2,1)S(1)}, bf16[224,256]{1,0:T(8,128)(2,1)S(1)}, u32[]{:S(2)}, u32[]{:S(2)}) collective-permute-start(bf16[224,256]{1,0:T(8,128)(2,1)S(1)} %fusion.6), channel_id=1, source_target_pairs={{0,1},{1,0},{2,3},{3,2},{4,5},{5,4},{6,7},{7,6},{8,9},{9,8},{10,11... | collective-permute-start | bytes 344072 | tf_op jit(solution)/shard_map/ppermute | solution.py:239
  102.9 0.8 maximum_subtract_fusion
  103.7 0.1 collective-permute-done.23
  103.9 0.7 pad_maximum_fusion.1
  (42 shorter events, 0.5 us)
Async XLA Ops:
  0.6 1.3 %copy-start = (bf16[2,256,512]{2,1,0:T(8,128)(2,1)S(1)}, bf16[2,256,512]{2,1,0:T(8,128)(2,1)}, u32[]{:S(2)}) copy-start(bf16[2,256,512]{2,1,0:T(8,128)(2,1)} %param.5) | copy-start | bytes 1572868
  2.2 4.4 %collective-permute-start = (bf16[224,512]{1,0:T(8,128)(2,1)S(1)}, bf16[224,512]{1,0:T(8,128)(2,1)S(1)}, u32[]{:S(2)}, u32[]{:S(2)}) collective-permute-start(bf16[224,512]{1,0:T(8,128)(2,1)S(1)} %dynamic-slice_bitcast_fusion), channel_id=1, source_target_pairs={{0,1},{1,0},{2,3},{3,2},{4,5},{5,4},{6,7},{7,6},{8,9},{9,8},{10,11... | collective-permute-start | bytes 688136 | tf_op jit(solution)/shard_map/ppermute | solution.py:239
  6.7 5.7 %collective-permute-start.3 = (bf16[112,512]{1,0:T(8,128)(2,1)S(1)}, bf16[112,512]{1,0:T(8,128)(2,1)S(1)}, u32[]{:S(2)}, u32[]{:S(2)}) collective-permute-start(bf16[112,512]{1,0:T(8,128)(2,1)S(1)} %get-tuple-element.10), channel_id=1, source_target_pairs={{0,6},{2,4},{4,2},{6,0},{1,7},{3,5},{5,3},{7,1},{8,14},{10,12},{12... | collective-permute-start | bytes 344072 | tf_op jit(solution)/shard_map/ppermute | solution.py:239
  7.8 4.6 %collective-permute-start.1 = (bf16[112,512]{1,0:T(8,128)(2,1)S(1)}, bf16[112,512]{1,0:T(8,128)(2,1)S(1)}, u32[]{:S(2)}, u32[]{:S(2)}) collective-permute-start(bf16[112,512]{1,0:T(8,128)(2,1)S(1)} %get-tuple-element.11), channel_id=1, source_target_pairs={{0,2},{2,0},{4,6},{6,4},{1,3},{3,1},{5,7},{7,5},{8,10},{10,8},{12,... | collective-permute-start | bytes 344072 | tf_op jit(solution)/shard_map/ppermute | solution.py:239
  12.4 3.7 %collective-permute-start.4 = (bf16[112,512]{1,0:T(8,128)(2,1)S(1)}, bf16[112,512]{1,0:T(8,128)(2,1)S(1)}, u32[]{:S(2)}, u32[]{:S(2)}) collective-permute-start(bf16[112,512]{1,0:T(8,128)(2,1)S(1)} %get-tuple-element.8), channel_id=1, source_target_pairs={{0,2},{2,0},{4,6},{6,4},{1,3},{3,1},{5,7},{7,5},{8,10},{10,8},{12,... | collective-permute-start | bytes 344072 | tf_op jit(solution)/shard_map/ppermute | solution.py:239
  12.5 4.9 %collective-permute-start.2 = (bf16[112,512]{1,0:T(8,128)(2,1)S(1)}, bf16[112,512]{1,0:T(8,128)(2,1)S(1)}, u32[]{:S(2)}, u32[]{:S(2)}) collective-permute-start(bf16[112,512]{1,0:T(8,128)(2,1)S(1)} %get-tuple-element.9), channel_id=1, source_target_pairs={{0,6},{2,4},{4,2},{6,0},{1,7},{3,5},{5,3},{7,1},{8,14},{10,12},{12... | collective-permute-start | bytes 344072 | tf_op jit(solution)/shard_map/ppermute | solution.py:239
  18.0 6.6 %collective-permute-start.7 = (f32[32,384]{1,0:T(8,128)S(1)}, f32[32,384]{1,0:T(8,128)S(1)}, u32[]{:S(2)}, u32[]{:S(2)}) collective-permute-start(f32[32,384]{1,0:T(8,128)S(1)} %get-tuple-element.14), channel_id=1, source_target_pairs={{0,192},{64,128},{128,64},{192,0},{1,193},{65,129},{129,65},{193,1... | collective-permute-start | bytes 147464 | tf_op jit(solution)/shard_map/ppermute | solution.py:239
  20.1 4.6 %collective-permute-start.6 = (f32[32,384]{1,0:T(8,128)S(1)}, f32[32,384]{1,0:T(8,128)S(1)}, u32[]{:S(2)}, u32[]{:S(2)}) collective-permute-start(f32[32,384]{1,0:T(8,128)S(1)} %get-tuple-element.15), channel_id=1, source_target_pairs={{0,128},{64,192},{128,0},{192,64},{1,129},{65,193},{129,1},{193,65... | collective-permute-start | bytes 147464 | tf_op jit(solution)/shard_map/ppermute | solution.py:239
  20.6 4.0 %collective-permute-start.5 = (f32[32,384]{1,0:T(8,128)S(1)}, f32[32,384]{1,0:T(8,128)S(1)}, u32[]{:S(2)}, u32[]{:S(2)}) collective-permute-start(f32[32,384]{1,0:T(8,128)S(1)} %get-tuple-element.16), channel_id=1, source_target_pairs={{0,64},{64,0},{128,192},{192,128},{1,65},{65,1},{129,193},{193,129... | collective-permute-start | bytes 147464 | tf_op jit(solution)/shard_map/ppermute | solution.py:239
  21.4 15.4 %collective-permute-start.18 = (bf16[224,256]{1,0:T(8,128)(2,1)S(1)}, bf16[224,256]{1,0:T(8,128)(2,1)S(1)}, u32[]{:S(2)}, u32[]{:S(2)}) collective-permute-start(bf16[224,256]{1,0:T(8,128)(2,1)S(1)} %get-tuple-element.7), channel_id=1, source_target_pairs={{0,1},{1,0},{2,3},{3,2},{4,5},{5,4},{6,7},{7,6},{8,9},{9,8},{10,11... | collective-permute-start | bytes 344072 | tf_op jit(solution)/shard_map/ppermute | solution.py:239
  24.7 8.4 %collective-permute-start.8 = (f32[32,384]{1,0:T(8,128)S(1)}, f32[32,384]{1,0:T(8,128)S(1)}, u32[]{:S(2)}, u32[]{:S(2)}) collective-permute-start(f32[32,384]{1,0:T(8,128)S(1)} %fusion.20), channel_id=1, source_target_pairs={{0,32},{8,40},{16,48},{24,56},{32,0},{40,8},{48,16},{56,24},{1,33}... | collective-permute-start | bytes 147464 | tf_op jit(solution)/shard_map/ppermute | solution.py:239
  33.1 14.3 %collective-permute-start.11 = (f32[32,384]{1,0:T(8,128)S(1)}, f32[32,384]{1,0:T(8,128)S(1)}, u32[]{:S(2)}, u32[]{:S(2)}) collective-permute-start(f32[32,384]{1,0:T(8,128)S(1)} %add.63), channel_id=1, source_target_pairs={{0,24},{8,16},{16,8},{24,0},{32,56},{40,48},{48,40},{56,32},{1,25}... | collective-permute-start | bytes 147464 | tf_op jit(solution)/shard_map/ppermute | solution.py:239
  36.0 11.4 %collective-permute-start.10 = (f32[32,384]{1,0:T(8,128)S(1)}, f32[32,384]{1,0:T(8,128)S(1)}, u32[]{:S(2)}, u32[]{:S(2)}) collective-permute-start(f32[32,384]{1,0:T(8,128)S(1)} %add.63), channel_id=1, source_target_pairs={{0,16},{8,24},{16,0},{24,8},{32,48},{40,56},{48,32},{56,40},{1,17}... | collective-permute-start | bytes 147464 | tf_op jit(solution)/shard_map/ppermute | solution.py:239
  36.0 11.4 %collective-permute-start.9 = (f32[32,384]{1,0:T(8,128)S(1)}, f32[32,384]{1,0:T(8,128)S(1)}, u32[]{:S(2)}, u32[]{:S(2)}) collective-permute-start(f32[32,384]{1,0:T(8,128)S(1)} %add.63), channel_id=1, source_target_pairs={{0,8},{8,0},{16,24},{24,16},{32,40},{40,32},{48,56},{56,48},{1,9},... | collective-permute-start | bytes 147464 | tf_op jit(solution)/shard_map/ppermute | solution.py:239
  37.9 20.9 %all-to-all-start = ((bf16[32,16,512]{2,1,0:T(8,128)(2,1)}), bf16[32,16,512]{2,1,0:T(8,128)(2,1)S(1)}, u32[]{:S(2)}, u32[]{:S(2)}) async-start(bf16[32,16,512]{2,1,0:T(8,128)(2,1)} %bitcast.16), calls=%async_computation | async-start | bytes 1048576 | tf_op jit(solution)/shard_map/all_to_all | solution.py:235
  47.4 3.9 %collective-permute-start.12 = (f32[32,384]{1,0:T(8,128)S(1)}, f32[32,384]{1,0:T(8,128)S(1)}, u32[]{:S(2)}, u32[]{:S(2)}) collective-permute-start(f32[32,384]{1,0:T(8,128)S(1)} %add_add_fusion), channel_id=1, source_target_pairs={{0,64},{64,0},{128,192},{192,128},{1,65},{65,1},{129,193},{193,129... | collective-permute-start | bytes 147464 | tf_op jit(solution)/shard_map/ppermute | solution.py:239
  48.8 4.6 %collective-permute-start.13 = (f32[32,384]{1,0:T(8,128)S(1)}, f32[32,384]{1,0:T(8,128)S(1)}, u32[]{:S(2)}, u32[]{:S(2)}) collective-permute-start(f32[32,384]{1,0:T(8,128)S(1)} %add_add_fusion), channel_id=1, source_target_pairs={{0,128},{64,192},{128,0},{192,64},{1,129},{65,193},{129,1},{193,65... | collective-permute-start | bytes 147464 | tf_op jit(solution)/shard_map/ppermute | solution.py:239
  51.2 4.5 %collective-permute-start.14 = (f32[32,384]{1,0:T(8,128)S(1)}, f32[32,384]{1,0:T(8,128)S(1)}, u32[]{:S(2)}, u32[]{:S(2)}) collective-permute-start(f32[32,384]{1,0:T(8,128)S(1)} %add_add_fusion), channel_id=1, source_target_pairs={{0,192},{64,128},{128,64},{192,0},{1,193},{65,129},{129,65},{193,1... | collective-permute-start | bytes 147464 | tf_op jit(solution)/shard_map/ppermute | solution.py:239
  55.7 10.6 %collective-permute-start.17 = (f32[128,384]{1,0:T(8,128)S(1)}, f32[128,384]{1,0:T(8,128)S(1)}, u32[]{:S(2)}, u32[]{:S(2)}) collective-permute-start(f32[128,384]{1,0:T(8,128)S(1)} %bitcast.51), channel_id=1, source_target_pairs={{0,6},{2,0},{4,2},{6,4},{1,7},{3,1},{5,3},{7,5},{8,14},{10,8},{12,... | collective-permute-start | bytes 589832 | tf_op jit(solution)/shard_map/ppermute | solution.py:299
  56.8 9.5 %collective-permute-start.16 = (f32[128,384]{1,0:T(8,128)S(1)}, f32[128,384]{1,0:T(8,128)S(1)}, u32[]{:S(2)}, u32[]{:S(2)}) collective-permute-start(f32[128,384]{1,0:T(8,128)S(1)} %bitcast.52), channel_id=1, source_target_pairs={{0,4},{2,6},{4,0},{6,2},{1,5},{3,7},{5,1},{7,3},{8,12},{10,14},{12... | collective-permute-start | bytes 589832 | tf_op jit(solution)/shard_map/ppermute | solution.py:299
  57.9 8.5 %collective-permute-start.15 = (f32[128,384]{1,0:T(8,128)S(1)}, f32[128,384]{1,0:T(8,128)S(1)}, u32[]{:S(2)}, u32[]{:S(2)}) collective-permute-start(f32[128,384]{1,0:T(8,128)S(1)} %bitcast.53), channel_id=1, source_target_pairs={{0,2},{2,4},{4,6},{6,0},{1,3},{3,5},{5,7},{7,1},{8,10},{10,12},{12... | collective-permute-start | bytes 589832 | tf_op jit(solution)/shard_map/ppermute | solution.py:299
  59.7 26.1 %all-to-all-start.1 = ((bf16[32,16,512]{2,1,0:T(8,128)(2,1)}), bf16[32,16,512]{2,1,0:T(8,128)(2,1)S(1)}, u32[]{:S(2)}, u32[]{:S(2)}) async-start(bf16[32,16,512]{2,1,0:T(8,128)(2,1)} %broadcast_in_dim.4), calls=%async_computation.1 | async-start | bytes 1048576 | tf_op jit(solution)/shard_map/all_to_all | solution.py:235
  86.3 12.5 %collective-permute-start.22 = (f32[1,512]{1,0:T(1,128)S(1)}, f32[1,512]{1,0:T(1,128)S(1)}, u32[]{:S(2)}, u32[]{:S(2)}) collective-permute-start(f32[1,512]{1,0:T(1,128)S(1)} %bitcast.58), channel_id=1, source_target_pairs={{0,6},{2,4},{4,2},{6,0},{1,7},{3,5},{5,3},{7,1},{8,14},{10,12},{12... | collective-permute-start | bytes 6152 | tf_op jit(solution)/shard_map/ppermute | solution.py:239
  89.1 9.8 %collective-permute-start.21 = (f32[1,512]{1,0:T(1,128)S(1)}, f32[1,512]{1,0:T(1,128)S(1)}, u32[]{:S(2)}, u32[]{:S(2)}) collective-permute-start(f32[1,512]{1,0:T(1,128)S(1)} %bitcast.59), channel_id=1, source_target_pairs={{0,4},{2,6},{4,0},{6,2},{1,5},{3,7},{5,1},{7,3},{8,12},{10,14},{12... | collective-permute-start | bytes 6152 | tf_op jit(solution)/shard_map/ppermute | solution.py:239
  89.9 9.0 %collective-permute-start.20 = (f32[1,512]{1,0:T(1,128)S(1)}, f32[1,512]{1,0:T(1,128)S(1)}, u32[]{:S(2)}, u32[]{:S(2)}) collective-permute-start(f32[1,512]{1,0:T(1,128)S(1)} %bitcast.60), channel_id=1, source_target_pairs={{0,2},{2,0},{4,6},{6,4},{1,3},{3,1},{5,7},{7,5},{8,10},{10,8},{12,... | collective-permute-start | bytes 6152 | tf_op jit(solution)/shard_map/ppermute | solution.py:239
  90.2 12.6 %collective-permute-start.19 = (bf16[224,256]{1,0:T(8,128)(2,1)S(1)}, bf16[224,256]{1,0:T(8,128)(2,1)S(1)}, u32[]{:S(2)}, u32[]{:S(2)}) collective-permute-start(bf16[224,256]{1,0:T(8,128)(2,1)S(1)} %fusion.8), channel_id=1, source_target_pairs={{0,1},{1,0},{2,3},{3,2},{4,5},{5,4},{6,7},{7,6},{8,9},{9,8},{10,11... | collective-permute-start | bytes 344072 | tf_op jit(solution)/shard_map/ppermute | solution.py:239
  99.3 4.5 %collective-permute-start.23 = (bf16[224,256]{1,0:T(8,128)(2,1)S(1)}, bf16[224,256]{1,0:T(8,128)(2,1)S(1)}, u32[]{:S(2)}, u32[]{:S(2)}) collective-permute-start(bf16[224,256]{1,0:T(8,128)(2,1)S(1)} %fusion.6), channel_id=1, source_target_pairs={{0,1},{1,0},{2,3},{3,2},{4,5},{5,4},{6,7},{7,6},{8,9},{9,8},{10,11... | collective-permute-start | bytes 344072 | tf_op jit(solution)/shard_map/ppermute | solution.py:239
